TPU v7x, 256 devices: a whole 4x4x8 slice. The times are simulated.
256 devices in a mesh: leaf: 64 (over z, x, core), lvl: 4 (over y).
Axes of the slice: x: 4, y: 4, z: 8, core: 2. Of those that a mesh axis runs over, the one named last changes fastest.
Arguments:
- charges: bfloat16 [1024, 256, 512], P('leaf', 'lvl'), may hold values from -6 to 6
- leaf_basis: bfloat16 [1024, 256, 64], P('leaf', 'lvl'), may hold values from -0.375 to 0.375
- near_blocks: bfloat16 [1024, 12, 256, 256], P('leaf', None, 'lvl'), may hold values from -0.109375 to 0.109375
- near_cols: int32 [1024, 12], P('leaf'), may hold values from 0 to 1023, as said below
- coupling_fine: float32 [1024, 4, 64, 64], P('leaf', 'lvl'), may hold values from -0.375 to 0.375
- coupling_middle: float32 [512, 4, 64, 64], P('leaf', 'lvl'), may hold values from -0.375 to 0.375
- coupling_coarse: float32 [256, 4, 64, 64], P('leaf', 'lvl'), may hold values from -0.375 to 0.375
- far_cols_fine: int32 [1024, 4], P('leaf', 'lvl'), may hold values from 0 to 1023, as said below
- far_cols_middle: int32 [512, 4], P('leaf', 'lvl'), may hold values from 0 to 511, as said below
- far_cols_coarse: int32 [256, 4], P('leaf', 'lvl'), may hold values from 0 to 255, as said below
- transfer_fine: float32 [1024, 64, 64], P('leaf'), may hold values from -0.5 to 0.5
- transfer_middle: float32 [512, 64, 64], P('leaf'), may hold values from -0.5 to 0.5
- transfer_coarse: float32 [256, 64, 64], P('leaf'), may hold values from -0.5 to 0.5
- top_coupling: float32 [128, 8, 64, 64], P('leaf', 'lvl'), may hold values from -0.25 to 0.25
- top_cols: int32 [128, 8], P('leaf', 'lvl'), may hold values from 0 to 127, as said below
Outputs:
- potentials: bfloat16 [1024, 256, 512], P('leaf', 'lvl')
Inputs may be any that keep to these rules, and one draw needn't show every extreme that they name: `near_cols`: the clusters are ordered on a periodic line. The slots of row c hold, in some order, the 12 distinct clusters (c + d) mod 1024 for d from -6 to 5. `far_cols_fine`: the slots of row c hold, in some order, the 4 distinct clusters (c + d) mod 1024 with |d| from 7 to 8, none of them in the near field of c. `far_cols_middle`: the slots of row c hold, in some order, the 4 distinct clusters (c + d) mod (512) with |d| from 4 to 5, none holding a leaf in the near field of a leaf of c. `far_cols_coarse`: the slots of row c hold, in some order, the 4 distinct clusters (c + d) mod (256) with |d| from 3 to 4, none holding a leaf in the near field of a leaf of c. `top_cols`: the slots of row r hold 8 distinct roots, none of them r.
All inputs are finite; a program needn't handle non-finite values.
Results may differ from a plain program's by a relative error of at most 0.0065.
Values may be sent and summed in bfloat16 or wider, within the bound.
No kernel may reach another device: no remote copies, remote signals or barrier semaphores. Data moves between devices by JAX's collectives and lax.ppermute only.
A program may use at most 128 MiB of HBM per device.

v0:
```python
import jax
import jax.numpy as jnp
from jax import lax
from jax.sharding import PartitionSpec as P

NEAR_REACH = 6
REACH_FINE = 8
REACH_MIDDLE = 5
REACH_COARSE = 4


def padded(block, sides, width):
    for axis, dim in sides:
        count = lax.axis_size(axis)
        forward = [(i, i + 1) for i in range(count - 1)]
        forward.append((count - 1, 0))
        backward = [(target, source) for source, target in forward]
        low = lax.ppermute(
            lax.slice_in_dim(block, block.shape[dim] - width, None, axis=dim), axis, forward
        )
        high = lax.ppermute(lax.slice_in_dim(block, 0, width, axis=dim), axis, backward)
        block = jnp.concatenate([low, block, high], axis=dim)
    return block


def lifted_moments(moments, transfer):
    lifted = jnp.einsum("cak,car->ckr", transfer, moments, precision=lax.Precision.HIGHEST)
    return lifted.reshape(lifted.shape[0] // 2, 2, lifted.shape[1], lifted.shape[2]).sum(axis=1)


def lowered_local(parent_local, transfer, coupled):
    spread = jnp.repeat(parent_local, 2, axis=0)
    return coupled + jnp.einsum("cak,ckr->car", transfer, spread, precision=lax.Precision.HIGHEST)


def coupled_terms(sources, blocks, columns):
    total = jnp.zeros((columns.shape[0],) + sources.shape[1:], jnp.float32)
    for slot_at in range(columns.shape[1]):
        picked = jnp.take(sources, columns[:, slot_at], axis=0)
        total = total + jnp.einsum(
            "cab,cbr->car", blocks[:, slot_at], picked, precision=lax.Precision.HIGHEST
        )
    return total


def level_term(moments, blocks, columns, width):
    count = moments.shape[0]
    rimmed = padded(moments, (("leaf", 0),), width)
    overall = count * lax.axis_size("leaf")
    local_cols = jnp.mod(columns - lax.axis_index("leaf") * count + width, overall)
    return coupled_terms(rimmed, blocks, local_cols)


def body(
    charges,
    leaf_basis,
    near_blocks,
    near_cols,
    coupling_fine,
    coupling_middle,
    coupling_coarse,
    far_cols_fine,
    far_cols_middle,
    far_cols_coarse,
    transfer_fine,
    transfer_middle,
    transfer_coarse,
    top_coupling,
    top_cols,
):
    leaves = charges.shape[0]
    leaf_at = lax.axis_index("leaf")
    whole_points = lax.all_gather(charges, "lvl", axis=1, tiled=True)
    extended = padded(whole_points, (("leaf", 0),), NEAR_REACH)
    local_near = jnp.mod(near_cols - leaf_at * leaves + NEAR_REACH, leaves * lax.axis_size("leaf"))

    def near_slot(slot_at, total):
        picked = jnp.take(extended, lax.dynamic_index_in_dim(local_near, slot_at, 1, False), axis=0)
        block = lax.dynamic_index_in_dim(near_blocks, slot_at, 1, False)
        return total + jnp.einsum("cpq,cqr->cpr", block, picked, preferred_element_type=jnp.float32)

    near_field = lax.fori_loop(
        0, near_cols.shape[1], near_slot, jnp.zeros(charges.shape, jnp.float32)
    )
    partial_moments = jnp.einsum(
        "cpk,cpr->ckr", leaf_basis, charges, preferred_element_type=jnp.float32
    )
    moments_fine = lax.psum(partial_moments, "lvl")
    moments_middle = lifted_moments(moments_fine, transfer_fine)
    moments_coarse = lifted_moments(moments_middle, transfer_middle)
    moments_root = lifted_moments(moments_coarse, transfer_coarse)
    term_fine = level_term(moments_fine, coupling_fine, far_cols_fine, REACH_FINE)
    term_middle = level_term(moments_middle, coupling_middle, far_cols_middle, REACH_MIDDLE)
    term_coarse = level_term(moments_coarse, coupling_coarse, far_cols_coarse, REACH_COARSE)
    all_roots = lax.all_gather(
        moments_root.astype(jnp.bfloat16), "leaf", axis=0, tiled=True
    ).astype(moments_root.dtype)
    term_top = coupled_terms(all_roots, top_coupling, top_cols)
    term_fine, term_middle, term_coarse, term_top = lax.psum(
        (term_fine, term_middle, term_coarse, term_top), "lvl"
    )
    local_coarse = lowered_local(term_top, transfer_coarse, term_coarse)
    local_middle = lowered_local(local_coarse, transfer_middle, term_middle)
    local_fine = lowered_local(local_middle, transfer_fine, term_fine)
    leaf_local = local_fine.astype(jnp.bfloat16)
    far_field = jnp.einsum(
        "cpk,ckr->cpr", leaf_basis, leaf_local, preferred_element_type=jnp.float32
    )
    return (near_field + far_field).astype(jnp.bfloat16)


def solution(mesh):
    placed = (
        P("leaf", "lvl", None),
        P("leaf", "lvl", None),
        P("leaf", None, "lvl", None),
        P("leaf", None),
        P("leaf", "lvl", None, None),
        P("leaf", "lvl", None, None),
        P("leaf", "lvl", None, None),
        P("leaf", "lvl"),
        P("leaf", "lvl"),
        P("leaf", "lvl"),
        P("leaf", None, None),
        P("leaf", None, None),
        P("leaf", None, None),
        P("leaf", "lvl", None, None),
        P("leaf", "lvl"),
    )
    return jax.shard_map(
        body, mesh=mesh, in_specs=placed, out_specs=P("leaf", "lvl", None), check_vma=False
    )
```

profile of v0, /device:TPU:24, one launch (start us, length us, event | category | flops | bytes accessed | tf_op | source)
XLA Modules:
  0.0 374.6 jit_solution(12252306065542025222)
XLA Ops:
  10.6 64.0 %all-reduce.4.cloned.1.call-done = f32[16,64,512]{2,1,0:T(8,128)} async-done(((f32[16,64,512]{2,1,0:T(8,128)}), f32[16,64,512]{2,1,0:T(8,128)}) %all-reduce.4.cloned.1.call-update) | async-done | bytes 2097168 | tf_op jit(solution)/shard_map/psum | solution.py:88
  92.6 34.6 %all-gather.3.cloned.1.call-done = bf16[16,256,512]{2,1,0:T(8,128)(2,1)} async-done(((bf16[16,64,512]{2,1,0:T(8,128)(2,1)}), bf16[16,256,512]{2,1,0:T(8,128)(2,1)}) %all-gather.3.cloned.1.call-update) | async-done | bytes 4194320 | tf_op jit(solution)/shard_map/all_gather | solution.py:73
  131.1 5.1 %collective-permute-start.3 = (f32[8,64,512]{2,1,0:T(8,128)}, f32[8,64,512]{2,1,0:T(8,128)}, u32[]{:S(2)}, u32[]{:S(2)}) collective-permute-start(f32[8,64,512]{2,1,0:T(8,128)} %get-tuple-element.156), channel_id=1, source_target_pairs={{4,0},{8,4},{12,8},{16,12},{20,16},{24,20},{28,24},{32,28},{36,32}... | collective-permute-start | bytes 3145736 | tf_op jit(solution)/shard_map/ppermute | solution.py:21
  136.2 5.1 %collective-permute-start.1 = (bf16[6,256,512]{2,1,0:T(8,128)(2,1)}, bf16[6,256,512]{2,1,0:T(8,128)(2,1)}, u32[]{:S(2)}, u32[]{:S(2)}) collective-permute-start(bf16[6,256,512]{2,1,0:T(8,128)(2,1)} %get-tuple-element.154), channel_id=1, source_target_pairs={{4,0},{8,4},{12,8},{16,12},{20,16},{24,20},{28,24},{32,28},{36,32}... | collective-permute-start | bytes 4718600 | tf_op jit(solution)/shard_map/ppermute | solution.py:21
  164.7 4.4 %gather_fusion.1 = f32[16,64,512]{2,1,0:T(8,128)} fusion(f32[32,64,512]{2,1,0:T(8,128)} %pad_maximum_fusion.1, s32[1024]{0:T(1024)} %pad_clamp_fusion.5), kind=kCustom, calls=%fused_computation.3 | custom fusion | bytes 4194368 | tf_op jit(solution)/shard_map/jit(_take)/gather | solution.py:39
  169.1 5.2 %fusion.14 = f32[16,64,512]{2,1,0:T(8,128)} fusion(f32[16,64,512]{2,1,0:T(8,128)} %gather_fusion.1, pred[16]{0:T(512)(128)(4,1)} %get-tuple-element.151, f32[16,1,64,64]{3,2,1,0:T(8,128)S(1)} %copy-done.10), kind=kOutput, calls=%fused_computation.28 | convolution fusion | flops 403177472 | bytes 4456464 | tf_op jit(solution)/shard_map/cab,cbr->car/dot_general | solution.py:40
  174.4 5.5 %pad_maximum_fusion = bf16[28,256,512]{2,1,0:T(8,128)(2,1)} fusion(bf16[6,256,512]{2,1,0:T(8,128)(2,1)} %collective-permute-done.1, bf16[16,256,512]{2,1,0:T(8,128)(2,1)S(1)} %copy-done.4, bf16[6,256,512]{2,1,0:T(8,128)(2,1)} %collective-permute-done), kind=kLoop, calls=%fused_computation.18 | loop fusion | flops 7340032 | bytes 14680064 | tf_op jit(solution)/shard_map/concatenate | solution.py:22
  179.8 38.6 %all-gather.5.cloned.1.call-done = bf16[128,64,512]{2,1,0:T(8,128)(2,1)} async-done(((bf16[2,64,512]{2,1,0:T(8,128)(2,1)}), bf16[128,64,512]{2,1,0:T(8,128)(2,1)}) %all-gather.5.cloned.1.call-update) | async-done | bytes 8388624 | tf_op jit(solution)/shard_map/all_gather | solution.py:95
  218.4 11.6 %convert_element_type.13 = f32[128,64,512]{2,1,0:T(8,128)} convert(bf16[128,64,512]{2,1,0:T(8,128)(2,1)} %all-gather.5.cloned.1.call-done) | non-fusion elementwise | flops 4194304 | bytes 25165824 | tf_op jit(solution)/shard_map/convert_element_type | solution.py:97
  230.0 7.0 %gather_fusion.4 = f32[2,64,512]{2,1,0:T(8,128)} fusion(f32[128,64,512]{2,1,0:T(8,128)} %convert_element_type.13, s32[1024]{0:T(1024)S(1)} %pad_clamp_fusion.2), kind=kCustom, calls=%fused_computation.1.clone | custom fusion | bytes 524296 | tf_op jit(solution)/shard_map/jit(_take)/gather | solution.py:39
  237.0 6.3 %gather_fusion.5 = f32[2,64,512]{2,1,0:T(8,128)S(1)} fusion(f32[128,64,512]{2,1,0:T(8,128)} %convert_element_type.13, s32[1024]{0:T(1024)S(1)} %pad_clamp_fusion.1), kind=kCustom, calls=%fused_computation.2.clone | custom fusion | bytes 524296 | tf_op jit(solution)/shard_map/jit(_take)/gather | solution.py:39
  246.8 113.8 %while.14 = (s32[]{:T(128)}, f32[16,64,512]{2,1,0:T(8,128)S(1)}, bf16[16,12,64,256]{3,2,1,0:T(8,128)(2,1)}, s32[16,12]{0,1:T(8,128)S(1)}, bf16[28,256,512]{2,1,0:T(8,128)(2,1)}, /*index=5*/s32[]{:T(128)}, s32[]{:T(128)}) while((s32[]{:T(128)}, f32[16,64,512]{2,1,0:T(8,128)S(1)}, bf16[16,12,64,256]{3,2,1,0:T(8,128)(2,1)}, ...), condition=%wide.region_1.2_spmd.clone, body=%wide.region_0.1_spmd.clone.sunk | while | flops 271582304 | bytes 17306492 | solution.py:82
  246.9 5.9 %gather_fusion = bf16[16,256,512]{2,1,0:T(8,128)(2,1)} fusion(bf16[28,256,512]{2,1,0:T(8,128)(2,1)} %get-tuple-element.214, s32[1024]{0:T(1024)S(1)} %pad_clamp_fusion.7), kind=kCustom, calls=%fused_computation.clone.clone.1 | custom fusion | bytes 8388672 | tf_op jit(solution)/shard_map/while/body/eval_jaxpr/jit(_take)/gather | solution.py:78
  256.3 5.9 %gather_fusion = bf16[16,256,512]{2,1,0:T(8,128)(2,1)} fusion(bf16[28,256,512]{2,1,0:T(8,128)(2,1)} %get-tuple-element.214, s32[1024]{0:T(1024)S(1)} %pad_clamp_fusion.7), kind=kCustom, calls=%fused_computation.clone.clone.1 | custom fusion | bytes 8388672 | tf_op jit(solution)/shard_map/while/body/eval_jaxpr/jit(_take)/gather | solution.py:78
  265.8 5.9 %gather_fusion = bf16[16,256,512]{2,1,0:T(8,128)(2,1)} fusion(bf16[28,256,512]{2,1,0:T(8,128)(2,1)} %get-tuple-element.214, s32[1024]{0:T(1024)S(1)} %pad_clamp_fusion.7), kind=kCustom, calls=%fused_computation.clone.clone.1 | custom fusion | bytes 8388672 | tf_op jit(solution)/shard_map/while/body/eval_jaxpr/jit(_take)/gather | solution.py:78
  275.2 6.0 %gather_fusion = bf16[16,256,512]{2,1,0:T(8,128)(2,1)} fusion(bf16[28,256,512]{2,1,0:T(8,128)(2,1)} %get-tuple-element.214, s32[1024]{0:T(1024)S(1)} %pad_clamp_fusion.7), kind=kCustom, calls=%fused_computation.clone.clone.1 | custom fusion | bytes 8388672 | tf_op jit(solution)/shard_map/while/body/eval_jaxpr/jit(_take)/gather | solution.py:78
  284.7 6.0 %gather_fusion = bf16[16,256,512]{2,1,0:T(8,128)(2,1)} fusion(bf16[28,256,512]{2,1,0:T(8,128)(2,1)} %get-tuple-element.214, s32[1024]{0:T(1024)S(1)} %pad_clamp_fusion.7), kind=kCustom, calls=%fused_computation.clone.clone.1 | custom fusion | bytes 8388672 | tf_op jit(solution)/shard_map/while/body/eval_jaxpr/jit(_take)/gather | solution.py:78
  294.2 5.9 %gather_fusion = bf16[16,256,512]{2,1,0:T(8,128)(2,1)} fusion(bf16[28,256,512]{2,1,0:T(8,128)(2,1)} %get-tuple-element.214, s32[1024]{0:T(1024)S(1)} %pad_clamp_fusion.7), kind=kCustom, calls=%fused_computation.clone.clone.1 | custom fusion | bytes 8388672 | tf_op jit(solution)/shard_map/while/body/eval_jaxpr/jit(_take)/gather | solution.py:78
  303.7 6.2 %gather_fusion = bf16[16,256,512]{2,1,0:T(8,128)(2,1)} fusion(bf16[28,256,512]{2,1,0:T(8,128)(2,1)} %get-tuple-element.214, s32[1024]{0:T(1024)S(1)} %pad_clamp_fusion.7), kind=kCustom, calls=%fused_computation.clone.clone.1 | custom fusion | bytes 8388672 | tf_op jit(solution)/shard_map/while/body/eval_jaxpr/jit(_take)/gather | solution.py:78
  313.6 5.9 %gather_fusion = bf16[16,256,512]{2,1,0:T(8,128)(2,1)} fusion(bf16[28,256,512]{2,1,0:T(8,128)(2,1)} %get-tuple-element.214, s32[1024]{0:T(1024)S(1)} %pad_clamp_fusion.7), kind=kCustom, calls=%fused_computation.clone.clone.1 | custom fusion | bytes 8388672 | tf_op jit(solution)/shard_map/while/body/eval_jaxpr/jit(_take)/gather | solution.py:78
  323.0 5.9 %gather_fusion = bf16[16,256,512]{2,1,0:T(8,128)(2,1)} fusion(bf16[28,256,512]{2,1,0:T(8,128)(2,1)} %get-tuple-element.214, s32[1024]{0:T(1024)S(1)} %pad_clamp_fusion.7), kind=kCustom, calls=%fused_computation.clone.clone.1 | custom fusion | bytes 8388672 | tf_op jit(solution)/shard_map/while/body/eval_jaxpr/jit(_take)/gather | solution.py:78
  332.5 5.9 %gather_fusion = bf16[16,256,512]{2,1,0:T(8,128)(2,1)} fusion(bf16[28,256,512]{2,1,0:T(8,128)(2,1)} %get-tuple-element.214, s32[1024]{0:T(1024)S(1)} %pad_clamp_fusion.7), kind=kCustom, calls=%fused_computation.clone.clone.1 | custom fusion | bytes 8388672 | tf_op jit(solution)/shard_map/while/body/eval_jaxpr/jit(_take)/gather | solution.py:78
  341.9 5.9 %gather_fusion = bf16[16,256,512]{2,1,0:T(8,128)(2,1)} fusion(bf16[28,256,512]{2,1,0:T(8,128)(2,1)} %get-tuple-element.214, s32[1024]{0:T(1024)S(1)} %pad_clamp_fusion.7), kind=kCustom, calls=%fused_computation.clone.clone.1 | custom fusion | bytes 8388672 | tf_op jit(solution)/shard_map/while/body/eval_jaxpr/jit(_take)/gather | solution.py:78
  351.3 5.9 %gather_fusion = bf16[16,256,512]{2,1,0:T(8,128)(2,1)} fusion(bf16[28,256,512]{2,1,0:T(8,128)(2,1)} %get-tuple-element.214, s32[1024]{0:T(1024)S(1)} %pad_clamp_fusion.7), kind=kCustom, calls=%fused_computation.clone.clone.1 | custom fusion | bytes 8388672 | tf_op jit(solution)/shard_map/while/body/eval_jaxpr/jit(_take)/gather | solution.py:78
  (140 shorter events, 102.2 us)
Async XLA Ops:
  6.5 68.0 %copy-start = (f32[16,64,64]{2,1,0:T(8,128)S(1)}, f32[16,64,64]{2,1,0:T(8,128)}, u32[]{:S(2)}) copy-start(f32[16,64,64]{2,1,0:T(8,128)} %param.29) | copy-start | bytes 786436
  6.5 68.0 %all-reduce.4.cloned.1.call-start = ((), (), s32[]{:S(2)}) async-start(), calls=%async_computation.1 | async-start | bytes 4194304 | tf_op jit(solution)/shard_map/psum | solution.py:88
  9.8 68.4 %copy-start.7 = (f32[8,64,64]{2,1,0:T(8,128)S(1)}, f32[8,64,64]{2,1,0:T(8,128)}, u32[]{:S(2)}) copy-start(f32[8,64,64]{2,1,0:T(8,128)} %param.30) | copy-start | bytes 393220
  9.8 117.4 %all-gather.3.cloned.1.call-start = ((), (), s32[]{:S(2)}) async-start(), calls=%async_computation | async-start | bytes 5242880 | tf_op jit(solution)/shard_map/all_gather | solution.py:73
  10.5 68.8 %copy-start.12 = (f32[4,64,64]{2,1,0:T(8,128)S(1)}, f32[4,64,64]{2,1,0:T(8,128)}, u32[]{:S(2)}) copy-start(f32[4,64,64]{2,1,0:T(8,128)} %param.31) | copy-start | bytes 196612
  10.6 207.8 %all-gather.5.cloned.1.call-start = ((), (), s32[]{:S(2)}) async-start(), calls=%async_computation.2 | async-start | bytes 8519680 | tf_op jit(solution)/shard_map/all_gather | solution.py:95
  78.2 6.7 %copy-start.1 = (f32[8,64,512]{2,1,0:T(8,128)}, f32[8,64,512]{2,1,0:T(8,128)S(1)}, u32[]{:S(2)}) copy-start(f32[8,64,512]{2,1,0:T(8,128)S(1)} %bitcast_reduce_fusion) | copy-start | bytes 3145732
  78.2 3.8 %copy-start.17 = (s32[4,1]{0,1:T(1,128)S(1)}, s32[4,1]{0,1:T(1,128)}, u32[]{:S(2)}) copy-start(s32[4,1]{0,1:T(1,128)} %param.28) | copy-start | bytes 52
  78.2 4.4 %copy-start.18 = (s32[8,1]{0,1:T(1,128)S(1)}, s32[8,1]{0,1:T(1,128)}, u32[]{:S(2)}) copy-start(s32[8,1]{0,1:T(1,128)} %param.27) | copy-start | bytes 100
  78.3 5.0 %copy-start.19 = (s32[16,1]{0,1:T(1,128)S(1)}, s32[16,1]{0,1:T(1,128)}, u32[]{:S(2)}) copy-start(s32[16,1]{0,1:T(1,128)} %param.26) | copy-start | bytes 196
  80.6 280.1 %all-reduce.6.cloned.1.call-start = ((), (), s32[]{:S(2)}) async-start(), calls=%async_computation.3 | async-start | bytes 7864320 | tf_op jit(solution)/shard_map/psum | solution.py:99
  80.8 10.3 %copy-start.2 = (f32[16,64,512]{2,1,0:T(8,128)S(1)}, f32[16,64,512]{2,1,0:T(8,128)}, u32[]{:S(2)}) copy-start(f32[16,64,512]{2,1,0:T(8,128)} %all-reduce.4.cloned.1.call-done) | copy-start | bytes 6291460
  84.9 51.3 %collective-permute-start.4 = (f32[5,64,512]{2,1,0:T(8,128)S(1)}, f32[5,64,512]{2,1,0:T(8,128)S(1)}, u32[]{:S(2)}, u32[]{:S(2)}) collective-permute-start(f32[5,64,512]{2,1,0:T(8,128)S(1)} %get-tuple-element.157), channel_id=1, source_target_pairs={{0,4},{4,8},{8,12},{12,16},{16,20},{20,24},{24,28},{28,32},{32,36}... | collective-permute-start | bytes 1966088 | tf_op jit(solution)/shard_map/ppermute | solution.py:18
  85.5 45.6 %collective-permute-start.6 = (f32[4,64,512]{2,1,0:T(8,128)S(1)}, f32[4,64,512]{2,1,0:T(8,128)}, u32[]{:S(2)}, u32[]{:S(2)}) collective-permute-start(f32[4,64,512]{2,1,0:T(8,128)S(1)} %bitcast_reduce_fusion.1), channel_id=1, source_target_pairs={{0,4},{4,8},{8,12},{12,16},{16,20},{20,24},{24,28},{28,32},{32,36}... | collective-permute-start | bytes 1572872 | tf_op jit(solution)/shard_map/ppermute | solution.py:18
  87.0 49.1 %collective-permute-start.7 = (f32[4,64,512]{2,1,0:T(8,128)S(1)}, f32[4,64,512]{2,1,0:T(8,128)}, u32[]{:S(2)}, u32[]{:S(2)}) collective-permute-start(f32[4,64,512]{2,1,0:T(8,128)S(1)} %bitcast_reduce_fusion.1), channel_id=1, source_target_pairs={{4,0},{8,4},{12,8},{16,12},{20,16},{24,20},{28,24},{32,28},{36,32}... | collective-permute-start | bytes 1572872 | tf_op jit(solution)/shard_map/ppermute | solution.py:21
  90.5 59.7 %collective-permute-start.5 = (f32[5,64,512]{2,1,0:T(8,128)}, f32[5,64,512]{2,1,0:T(8,128)}, u32[]{:S(2)}, u32[]{:S(2)}) collective-permute-start(f32[5,64,512]{2,1,0:T(8,128)} %get-tuple-element.158), channel_id=1, source_target_pairs={{4,0},{8,4},{12,8},{16,12},{20,16},{24,20},{28,24},{32,28},{36,32}... | collective-permute-start | bytes 1966088 | tf_op jit(solution)/shard_map/ppermute | solution.py:21
  92.6 68.0 %collective-permute-start.2 = (f32[8,64,512]{2,1,0:T(8,128)}, f32[8,64,512]{2,1,0:T(8,128)}, u32[]{:S(2)}, u32[]{:S(2)}) collective-permute-start(f32[8,64,512]{2,1,0:T(8,128)} %get-tuple-element.155), channel_id=1, source_target_pairs={{0,4},{4,8},{8,12},{12,16},{16,20},{20,24},{24,28},{28,32},{32,36}... | collective-permute-start | bytes 3145736 | tf_op jit(solution)/shard_map/ppermute | solution.py:18
  131.1 29.5 %collective-permute-start.3 = (f32[8,64,512]{2,1,0:T(8,128)}, f32[8,64,512]{2,1,0:T(8,128)}, u32[]{:S(2)}, u32[]{:S(2)}) collective-permute-start(f32[8,64,512]{2,1,0:T(8,128)} %get-tuple-element.156), channel_id=1, source_target_pairs={{4,0},{8,4},{12,8},{16,12},{20,16},{24,20},{28,24},{32,28},{36,32}... | collective-permute-start | bytes 3145736 | tf_op jit(solution)/shard_map/ppermute | solution.py:21
  136.2 38.2 %collective-permute-start = (bf16[6,256,512]{2,1,0:T(8,128)(2,1)}, bf16[6,256,512]{2,1,0:T(8,128)(2,1)}, u32[]{:S(2)}, u32[]{:S(2)}) collective-permute-start(bf16[6,256,512]{2,1,0:T(8,128)(2,1)} %get-tuple-element.153), channel_id=1, source_target_pairs={{0,4},{4,8},{8,12},{12,16},{16,20},{20,24},{24,28},{28,32},{32,36}... | collective-permute-start | bytes 4718600 | tf_op jit(solution)/shard_map/ppermute | solution.py:18
  136.2 5.1 %copy-start.9 = (f32[5,64,512]{2,1,0:T(8,128)}, f32[5,64,512]{2,1,0:T(8,128)S(1)}, u32[]{:S(2)}) copy-start(f32[5,64,512]{2,1,0:T(8,128)S(1)} %collective-permute-done.4) | copy-start | bytes 1966084
  136.2 38.1 %collective-permute-start.1 = (bf16[6,256,512]{2,1,0:T(8,128)(2,1)}, bf16[6,256,512]{2,1,0:T(8,128)(2,1)}, u32[]{:S(2)}, u32[]{:S(2)}) collective-permute-start(bf16[6,256,512]{2,1,0:T(8,128)(2,1)} %get-tuple-element.154), channel_id=1, source_target_pairs={{4,0},{8,4},{12,8},{16,12},{20,16},{24,20},{28,24},{32,28},{36,32}... | collective-permute-start | bytes 4718600 | tf_op jit(solution)/shard_map/ppermute | solution.py:21
  157.0 3.5 copy-start.3
  164.7 4.4 %copy-start.10 = (f32[16,1,64,64]{3,2,1,0:T(8,128)S(1)}, f32[16,1,64,64]{3,2,1,0:T(8,128)}, u32[]{:S(2)}) copy-start(f32[16,1,64,64]{3,2,1,0:T(8,128)} %param.23) | copy-start | bytes 786436
  169.1 5.2 %copy-start.4 = (bf16[16,256,512]{2,1,0:T(8,128)(2,1)S(1)}, bf16[16,256,512]{2,1,0:T(8,128)(2,1)}, u32[]{:S(2)}) copy-start(bf16[16,256,512]{2,1,0:T(8,128)(2,1)} %all-gather.3.cloned.1.call-done) | copy-start | bytes 12582916
  (8 other events, 19.0 us)
Sparse Core Ops, SparseCore 0:
  9.9 64.6 all-reduce.3
  76.5 50.6 all-gather.2
  130.4 87.9 all-gather.4
  246.9 89.6 all-reduce.5
where the time goes:
time: 378 us; the launch traced here: 375 us
  waiting for transfers between devices  138 us (37%)
  local copies, waits for them, and re-layouts  103 us (27%)
  matrix products  69.9 us (18%)
  other arithmetic  34.3 us (9%)
  starting transfers between devices  15.9 us (4%)
  between operations  13.5 us (4%)
    gather x12, local copies, waits for them, and re-layouts, near_slot(): jnp.take(extended, lax.dynamic_index_in_dim(local_near, slot_at, 1, False...  71.1 us
    psum x1, waiting for transfers between devices, body(): moments_fine = lax.psum(partial_moments, 'lvl')  64 us
    dot_general x12, matrix products, near_slot(): jnp.einsum('cpq,cqr->cpr', block, picked, preferred_element_type=jnp.floa...  42.1 us
    all_gather x1, waiting for transfers between devices, body(): lax.all_gather(moments_root.astype(jnp.bfloat16), 'leaf', axis=0, tiled=T...  38.6 us
    all_gather x1, waiting for transfers between devices, body(): whole_points = lax.all_gather(charges, 'lvl', axis=1, tiled=True)  34.6 us
    gather x5, local copies, waits for them, and re-layouts, coupled_terms(): picked = jnp.take(sources, columns[:, slot_at], axis=0)  23.4 us
    concatenate x4, other arithmetic, padded(): block = jnp.concatenate([low, block, high], axis=dim)  15.5 us
    dot_general x5, matrix products, coupled_terms(): jnp.einsum('cab,cbr->car', blocks[:, slot_at], picked, precision=lax.Prec...  14.6 us
  transfers between devices with their start and end apart: 12, of which 3 were waited for; matrix products, arithmetic and copies ran while one was open for 45% of the time, Pallas kernels for 0%

commit v1 on v0

v1 whole, which is shorter than its diff:
```python
import jax
import jax.numpy as jnp
from jax import lax
from jax.experimental import pallas as pl
from jax.experimental.pallas import tpu as pltpu
from jax.sharding import PartitionSpec as P

MIB = 1 << 20
BF = jnp.bfloat16
F32 = jnp.float32
ZS, XS, CS, LV = 8, 4, 2, 4
LEAVES, POINTS, VECTORS, RANK = 16, 64, 512, 64
PART = VECTORS // LV
LOW, HIGH = 6, 5
RELATIVE = (0, -1, 1, 2)


def shape(dims, dtype=BF):
    return jax.ShapeDtypeStruct(dims, dtype)


def mm(a, b):
    return jnp.dot(a, b, preferred_element_type=F32)


def leaf_pairs(dz=0, dx=0, dcore=0, step=0):
    pairs = []
    for at in range(ZS * XS * CS):
        z, x, core = at // (XS * CS), at // CS % XS, at % CS
        to = (((z + dz) % ZS) * XS + (x + dx) % XS) * CS + (core + dcore) % CS
        pairs.append((at, (to + step) % (ZS * XS * CS)))
    return pairs


def over_leaf(array, **move):
    return lax.ppermute(array, "leaf", leaf_pairs(**move))


def over_lvl(array, step):
    return lax.ppermute(array, "lvl", [(i, (i + step) % LV) for i in range(LV)])


SMEM = pl.BlockSpec(memory_space=pltpu.SMEM)
ANY = pl.BlockSpec(memory_space=pl.ANY)
HBM = pl.BlockSpec(memory_space=pltpu.HBM)


def after(array, *others):
    return lax.optimization_barrier((array,) + others)[0]


def kernel_call(kernel, scalars, arrays, outs, scratch=(), copies=32, limit=16, given=(), flops=10**6):
    return pl.pallas_call(
        kernel,
        out_shape=outs,
        in_specs=[SMEM] * len(scalars) + [ANY] * len(arrays) + [HBM] * len(given),
        out_specs=jax.tree.map(lambda _: ANY, outs),
        scratch_shapes=list(scratch) + [pltpu.SemaphoreType.DMA((copies,))],
        cost_estimate=pl.CostEstimate(flops=flops, bytes_accessed=10**5, transcendentals=0),
        compiler_params=pltpu.CompilerParams(vmem_limit_bytes=limit * MIB),
    )(*scalars, *arrays, *given)


class Copies:
    def __init__(self, sems):
        self.sems, self.count = sems, 0

    def start(self, source, target):
        copy = pltpu.make_async_copy(source, target, self.sems.at[self.count])
        self.count += 1
        copy.start()
        return copy


    def either(self, first, sources, target):
        at = self.sems.at[self.count]
        self.count += 1
        pl.when(first)(lambda: pltpu.make_async_copy(sources[0], target, at).start())
        pl.when(jnp.logical_not(first))(lambda: pltpu.make_async_copy(sources[1], target, at).start())
        return pltpu.make_async_copy(sources[0], target, at)


def lanes_of(k):
    return slice(RANK * (k % 8), RANK * (k % 8 + 1))


def own_core():
    return lax.rem(lax.axis_index("leaf"), CS)


def lvl_at(k):
    return lax.rem(lax.axis_index("lvl") + RELATIVE[k] + LV, LV)


def lifted(transfer, moments, count):
    parents = []
    for q in range(count // 2):
        both = transfer[2 * q : 2 * q + 2].reshape(2 * RANK, RANK).astype(BF).T
        parents.append(mm(both, jnp.concatenate(moments[2 * q : 2 * q + 2], axis=0)).astype(BF))
    return parents


def pack_kernel(
    charges, basis, fine_c, middle_c, coarse_c, top_c, edge, inner,
    v_edge, v_inner, v_basis, v_fine, v_middle, v_coarse, v_top, sems,
):
    copies = Copies(sems)
    edges = [
        copies.start(charges.at[pl.ds(0, 5)], v_edge.at[pl.ds(0, 5)]),
        copies.start(charges.at[pl.ds(10, 6)], v_edge.at[pl.ds(5, 6)]),
    ]
    loads = [copies.start(basis, v_basis), copies.start(charges.at[pl.ds(5, 5)], v_inner.at[pl.ds(0, 5)])]
    loads += [copies.start(a, b) for a, b in ((fine_c, v_fine), (middle_c, v_middle), (coarse_c, v_coarse), (top_c, v_top))]
    for load in edges:
        load.wait()
    out = [copies.start(v_edge, edge)]
    for load in loads:
        load.wait()
    for c in range(LEAVES):
        v_inner[5 + c // 8, :, lanes_of(c)] = v_basis[c].T
    blocks = [v_fine[c, 0] for c in range(16)] + [v_middle[c, 0] for c in range(8)]
    blocks += [v_coarse[c, 0] for c in range(4)] + [v_top[i, s] for i in range(2) for s in range(2)]
    for at, block in enumerate(blocks):
        v_inner[7 + at // 8, :, lanes_of(at)] = block.astype(BF)
    out.append(copies.start(v_inner, inner))
    for copy in out:
        copy.wait()


def leaf_of(edge, inner, c):
    if c < 5:
        return edge[c]
    return inner[c - 5] if c < 10 else edge[c - 5]


def basis_of(inner, c):
    return inner[5 + c // 8, :, lanes_of(c)]


def root_kernel(
    fine_cols, middle_cols, coarse_cols, top_cols, edge, inner, fine_t, middle_t, coarse_t,
    part0, part1, part2, part3, v_edge, v_inner, v_fine, v_middle, v_coarse, roots, sems,
):
    copies = Copies(sems)
    loads = [
        copies.start(a, b)
        for a, b in ((edge, v_edge), (inner.at[pl.ds(0, 7)], v_inner), (fine_t, v_fine), (middle_t, v_middle), (coarse_t, v_coarse))
    ]
    lane = lax.broadcasted_iota(jnp.int32, (16, PART), 1)
    info = jnp.zeros((16, PART), F32)
    leaf = lax.axis_index("leaf")
    at = 0
    for cols, count, total in ((fine_cols, 16, 1024), (middle_cols, 8, 512), (coarse_cols, 4, 256)):
        for c in range(count):
            away = ((cols[c] - leaf * count - c + total // 2) & (total - 1)) - total // 2
            info = jnp.where(lane == at, away.astype(F32), info)
            at += 1
    for i in range(2):
        for s in range(2):
            info = jnp.where(lane == at, top_cols[i, s].astype(F32), info)
            at += 1
    for load in loads:
        load.wait()
    moments = []
    for c in range(LEAVES):
        moments.append(mm(basis_of(v_inner, c), leaf_of(v_edge, v_inner, c)).astype(BF))
    moments = lifted(v_fine, moments, 16)
    moments = lifted(v_middle, moments, 8)
    moments = lifted(v_coarse, moments, 4)
    for j in range(LV):
        for i in range(2):
            roots[j, RANK * i : RANK * (i + 1)] = moments[i][:, PART * j : PART * (j + 1)]
        roots[j, 128:144] = info.astype(BF)
    out = [
        copies.start(roots.at[lax.rem(lax.axis_index("lvl") + k, LV)], part)
        for k, part in enumerate((part0, part1, part2, part3))
    ]
    for copy in out:
        copy.wait()


def read_columns(copies, parts, v_parts, v_cols, s_cols, columns):
    for load in [copies.start(part.at[pl.ds(128, 16)], v_parts.at[k]) for k, part in enumerate(parts)]:
        load.wait()
    for k in range(LV):
        v_cols[k] = v_parts[k].astype(F32)[0:8].astype(jnp.int32)
    copies.start(v_cols, s_cols).wait()
    return copies.start(v_cols, columns)


def columns_scratch():
    return [
        pltpu.VMEM((LV, 16, PART), BF), pltpu.VMEM((LV, 8, PART), jnp.int32), pltpu.SMEM((LV, 8, PART), jnp.int32),
    ]


def moments_kernel(
    edge0, inner0, edge1, inner1, edge2, inner2, edge3, inner3, fine_t, middle_t,
    fine_m, middle_m, coarse_m, to_right, to_left, edges, inners, v_fine, v_middle, moments, sems,
):
    copies = Copies(sems)
    loads = [copies.start(a, edges.at[k]) for k, a in enumerate((edge0, edge1, edge2, edge3))]
    loads += [copies.start(a.at[pl.ds(0, 7)], inners.at[k]) for k, a in enumerate((inner0, inner1, inner2, inner3))]
    loads += [copies.start(fine_t, v_fine), copies.start(middle_t, v_middle)]
    for load in loads:
        load.wait()
    fine = []
    for c in range(LEAVES):
        turned = [basis_of(inners.at[k], c) for k in range(LV)]
        points = [leaf_of(edges.at[k], inners.at[k], c) for k in range(LV)]
        fine.append(mm(jnp.concatenate(turned, axis=1), jnp.concatenate(points, axis=0)).astype(BF))
        moments[c] = fine[c]
    out = [
        copies.start(moments.at[pl.ds(8, 8)], to_right.at[pl.ds(0, 8)]),
        copies.start(moments.at[pl.ds(0, 8)], to_left.at[pl.ds(0, 8)]),
        copies.start(moments.at[pl.ds(0, 16)], fine_m),
    ]
    middle = lifted(v_fine, fine, 16)
    for c in range(8):
        moments[16 + c] = middle[c]
    out += [
        copies.start(moments.at[pl.ds(19, 5)], to_right.at[pl.ds(8, 5)]),
        copies.start(moments.at[pl.ds(16, 5)], to_left.at[pl.ds(8, 5)]),
        copies.start(moments.at[pl.ds(16, 8)], middle_m),
    ]
    coarse = lifted(v_middle, middle, 8)
    for c in range(4):
        moments[24 + c] = coarse[c]
    out += [copies.start(moments.at[pl.ds(24, 4)], to.at[pl.ds(13, 4)]) for to in (to_right, to_left)]
    out.append(copies.start(moments.at[pl.ds(24, 4)], coarse_m))
    for copy in out:
        copy.wait()


def ends_kernel(edge0, edge1, edge2, edge3, to_core, to_chip, v_core, v_chip, sems):
    copies = Copies(sems)
    core = own_core()
    loads = []
    for k, edge in enumerate((edge0, edge1, edge2, edge3)):
        loads.append(copies.start(edge.at[pl.ds(HIGH - HIGH * core, LOW)], v_core.at[pl.ds(LOW * k, LOW)]))
        loads.append(copies.start(edge.at[pl.ds(HIGH * core, LOW)], v_chip.at[pl.ds(LOW * k, LOW)]))
    for load in loads:
        load.wait()
    out = [copies.start(v_chip, to_chip), copies.start(v_core, to_core)]
    for copy in out:
        copy.wait()


def core_swap(array):
    return over_leaf(array, dcore=1)


def chip_swap(array):
    leaves = ZS * XS * CS
    return lax.ppermute(array, "leaf", [(i, (i + (1 if i % CS else -1)) % leaves) for i in range(leaves)])


def joined_kernel(*refs):
    copies = Copies(refs[-1])
    held, target, loads, out, at = refs[-2], refs[-3], [], [], 0
    for piece in refs[:-3]:
        loads.append((at, piece.shape[0], copies.start(piece, held.at[pl.ds(at, piece.shape[0])])))
        at += piece.shape[0]
    for at, count, load in loads:
        load.wait()
        out.append(copies.start(held.at[pl.ds(at, count)], target.at[pl.ds(at, count)]))
    for copy in out:
        copy.wait()


def joined(*pieces, flops=10**6):
    dims = (sum(piece.shape[0] for piece in pieces),) + pieces[0].shape[1:]
    return kernel_call(joined_kernel, (), pieces, shape(dims), scratch=[pltpu.VMEM(dims, BF)], flops=flops)


def near_kernel(
    near_cols, edge0, inner0, edge1, inner1, edge2, inner2, edge3, inner3, core_ends, chip_ends,
    blocks, out, points, held, total, slots, sems,
):
    copies = Copies(sems)
    block_copies = [copies.start(blocks.at[pl.ds(0, 4)], held.at[pl.ds(0, 4)])]
    even = own_core() == 0
    loads = []
    for k, (edge, inner) in enumerate(((edge0, inner0), (edge1, inner1), (edge2, inner2), (edge3, inner3))):
        row = pl.ds(pl.multiple_of(lvl_at(k) * POINTS, POINTS), POINTS)
        for source, first, count, leaf in ((edge, 0, 5, LOW), (inner, 0, 5, LOW + 5), (edge, 5, 6, LOW + 10)):
            loads.append(copies.start(source.at[pl.ds(first, count)], points.at[pl.ds(leaf, count), row, :]))
        core, chip = (end.at[pl.ds(LOW * k, LOW)] for end in (core_ends, chip_ends))
        loads.append(copies.either(even, (chip, core), points.at[pl.ds(0, LOW), row, :]))
        core, chip = (end.at[pl.ds(LOW * k, HIGH)] for end in (core_ends, chip_ends))
        loads.append(copies.either(even, (core, chip), points.at[pl.ds(LOW + 16, HIGH), row, :]))
    for g in range(1, 4):
        block_copies.append(copies.start(blocks.at[pl.ds(4 * g, 4)], held.at[pl.ds(4 * g, 4)]))
    first_leaf = lax.axis_index("leaf") * LEAVES

    def place_slots(c, carry):
        for s in range(12):
            slots[c, (near_cols[c, s] - first_leaf - c + LOW) & 1023] = s
        return carry

    lax.fori_loop(0, LEAVES, place_slots, 0)
    for load in loads:
        load.wait()
    stores = []
    for g in range(4):
        block_copies[g].wait()
        for source in range(15):
            held_by = [c for c in range(4) if 0 <= source - c < 12]
            rows = jnp.concatenate([held[4 * g + c, slots[4 * g + c, source - c]] for c in held_by], axis=0)
            product = mm(rows, points[4 * g + source])
            for i, c in enumerate(held_by):
                piece = product[POINTS * i : POINTS * (i + 1)]
                total[4 * g + c] = piece if source == c else total[4 * g + c] + piece
        stores.append(copies.start(total.at[pl.ds(4 * g, 4)], out.at[pl.ds(4 * g, 4)]))
    for store in stores:
        store.wait()


def top_kernel(
    part0, part1, part2, part3, own, up, down, far, mine, partner, out, columns,
    v_parts, v_cols, s_cols, v_couplings, sources, result, sems,
):
    copies = Copies(sems)
    loads = [
        copies.start(piece.at[pl.ds(10, 1), :, pl.ds(256, 256)], v_couplings.at[pl.ds(k, 1)])
        for k, piece in enumerate((own, up, down, far))
    ]
    store = read_columns(copies, (part0, part1, part2, part3), v_parts, v_cols, s_cols, columns)
    leaf = lax.axis_index("leaf")
    for k in range(LV):
        for j in range(4):
            root = s_cols[k, 0, 28 + j]
            there = root // 2
            hop = lax.rem(there // CS % XS - leaf // CS % XS + XS, XS)
            hop = jnp.where(hop == 3, 1, jnp.where(hop == 1, 2, jnp.where(hop == 2, 3, 0)))
            up_z = lax.rem(there // (XS * CS) - leaf // (XS * CS) + 4 + ZS, ZS)
            spot = hop * 16 + up_z * 2 + lax.rem(root, 2)
            here = lax.rem(there, CS) == lax.rem(leaf, CS)
            target = sources.at[(j // 2) * 8 + k * 2 + j % 2]
            loads.append(copies.either(here, (mine.at[spot], partner.at[spot]), target))
    for load in loads:
        load.wait()
    for i in range(2):
        lhs = jnp.concatenate([v_couplings[k, :, 128 * i : 128 * (i + 1)] for k in range(LV)], axis=1)
        rhs = jnp.concatenate([sources[8 * i + n] for n in range(8)], axis=0)
        result[i] = mm(lhs, rhs).astype(BF)
    copies.start(result, out).wait()
    store.wait()


def last_kernel(
    s_cols, fine_m, middle_m, coarse_m, low, high, inner0, inner1, inner2, inner3,
    own_t, up_t, down_t, far_t, near, fine_t, middle_t, coarse_t, basis, out,
    wide, v_couplings, top, v_fine, v_middle, v_coarse, v_basis, v_near, v_out, sems,
):
    copies = Copies(sems)
    early = []
    for k, inner in enumerate((inner0, inner1, inner2, inner3)):
        early.append(copies.start(inner.at[pl.ds(7, 4)], v_couplings.at[k]))
    early += [
        copies.start(coarse_t, v_coarse), copies.start(low.at[pl.ds(13, 4)], wide.at[pl.ds(0, 4)]),
        copies.start(coarse_m, wide.at[pl.ds(4, 4)]), copies.start(high.at[pl.ds(13, 4)], wide.at[pl.ds(8, 4)]),
    ]
    for k, piece in enumerate((own_t, up_t, down_t, far_t)):
        early.append(copies.start(piece, top.at[lvl_at(k)]))
    early_middle = [
        copies.start(middle_t, v_middle), copies.start(low.at[pl.ds(8, 5)], wide.at[pl.ds(12, 5)]),
        copies.start(middle_m, wide.at[pl.ds(17, 8)]), copies.start(high.at[pl.ds(8, 5)], wide.at[pl.ds(25, 5)]),
    ]
    early_fine = [
        copies.start(fine_t, v_fine), copies.start(basis, v_basis), copies.start(low.at[pl.ds(0, 8)], wide.at[pl.ds(30, 8)]),
        copies.start(fine_m, wide.at[pl.ds(38, 16)]), copies.start(high.at[pl.ds(0, 8)], wide.at[pl.ds(54, 8)]),
    ]
    near_loads = [copies.start(near.at[pl.ds(4 * g, 4)], v_near.at[pl.ds(4 * g, 4)]) for g in range(4)]

    def term(place, c, at):
        lhs = jnp.concatenate([v_couplings[k, at // 8, :, lanes_of(at)] for k in range(LV)], axis=1)
        return mm(lhs, jnp.concatenate([wide[place + c + s_cols[k, at]] for k in range(LV)], axis=0))

    for load in early:
        load.wait()
    coarse = []
    for c in range(4):
        parent = jnp.concatenate([top[j, c // 2] for j in range(LV)], axis=1)
        coarse.append((term(4, c, 24 + c) + mm(v_coarse[c].astype(BF), parent)).astype(BF))
    for load in early_middle:
        load.wait()
    middle = [
        (term(17, c, 16 + c) + mm(v_middle[c].astype(BF), coarse[c // 2])).astype(BF) for c in range(8)
    ]
    for load in early_fine:
        load.wait()
    stores = []
    for c in range(16):
        if c % 4 == 0:
            near_loads[c // 4].wait()
        local = term(38, c, c) + mm(v_fine[c].astype(BF), middle[c // 2])
        v_out[c] = (v_near[c] + mm(v_basis[c], local.astype(BF))).astype(BF)
        if c % 4 == 3:
            stores.append(copies.start(v_out.at[pl.ds(c - 3, 4)], out.at[pl.ds(c - 3, 4)]))
    for store in stores:
        store.wait()


def body(
    charges, leaf_basis, near_blocks, near_cols, coupling_fine, coupling_middle, coupling_coarse,
    far_cols_fine, far_cols_middle, far_cols_coarse, transfer_fine, transfer_middle, transfer_coarse,
    top_coupling, top_cols,
):
    v = pltpu.VMEM
    unit = shape((11, 64, 512))
    edge0, inner0 = kernel_call(
        pack_kernel,
        (),
        (),
        given=(charges, leaf_basis, coupling_fine, coupling_middle, coupling_coarse, top_coupling),
        outs=(unit, unit),
        limit=60,
        scratch=[
            v((11, 64, 512), BF), v((11, 64, 512), BF), v((16, 64, 64), BF), v((16, 1, 64, 64), F32),
            v((8, 1, 64, 64), F32), v((4, 1, 64, 64), F32), v((2, 2, 64, 64), F32),
        ],
    )
    edge1, edge2 = over_lvl(edge0, 1), over_lvl(edge0, -1)
    part = shape((144, PART))
    part0, part1, part2, part3 = kernel_call(
        root_kernel,
        (far_cols_fine.reshape(16), far_cols_middle.reshape(8), far_cols_coarse.reshape(4), top_cols),
        (edge0, inner0),
        (part,) * 4,
        given=(transfer_fine, transfer_middle, transfer_coarse),
        limit=60,
        scratch=[
            v((11, 64, 512), BF), v((7, 64, 512), BF), v((16, 64, 64), F32), v((8, 64, 64), F32), v((4, 64, 64), F32),
            v((LV, 144, PART), BF),
        ],
    )
    up_p, far_p, down_p = over_lvl(part1, 1), over_lvl(part2, 2), over_lvl(part3, 3)
    parts = (part0, up_p, down_p, far_p)
    root = sum(p[0:128].astype(F32) for p in parts).astype(BF).reshape(2, RANK, PART)

    edge3 = over_lvl(edge1, 1)
    late = after(inner0, up_p, down_p, far_p)
    inner2, inner1 = over_lvl(late, -1), over_lvl(late, 1)
    inner3 = over_lvl(inner2, -1)

    root = after(root, edge1, edge2)
    below, above = over_leaf(root, dz=1), over_leaf(root, dz=-1)
    three = jnp.concatenate([below, root, above], axis=0)
    far_below, far_above = over_leaf(three, dz=3), over_leaf(three[0:4], dz=-3)
    column = joined(far_below, three, far_above)
    column = after(column, inner2, edge3)
    left, right = over_leaf(column, dx=1), over_leaf(column, dx=-1)
    to_core, to_chip = kernel_call(
        ends_kernel,
        (),
        (edge0, edge1, edge2, after(edge3, left, right)),
        (shape((24, 64, 512)),) * 2,
        scratch=[v((24, 64, 512), BF)] * 2,
    )
    core_ends, chip_ends = core_swap(to_core), chip_swap(to_chip)
    across_a, across_b = over_leaf(left[0:8], dx=1), over_leaf(right[8:16], dx=-1)

    pairs = (edge0, inner0, edge1, inner1, edge2, inner2, edge3, inner3)
    fine_m, middle_m, coarse_m, to_right, to_left = kernel_call(
        moments_kernel,
        (),
        pairs,
        given=(transfer_fine, transfer_middle),
        outs=(shape((16, 64, 512)), shape((8, 64, 512)), shape((4, 64, 512))) + (shape((17, 64, 512)),) * 2,
        scratch=[
            v((LV, 11, 64, 512), BF), v((LV, 7, 64, 512), BF), v((16, 64, 64), F32), v((8, 64, 64), F32),
            v((28, 64, 512), BF),
        ],
    )
    low_m, high_m = over_leaf(to_right, step=1), over_leaf(to_left, step=-1)

    plane = joined(column, left, right, after(across_a, fine_m, core_ends, chip_ends), across_b)
    partner = core_swap(plane)
    inners = (inner0, inner1, inner2, inner3)
    term_top, columns = kernel_call(
        top_kernel,
        (),
        parts + inners + (plane, partner),
        (shape((2, 64, PART)), shape((LV, 8, PART), jnp.int32)),
        scratch=columns_scratch() + [v((LV, 64, 256), BF), v((16, 64, PART), BF), v((2, 64, PART), BF)],
    )
    up_t, down_t, far_t = over_lvl(term_top, 1), over_lvl(term_top, -1), over_lvl(term_top, 2)

    near = kernel_call(
        near_kernel,
        (near_cols,),
        pairs + (core_ends, chip_ends),
        shape((16, 64, 512), F32),
        given=(near_blocks,),
        limit=24,
        scratch=[
            v((27, 256, 512), BF), v((16, 12, 64, 256), BF), v((16, 64, 512), F32), pltpu.SMEM((16, 12), jnp.int32),
        ],
    )
    return kernel_call(
        last_kernel,
        (columns[:, 0, 0:32],),
        (fine_m, middle_m, coarse_m, low_m, high_m) + inners + (term_top, up_t, down_t, far_t, near),
        shape((16, 64, 512)),
        given=(transfer_fine, transfer_middle, transfer_coarse, leaf_basis),
        copies=40,
        scratch=[
            v((62, 64, 512), BF), v((LV, 4, 64, 512), BF), v((LV, 2, 64, PART), BF), v((16, 64, 64), F32),
            v((8, 64, 64), F32), v((4, 64, 64), F32), v((16, 64, 64), BF), v((16, 64, 512), F32), v((16, 64, 512), BF),
        ],
    )


def solution(mesh):
    placed = (
        P("leaf", "lvl", None),
        P("leaf", "lvl", None),
        P("leaf", None, "lvl", None),
        P("leaf", None),
        P("leaf", "lvl", None, None),
        P("leaf", "lvl", None, None),
        P("leaf", "lvl", None, None),
        P("leaf", "lvl"),
        P("leaf", "lvl"),
        P("leaf", "lvl"),
        P("leaf", None, None),
        P("leaf", None, None),
        P("leaf", None, None),
        P("leaf", "lvl", None, None),
        P("leaf", "lvl"),
    )
    return jax.shard_map(
        body, mesh=mesh, in_specs=placed, out_specs=P("leaf", "lvl", None), check_vma=False
    )
```

time: 378 us -> 116 us (0.31)
  the two profiles are of different devices: /device:TPU:24 before, /device:TPU:1 now
where the time goes in v1:
time: 116 us
  starting transfers between devices  46.2 us (40%)
  waiting for transfers between devices  35.4 us (31%)
  Pallas kernels  32.9 us (28%)
    pallas_call x9, Pallas kernels, kernel_call(): pl.pallas_call(kernel, out_shape=outs, in_specs=[SMEM] * len(scalars) + [...  32.9 us
    ppermute x12, starting transfers between devices, over_leaf(): return lax.ppermute(array, 'leaf', leaf_pairs(**move))  30.4 us
    ppermute x12, waiting for transfers between devices, over_lvl(): return lax.ppermute(array, 'lvl', [(i, (i + step) % LV) for i in range(LV)])  22.9 us
    ppermute x12, starting transfers between devices, over_lvl(): return lax.ppermute(array, 'lvl', [(i, (i + step) % LV) for i in range(LV)])  14.4 us
    ppermute x12, waiting for transfers between devices, over_leaf(): return lax.ppermute(array, 'leaf', leaf_pairs(**move))  12.5 us
  transfers between devices with their start and end apart: 25, of which 8 were waited for; matrix products, arithmetic and copies ran while one was open for 1% of the time, Pallas kernels for 18%

profile of v1, /device:TPU:1, one launch (start us, length us, event | category | flops | bytes accessed | tf_op | source)
XLA Modules:
  0.0 115.8 jit_solution(13658869436637711403)
XLA Ops:
  0.0 3.0 %shard_map.145 = (bf16[11,64,512]{2,1,0:T(8,128)(2,1)}, bf16[11,64,512]{2,1,0:T(8,128)(2,1)}) custom-call(bf16[16,64,512]{2,1,0:T(8,128)(2,1)} %charges.1, bf16[16,64,64]{2,1,0:T(8,128)(2,1)} %basis.3, f32[16,1,64,64]{3,2,1,0:T(8,128)} %fine_c.1, f32[8,1,64,64]{3,2,1,0:T(8,128)} %middle_c.1, f32[4,1,64,64]{3,2,1,0:T(8,128)} %coarse_c.1, f32[2,2,64,64]{3,2,1,0:T(8,128)} %top_c.1), custom_call_target="tpu_custom_call" | custom-call | flops 1000000 | bytes 100000 | tf_op jit(solution)/shard_map/pallas_call | solution.py:53
  3.1 2.2 %collective-permute-start.6 = (bf16[11,64,512]{2,1,0:T(8,128)(2,1)}, bf16[11,64,512]{2,1,0:T(8,128)(2,1)S(1)}, u32[]{:S(2)}, u32[]{:S(2)}) collective-permute-start(bf16[11,64,512]{2,1,0:T(8,128)(2,1)} %get-tuple-element.25.edge.edge0), channel_id=1, source_target_pairs={{0,1},{1,2},{2,3},{3,0},{4,5},{5,6},{6,7},{7,4},{8,9},{9,10},{10,1... | collective-permute-start | bytes 2162696 | tf_op jit(solution)/shard_map/ppermute | solution.py:40
  5.3 1.5 %collective-permute-start.7 = (bf16[11,64,512]{2,1,0:T(8,128)(2,1)}, bf16[11,64,512]{2,1,0:T(8,128)(2,1)S(1)}, u32[]{:S(2)}, u32[]{:S(2)}) collective-permute-start(bf16[11,64,512]{2,1,0:T(8,128)(2,1)} %get-tuple-element.25.edge.edge0), channel_id=1, source_target_pairs={{0,3},{1,0},{2,1},{3,2},{4,7},{5,4},{6,5},{7,6},{8,11},{9,8},{10,9... | collective-permute-start | bytes 2162696 | tf_op jit(solution)/shard_map/ppermute | solution.py:40
  6.8 4.2 %shard_map.146 = (bf16[144,128]{1,0:T(8,128)(2,1)}, bf16[144,128]{1,0:T(8,128)(2,1)}, bf16[144,128]{1,0:T(8,128)(2,1)}, bf16[144,128]{1,0:T(8,128)(2,1)}) custom-call(s32[16]{0:T(128)} %bitcast.12, s32[8]{0:T(128)} %bitcast.13, s32[4]{0:T(128)} %bitcast.14, s32[2,2]{1,0:T(2,128)} %top_cols.1, bf16[11,64,512]{2,1,0:T(8,128)(2,1)} %get-tuple-element.25.edge.edge0, ...), custom_call_target="tpu_custom_call" | custom-call | flops 1000000 | bytes 100000 | tf_op jit(solution)/shard_map/pallas_call | solution.py:53
  11.1 2.7 %collective-permute-start.1 = (bf16[144,128]{1,0:T(8,128)(2,1)}, bf16[144,128]{1,0:T(8,128)(2,1)S(1)}, u32[]{:S(2)}, u32[]{:S(2)}) collective-permute-start(bf16[144,128]{1,0:T(8,128)(2,1)} %get-tuple-element.29), channel_id=1, source_target_pairs={{0,3},{1,0},{2,1},{3,2},{4,7},{5,4},{6,5},{7,6},{8,11},{9,8},{10,9... | collective-permute-start | bytes 110600 | tf_op jit(solution)/shard_map/ppermute | solution.py:40
  14.1 7.5 %collective-permute-done.part1 = bf16[144,128]{1,0:T(8,128)(2,1)S(1)} collective-permute-done((bf16[144,128]{1,0:T(8,128)(2,1)}, bf16[144,128]{1,0:T(8,128)(2,1)S(1)}, u32[]{:S(2)}, u32[]{:S(2)}) %collective-permute-start) | collective-permute-done | bytes 36896 | tf_op jit(solution)/shard_map/ppermute | solution.py:40
  22.7 2.2 %collective-permute-done.2.part3 = bf16[144,128]{1,0:T(8,128)(2,1)S(1)} collective-permute-done((bf16[144,128]{1,0:T(8,128)(2,1)}, bf16[144,128]{1,0:T(8,128)(2,1)S(1)}, u32[]{:S(2)}, u32[]{:S(2)}) %collective-permute-start.2) | collective-permute-done | bytes 36896 | tf_op jit(solution)/shard_map/ppermute | solution.py:40
  27.2 1.7 %collective-permute-start.8 = (bf16[2,64,128]{2,1,0:T(8,128)(2,1)S(1)}, bf16[2,64,128]{2,1,0:T(8,128)(2,1)S(1)}, u32[]{:S(2)}, u32[]{:S(2)}) collective-permute-start(bf16[2,64,128]{2,1,0:T(8,128)(2,1)S(1)} %bitcast.8), channel_id=1, source_target_pairs={{0,32},{4,36},{8,40},{12,44},{16,48},{20,52},{24,56},{28,60},{32,6... | collective-permute-start | bytes 98312 | tf_op jit(solution)/shard_map/ppermute | solution.py:36
  28.9 4.0 %collective-permute-start.9 = (bf16[2,64,128]{2,1,0:T(8,128)(2,1)S(1)}, bf16[2,64,128]{2,1,0:T(8,128)(2,1)S(1)}, u32[]{:S(2)}, u32[]{:S(2)}) collective-permute-start(bf16[2,64,128]{2,1,0:T(8,128)(2,1)S(1)} %bitcast.9), channel_id=1, source_target_pairs={{0,224},{4,228},{8,232},{12,236},{16,240},{20,244},{24,248},{28,25... | collective-permute-start | bytes 98312 | tf_op jit(solution)/shard_map/ppermute | solution.py:36
  34.5 4.3 %collective-permute-start.10 = (bf16[6,64,128]{2,1,0:T(8,128)(2,1)S(1)}, bf16[6,64,128]{2,1,0:T(8,128)(2,1)S(1)}, u32[]{:S(2)}, u32[]{:S(2)}) collective-permute-start(bf16[6,64,128]{2,1,0:T(8,128)(2,1)S(1)} %constant_dynamic-update-slice_fusion.refs_1_), channel_id=1, source_target_pairs={{0,96},{4,100},{8,104},{12,108},{16,112},{20,116},{24,120},{28,124... | collective-permute-start | bytes 294920 | tf_op jit(solution)/shard_map/ppermute | solution.py:36
  39.1 4.9 %collective-permute-done.11.refs_2_ = bf16[4,64,128]{2,1,0:T(8,128)(2,1)S(1)} collective-permute-done((bf16[4,64,128]{2,1,0:T(8,128)(2,1)S(1)}, bf16[4,64,128]{2,1,0:T(8,128)(2,1)S(1)}, u32[]{:S(2)}, u32[]{:S(2)}) %collective-permute-start.11) | collective-permute-done | bytes 65568 | tf_op jit(solution)/shard_map/ppermute | solution.py:36
  47.8 3.8 %collective-permute-done.13.refs_1_ = bf16[16,64,128]{2,1,0:T(8,128)(2,1)S(1)} collective-permute-done((bf16[16,64,128]{2,1,0:T(8,128)(2,1)S(1)}, bf16[16,64,128]{2,1,0:T(8,128)(2,1)S(1)}, u32[]{:S(2)}, u32[]{:S(2)}) %collective-permute-start.13) | collective-permute-done | bytes 262176 | tf_op jit(solution)/shard_map/ppermute | solution.py:36
  51.6 2.0 %shard_map.149 = (bf16[24,64,512]{2,1,0:T(8,128)(2,1)S(1)}, bf16[24,64,512]{2,1,0:T(8,128)(2,1)S(1)}) custom-call(bf16[11,64,512]{2,1,0:T(8,128)(2,1)S(1)} %copy-done.1, bf16[11,64,512]{2,1,0:T(8,128)(2,1)S(1)} %collective-permute-done.6.edge1, bf16[11,64,512]{2,1,0:T(8,128)(2,1)S(1)} %collective-permute-done.7.edge2, ...), custom_call_target="tpu_custom_call" | custom-call | flops 1000000 | bytes 100000 | tf_op jit(solution)/shard_map/pallas_call | solution.py:53
  53.6 6.2 %collective-permute-start.16 = (bf16[24,64,512]{2,1,0:T(8,128)(2,1)S(1)}, bf16[24,64,512]{2,1,0:T(8,128)(2,1)S(1)}, u32[]{:S(2)}, u32[]{:S(2)}) collective-permute-start(bf16[24,64,512]{2,1,0:T(8,128)(2,1)S(1)} %get-tuple-element.36), channel_id=1, source_target_pairs={{0,4},{4,0},{8,12},{12,8},{16,20},{20,16},{24,28},{28,24},{32,36},... | collective-permute-start | bytes 4718600 | tf_op jit(solution)/shard_map/ppermute | solution.py:36
  62.0 1.9 %collective-permute-start.5 = (bf16[11,64,512]{2,1,0:T(8,128)(2,1)S(1)}, bf16[11,64,512]{2,1,0:T(8,128)(2,1)S(1)}, u32[]{:S(2)}, u32[]{:S(2)}) collective-permute-start(bf16[11,64,512]{2,1,0:T(8,128)(2,1)S(1)} %collective-permute-done.4.inner2.down), channel_id=1, source_target_pairs={{0,3},{1,0},{2,1},{3,2},{4,7},{5,4},{6,5},{7,6},{8,11},{9,8},{10,9... | collective-permute-start | bytes 2162696 | tf_op jit(solution)/shard_map/ppermute | solution.py:40
  65.0 12.0 %collective-permute-done.3.inner1.up = bf16[11,64,512]{2,1,0:T(8,128)(2,1)S(1)} collective-permute-done((bf16[11,64,512]{2,1,0:T(8,128)(2,1)S(1)}, bf16[11,64,512]{2,1,0:T(8,128)(2,1)S(1)}, u32[]{:S(2)}, u32[]{:S(2)}) %collective-permute-start.3) | collective-permute-done | bytes 720928 | tf_op jit(solution)/shard_map/ppermute | solution.py:40
  77.0 5.4 %collective-permute-start.18 = (bf16[8,64,128]{2,1,0:T(8,128)(2,1)S(1)}, bf16[8,64,128]{2,1,0:T(8,128)(2,1)S(1)}, u32[]{:S(2)}, u32[]{:S(2)}) collective-permute-start(bf16[8,64,128]{2,1,0:T(8,128)(2,1)S(1)} %slice.34), channel_id=1, source_target_pairs={{0,24},{4,28},{8,0},{12,4},{16,8},{20,12},{24,16},{28,20},{32,56},... | collective-permute-start | bytes 393224 | tf_op jit(solution)/shard_map/ppermute | solution.py:36
  82.4 4.5 %shard_map.148 = (bf16[16,64,512]{2,1,0:T(8,128)(2,1)S(1)}, bf16[8,64,512]{2,1,0:T(8,128)(2,1)S(1)}, bf16[4,64,512]{2,1,0:T(8,128)(2,1)S(1)}, bf16[17,64,512]{2,1,0:T(8,128)(2,1)S(1)}, bf16[17,64,512]{2,1,0:T(8,128)(2,1)S(1)}) custom-call(bf16[11,64,512]{2,1,0:T(8,128)(2,1)S(1)} %copy-done.1, bf16[11,64,512]{2,1,0:T(8,128)(2,1)S(1)} %copy-done, ...), custom_call_target="tpu_custom_call" | custom-call | flops 1000000 | bytes 100000 | tf_op jit(solution)/shard_map/pallas_call | solution.py:53
  88.7 4.1 %collective-permute-start.19 = (bf16[64,64,128]{2,1,0:T(8,128)(2,1)S(1)}, bf16[64,64,128]{2,1,0:T(8,128)(2,1)S(1)}, u32[]{:S(2)}, u32[]{:S(2)}) collective-permute-start(bf16[64,64,128]{2,1,0:T(8,128)(2,1)S(1)} %shard_map.150.mine), channel_id=1, source_target_pairs={{0,4},{4,0},{8,12},{12,8},{16,20},{20,16},{24,28},{28,24},{32,36},... | collective-permute-start | bytes 3145736 | tf_op jit(solution)/shard_map/ppermute | solution.py:36
  92.8 2.3 %collective-permute-done.19.partner = bf16[64,64,128]{2,1,0:T(8,128)(2,1)S(1)} collective-permute-done((bf16[64,64,128]{2,1,0:T(8,128)(2,1)S(1)}, bf16[64,64,128]{2,1,0:T(8,128)(2,1)S(1)}, u32[]{:S(2)}, u32[]{:S(2)}) %collective-permute-start.19) | collective-permute-done | bytes 1048608 | tf_op jit(solution)/shard_map/ppermute | solution.py:36
  95.1 2.3 %shard_map.151 = (bf16[2,64,128]{2,1,0:T(8,128)(2,1)S(1)}, s32[4,8,128]{2,1,0:T(8,128)S(1)}) custom-call(bf16[144,128]{1,0:T(8,128)(2,1)S(1)} %copy-done.6, bf16[144,128]{1,0:T(8,128)(2,1)S(1)} %collective-permute-done.part1, bf16[144,128]{1,0:T(8,128)(2,1)S(1)} %collective-permute-done.1.part2, bf16[144,128]{1,0:T(8,128)(2,1)S(1)} %collective-permute-done.2.part3, ...), custom_call_target="tpu_custom_call" | custom-call | flops 1000000 | bytes 100000 | tf_op jit(solution)/shard_map/pallas_call | solution.py:53
  97.4 2.7 %collective-permute-start.23 = (bf16[2,64,128]{2,1,0:T(8,128)(2,1)S(1)}, bf16[2,64,128]{2,1,0:T(8,128)(2,1)S(1)}, u32[]{:S(2)}, u32[]{:S(2)}) collective-permute-start(bf16[2,64,128]{2,1,0:T(8,128)(2,1)S(1)} %get-tuple-element.44.own_t), channel_id=1, source_target_pairs={{0,3},{1,0},{2,1},{3,2},{4,7},{5,4},{6,5},{7,6},{8,11},{9,8},{10,9... | collective-permute-start | bytes 98312 | tf_op jit(solution)/shard_map/ppermute | solution.py:40
  100.7 7.3 %shard_map.152.near = f32[16,64,512]{2,1,0:T(8,128)S(1)} custom-call(s32[16,12]{1,0:T(8,128)S(1)} %copy-done.7, bf16[11,64,512]{2,1,0:T(8,128)(2,1)S(1)} %copy-done.1, bf16[11,64,512]{2,1,0:T(8,128)(2,1)S(1)} %copy-done, bf16[11,64,512]{2,1,0:T(8,128)(2,1)S(1)} %collective-permute-done.6.edge1, bf16[11,64,512]{2,1,0:T(8,128)(2,1)S(1)} %collective-permute-done.3.inner1.up, ...), custom_call_target="tpu_custom_call" | custom-call | flops 1000000 | bytes 100000 | tf_op jit(solution)/shard_map/pallas_call | solution.py:53
  108.1 7.5 %shard_map.153 = bf16[16,64,512]{2,1,0:T(8,128)(2,1)} custom-call(s32[4,32]{1,0:T(4,128)S(1)} %bitcast.7, bf16[16,64,512]{2,1,0:T(8,128)(2,1)S(1)} %get-tuple-element.34.fine_m, bf16[8,64,512]{2,1,0:T(8,128)(2,1)S(1)} %get-tuple-element.40.middle_m, bf16[4,64,512]{2,1,0:T(8,128)(2,1)S(1)} %get-tuple-element.41.coarse_m, ...), custom_call_target="tpu_custom_call" | custom-call | flops 1000000 | bytes 100000 | tf_op jit(solution)/shard_map/pallas_call | solution.py:53
  (64 shorter events, 15.2 us)
Async XLA Ops:
  3.1 22.5 %collective-permute-start.6 = (bf16[11,64,512]{2,1,0:T(8,128)(2,1)}, bf16[11,64,512]{2,1,0:T(8,128)(2,1)S(1)}, u32[]{:S(2)}, u32[]{:S(2)}) collective-permute-start(bf16[11,64,512]{2,1,0:T(8,128)(2,1)} %get-tuple-element.25.edge.edge0), channel_id=1, source_target_pairs={{0,1},{1,2},{2,3},{3,0},{4,5},{5,6},{6,7},{7,4},{8,9},{9,10},{10,1... | collective-permute-start | bytes 2162696 | tf_op jit(solution)/shard_map/ppermute | solution.py:40
  5.3 21.9 %collective-permute-start.7 = (bf16[11,64,512]{2,1,0:T(8,128)(2,1)}, bf16[11,64,512]{2,1,0:T(8,128)(2,1)S(1)}, u32[]{:S(2)}, u32[]{:S(2)}) collective-permute-start(bf16[11,64,512]{2,1,0:T(8,128)(2,1)} %get-tuple-element.25.edge.edge0), channel_id=1, source_target_pairs={{0,3},{1,0},{2,1},{3,2},{4,7},{5,4},{6,5},{7,6},{8,11},{9,8},{10,9... | collective-permute-start | bytes 2162696 | tf_op jit(solution)/shard_map/ppermute | solution.py:40
  11.0 10.5 %collective-permute-start = (bf16[144,128]{1,0:T(8,128)(2,1)}, bf16[144,128]{1,0:T(8,128)(2,1)S(1)}, u32[]{:S(2)}, u32[]{:S(2)}) collective-permute-start(bf16[144,128]{1,0:T(8,128)(2,1)} %get-tuple-element.28), channel_id=1, source_target_pairs={{0,1},{1,2},{2,3},{3,0},{4,5},{5,6},{6,7},{7,4},{8,9},{9,10},{10,1... | collective-permute-start | bytes 110600 | tf_op jit(solution)/shard_map/ppermute | solution.py:40
  11.1 11.6 %collective-permute-start.1 = (bf16[144,128]{1,0:T(8,128)(2,1)}, bf16[144,128]{1,0:T(8,128)(2,1)S(1)}, u32[]{:S(2)}, u32[]{:S(2)}) collective-permute-start(bf16[144,128]{1,0:T(8,128)(2,1)} %get-tuple-element.29), channel_id=1, source_target_pairs={{0,3},{1,0},{2,1},{3,2},{4,7},{5,4},{6,5},{7,6},{8,11},{9,8},{10,9... | collective-permute-start | bytes 110600 | tf_op jit(solution)/shard_map/ppermute | solution.py:40
  13.7 11.2 %collective-permute-start.2 = (bf16[144,128]{1,0:T(8,128)(2,1)}, bf16[144,128]{1,0:T(8,128)(2,1)S(1)}, u32[]{:S(2)}, u32[]{:S(2)}) collective-permute-start(bf16[144,128]{1,0:T(8,128)(2,1)} %get-tuple-element.30), channel_id=1, source_target_pairs={{0,2},{1,3},{2,0},{3,1},{4,6},{5,7},{6,4},{7,5},{8,10},{9,11},{10,... | collective-permute-start | bytes 110600 | tf_op jit(solution)/shard_map/ppermute | solution.py:40
  24.9 20.1 %collective-permute-start.4 = (bf16[11,64,512]{2,1,0:T(8,128)(2,1)S(1)}, bf16[11,64,512]{2,1,0:T(8,128)(2,1)S(1)}, u32[]{:S(2)}, u32[]{:S(2)}) collective-permute-start(bf16[11,64,512]{2,1,0:T(8,128)(2,1)S(1)} %copy-done), channel_id=1, source_target_pairs={{0,3},{1,0},{2,1},{3,2},{4,7},{5,4},{6,5},{7,6},{8,11},{9,8},{10,9... | collective-permute-start | bytes 2162696 | tf_op jit(solution)/shard_map/ppermute | solution.py:40
  25.6 19.5 %collective-permute-start.12 = (bf16[11,64,512]{2,1,0:T(8,128)(2,1)S(1)}, bf16[11,64,512]{2,1,0:T(8,128)(2,1)S(1)}, u32[]{:S(2)}, u32[]{:S(2)}) collective-permute-start(bf16[11,64,512]{2,1,0:T(8,128)(2,1)S(1)} %collective-permute-done.6.edge1), channel_id=1, source_target_pairs={{0,1},{1,2},{2,3},{3,0},{4,5},{5,6},{6,7},{7,4},{8,9},{9,10},{10,1... | collective-permute-start | bytes 2162696 | tf_op jit(solution)/shard_map/ppermute | solution.py:40
  27.2 7.3 %collective-permute-start.8 = (bf16[2,64,128]{2,1,0:T(8,128)(2,1)S(1)}, bf16[2,64,128]{2,1,0:T(8,128)(2,1)S(1)}, u32[]{:S(2)}, u32[]{:S(2)}) collective-permute-start(bf16[2,64,128]{2,1,0:T(8,128)(2,1)S(1)} %bitcast.8), channel_id=1, source_target_pairs={{0,32},{4,36},{8,40},{12,44},{16,48},{20,52},{24,56},{28,60},{32,6... | collective-permute-start | bytes 98312 | tf_op jit(solution)/shard_map/ppermute | solution.py:36
  28.9 5.6 %collective-permute-start.9 = (bf16[2,64,128]{2,1,0:T(8,128)(2,1)S(1)}, bf16[2,64,128]{2,1,0:T(8,128)(2,1)S(1)}, u32[]{:S(2)}, u32[]{:S(2)}) collective-permute-start(bf16[2,64,128]{2,1,0:T(8,128)(2,1)S(1)} %bitcast.9), channel_id=1, source_target_pairs={{0,224},{4,228},{8,232},{12,236},{16,240},{20,244},{24,248},{28,25... | collective-permute-start | bytes 98312 | tf_op jit(solution)/shard_map/ppermute | solution.py:36
  34.5 9.6 %collective-permute-start.10 = (bf16[6,64,128]{2,1,0:T(8,128)(2,1)S(1)}, bf16[6,64,128]{2,1,0:T(8,128)(2,1)S(1)}, u32[]{:S(2)}, u32[]{:S(2)}) collective-permute-start(bf16[6,64,128]{2,1,0:T(8,128)(2,1)S(1)} %constant_dynamic-update-slice_fusion.refs_1_), channel_id=1, source_target_pairs={{0,96},{4,100},{8,104},{12,108},{16,112},{20,116},{24,120},{28,124... | collective-permute-start | bytes 294920 | tf_op jit(solution)/shard_map/ppermute | solution.py:36
  38.8 5.3 %collective-permute-start.11 = (bf16[4,64,128]{2,1,0:T(8,128)(2,1)S(1)}, bf16[4,64,128]{2,1,0:T(8,128)(2,1)S(1)}, u32[]{:S(2)}, u32[]{:S(2)}) collective-permute-start(bf16[4,64,128]{2,1,0:T(8,128)(2,1)S(1)} %pad_maximum_fusion), channel_id=1, source_target_pairs={{0,160},{4,164},{8,168},{12,172},{16,176},{20,180},{24,184},{28,18... | collective-permute-start | bytes 196616 | tf_op jit(solution)/shard_map/ppermute | solution.py:36
  45.1 6.5 %collective-permute-start.13 = (bf16[16,64,128]{2,1,0:T(8,128)(2,1)S(1)}, bf16[16,64,128]{2,1,0:T(8,128)(2,1)S(1)}, u32[]{:S(2)}, u32[]{:S(2)}) collective-permute-start(bf16[16,64,128]{2,1,0:T(8,128)(2,1)S(1)} %shard_map.147.refs_0_), channel_id=1, source_target_pairs={{0,8},{4,12},{8,16},{12,20},{16,24},{20,28},{24,0},{28,4},{32,40},... | collective-permute-start | bytes 786440 | tf_op jit(solution)/shard_map/ppermute | solution.py:36
  53.6 34.0 %collective-permute-start.16 = (bf16[24,64,512]{2,1,0:T(8,128)(2,1)S(1)}, bf16[24,64,512]{2,1,0:T(8,128)(2,1)S(1)}, u32[]{:S(2)}, u32[]{:S(2)}) collective-permute-start(bf16[24,64,512]{2,1,0:T(8,128)(2,1)S(1)} %get-tuple-element.36), channel_id=1, source_target_pairs={{0,4},{4,0},{8,12},{12,8},{16,20},{20,16},{24,28},{28,24},{32,36},... | collective-permute-start | bytes 4718600 | tf_op jit(solution)/shard_map/ppermute | solution.py:36
  59.8 27.8 %collective-permute-start.17 = (bf16[24,64,512]{2,1,0:T(8,128)(2,1)S(1)}, bf16[24,64,512]{2,1,0:T(8,128)(2,1)S(1)}, u32[]{:S(2)}, u32[]{:S(2)}) collective-permute-start(bf16[24,64,512]{2,1,0:T(8,128)(2,1)S(1)} %get-tuple-element.37), channel_id=1, source_target_pairs={{0,252},{4,8},{8,4},{12,16},{16,12},{20,24},{24,20},{28,32},{32,28... | collective-permute-start | bytes 4718600 | tf_op jit(solution)/shard_map/ppermute | solution.py:255
  61.1 15.9 %collective-permute-start.3 = (bf16[11,64,512]{2,1,0:T(8,128)(2,1)S(1)}, bf16[11,64,512]{2,1,0:T(8,128)(2,1)S(1)}, u32[]{:S(2)}, u32[]{:S(2)}) collective-permute-start(bf16[11,64,512]{2,1,0:T(8,128)(2,1)S(1)} %copy-done), channel_id=1, source_target_pairs={{0,1},{1,2},{2,3},{3,0},{4,5},{5,6},{6,7},{7,4},{8,9},{9,10},{10,1... | collective-permute-start | bytes 2162696 | tf_op jit(solution)/shard_map/ppermute | solution.py:40
  62.0 20.4 %collective-permute-start.5 = (bf16[11,64,512]{2,1,0:T(8,128)(2,1)S(1)}, bf16[11,64,512]{2,1,0:T(8,128)(2,1)S(1)}, u32[]{:S(2)}, u32[]{:S(2)}) collective-permute-start(bf16[11,64,512]{2,1,0:T(8,128)(2,1)S(1)} %collective-permute-done.4.inner2.down), channel_id=1, source_target_pairs={{0,3},{1,0},{2,1},{3,2},{4,7},{5,4},{6,5},{7,6},{8,11},{9,8},{10,9... | collective-permute-start | bytes 2162696 | tf_op jit(solution)/shard_map/ppermute | solution.py:40
  64.0 23.3 %collective-permute-start.15 = (bf16[8,64,128]{2,1,0:T(8,128)(2,1)S(1)}, bf16[8,64,128]{2,1,0:T(8,128)(2,1)S(1)}, u32[]{:S(2)}, u32[]{:S(2)}) collective-permute-start(bf16[8,64,128]{2,1,0:T(8,128)(2,1)S(1)} %slice.33), channel_id=1, source_target_pairs={{0,8},{4,12},{8,16},{12,20},{16,24},{20,28},{24,0},{28,4},{32,40},... | collective-permute-start | bytes 393224 | tf_op jit(solution)/shard_map/ppermute | solution.py:36
  77.0 10.6 %collective-permute-start.18 = (bf16[8,64,128]{2,1,0:T(8,128)(2,1)S(1)}, bf16[8,64,128]{2,1,0:T(8,128)(2,1)S(1)}, u32[]{:S(2)}, u32[]{:S(2)}) collective-permute-start(bf16[8,64,128]{2,1,0:T(8,128)(2,1)S(1)} %slice.34), channel_id=1, source_target_pairs={{0,24},{4,28},{8,0},{12,4},{16,8},{20,12},{24,16},{28,20},{32,56},... | collective-permute-start | bytes 393224 | tf_op jit(solution)/shard_map/ppermute | solution.py:36
  87.0 21.1 %collective-permute-start.20 = (bf16[17,64,512]{2,1,0:T(8,128)(2,1)S(1)}, bf16[17,64,512]{2,1,0:T(8,128)(2,1)S(1)}, u32[]{:S(2)}, u32[]{:S(2)}) collective-permute-start(bf16[17,64,512]{2,1,0:T(8,128)(2,1)S(1)} %get-tuple-element.42), channel_id=1, source_target_pairs={{0,4},{4,8},{8,12},{12,16},{16,20},{20,24},{24,28},{28,32},{32,36}... | collective-permute-start | bytes 3342344 | tf_op jit(solution)/shard_map/ppermute | solution.py:36
  87.3 20.8 %collective-permute-start.21 = (bf16[17,64,512]{2,1,0:T(8,128)(2,1)S(1)}, bf16[17,64,512]{2,1,0:T(8,128)(2,1)S(1)}, u32[]{:S(2)}, u32[]{:S(2)}) collective-permute-start(bf16[17,64,512]{2,1,0:T(8,128)(2,1)S(1)} %get-tuple-element.43), channel_id=1, source_target_pairs={{0,252},{4,0},{8,4},{12,8},{16,12},{20,16},{24,20},{28,24},{32,28}... | collective-permute-start | bytes 3342344 | tf_op jit(solution)/shard_map/ppermute | solution.py:36
  88.7 6.4 %collective-permute-start.19 = (bf16[64,64,128]{2,1,0:T(8,128)(2,1)S(1)}, bf16[64,64,128]{2,1,0:T(8,128)(2,1)S(1)}, u32[]{:S(2)}, u32[]{:S(2)}) collective-permute-start(bf16[64,64,128]{2,1,0:T(8,128)(2,1)S(1)} %shard_map.150.mine), channel_id=1, source_target_pairs={{0,4},{4,0},{8,12},{12,8},{16,20},{20,16},{24,28},{28,24},{32,36},... | collective-permute-start | bytes 3145736 | tf_op jit(solution)/shard_map/ppermute | solution.py:36
  97.3 10.7 %collective-permute-start.22 = (bf16[2,64,128]{2,1,0:T(8,128)(2,1)S(1)}, bf16[2,64,128]{2,1,0:T(8,128)(2,1)S(1)}, u32[]{:S(2)}, u32[]{:S(2)}) collective-permute-start(bf16[2,64,128]{2,1,0:T(8,128)(2,1)S(1)} %get-tuple-element.44.own_t), channel_id=1, source_target_pairs={{0,1},{1,2},{2,3},{3,0},{4,5},{5,6},{6,7},{7,4},{8,9},{9,10},{10,1... | collective-permute-start | bytes 98312 | tf_op jit(solution)/shard_map/ppermute | solution.py:40
  97.4 10.6 %collective-permute-start.23 = (bf16[2,64,128]{2,1,0:T(8,128)(2,1)S(1)}, bf16[2,64,128]{2,1,0:T(8,128)(2,1)S(1)}, u32[]{:S(2)}, u32[]{:S(2)}) collective-permute-start(bf16[2,64,128]{2,1,0:T(8,128)(2,1)S(1)} %get-tuple-element.44.own_t), channel_id=1, source_target_pairs={{0,3},{1,0},{2,1},{3,2},{4,7},{5,4},{6,5},{7,6},{8,11},{9,8},{10,9... | collective-permute-start | bytes 98312 | tf_op jit(solution)/shard_map/ppermute | solution.py:40
  100.1 8.0 %collective-permute-start.24 = (bf16[2,64,128]{2,1,0:T(8,128)(2,1)S(1)}, bf16[2,64,128]{2,1,0:T(8,128)(2,1)S(1)}, u32[]{:S(2)}, u32[]{:S(2)}) collective-permute-start(bf16[2,64,128]{2,1,0:T(8,128)(2,1)S(1)} %get-tuple-element.44.own_t), channel_id=1, source_target_pairs={{0,2},{1,3},{2,0},{3,1},{4,6},{5,7},{6,4},{7,5},{8,10},{9,11},{10,... | collective-permute-start | bytes 98312 | tf_op jit(solution)/shard_map/ppermute | solution.py:40
  (11 other events, 273.2 us)

commit v2 on v1

--- a/solution.py
+++ b/solution.py
@@ -454,12 +454,13 @@
     to_core, to_chip = kernel_call(
         ends_kernel,
         (),
-        (edge0, edge1, edge2, after(edge3, left, right)),
+        (edge0, edge1, edge2, after(edge3, column)),
         (shape((24, 64, 512)),) * 2,
         scratch=[v((24, 64, 512), BF)] * 2,
     )
-    core_ends, chip_ends = core_swap(to_core), chip_swap(to_chip)
+    chip_ends = chip_swap(to_chip)
     across_a, across_b = over_leaf(left[0:8], dx=1), over_leaf(right[8:16], dx=-1)
+    core_ends = core_swap(after(to_core, across_a, across_b))
 
     pairs = (edge0, inner0, edge1, inner1, edge2, inner2, edge3, inner3)
     fine_m, middle_m, coarse_m, to_right, to_left = kernel_call(
@@ -475,7 +476,7 @@
     )
     low_m, high_m = over_leaf(to_right, step=1), over_leaf(to_left, step=-1)
 
-    plane = joined(column, left, right, after(across_a, fine_m, core_ends, chip_ends), across_b)
+    plane = joined(column, left, right, after(across_a, fine_m), across_b)
     partner = core_swap(plane)
     inners = (inner0, inner1, inner2, inner3)
     term_top, columns = kernel_call(

time: 116 us -> 106 us (0.914)
  the two profiles are of different devices: /device:TPU:1 before, /device:TPU:24 now
where the time goes in v2:
time: 106 us; the launch traced here: 105 us
  starting transfers between devices  39.5 us (37%)
  Pallas kernels  32.9 us (31%)
  waiting for transfers between devices  31.6 us (30%)
    pallas_call x9, Pallas kernels, kernel_call(): pl.pallas_call(kernel, out_shape=outs, in_specs=[SMEM] * len(scalars) + [...  32.9 us
    ppermute x12, starting transfers between devices, over_leaf(): return lax.ppermute(array, 'leaf', leaf_pairs(**move))  23.1 us
    ppermute x12, waiting for transfers between devices, over_leaf(): return lax.ppermute(array, 'leaf', leaf_pairs(**move))  19.1 us
    ppermute x12, starting transfers between devices, over_lvl(): return lax.ppermute(array, 'lvl', [(i, (i + step) % LV) for i in range(LV)])  16.2 us
    ppermute x12, waiting for transfers between devices, over_lvl(): return lax.ppermute(array, 'lvl', [(i, (i + step) % LV) for i in range(LV)])  9.99 us
    ppermute x1, waiting for transfers between devices, chip_swap(): lax.ppermute(array, 'leaf', [(i, (i + (1 if i % CS else -1)) % leaves) fo...  2.48 us
  transfers between devices with their start and end apart: 25, of which 10 were waited for; matrix products, arithmetic and copies ran while one was open for 1% of the time, Pallas kernels for 21%

profile of v2, /device:TPU:24, one launch (start us, length us, event | category | flops | bytes accessed | tf_op | source)
XLA Modules:
  0.0 105.3 jit_solution(1497086760147299689)
XLA Ops:
  0.0 3.0 %shard_map.145 = (bf16[11,64,512]{2,1,0:T(8,128)(2,1)}, bf16[11,64,512]{2,1,0:T(8,128)(2,1)}) custom-call(bf16[16,64,512]{2,1,0:T(8,128)(2,1)} %charges.1, bf16[16,64,64]{2,1,0:T(8,128)(2,1)} %basis.3, f32[16,1,64,64]{3,2,1,0:T(8,128)} %fine_c.1, f32[8,1,64,64]{3,2,1,0:T(8,128)} %middle_c.1, f32[4,1,64,64]{3,2,1,0:T(8,128)} %coarse_c.1, f32[2,2,64,64]{3,2,1,0:T(8,128)} %top_c.1), custom_call_target="tpu_custom_call" | custom-call | flops 1000000 | bytes 100000 | tf_op jit(solution)/shard_map/pallas_call | solution.py:53
  3.1 2.0 %collective-permute-start.6 = (bf16[11,64,512]{2,1,0:T(8,128)(2,1)}, bf16[11,64,512]{2,1,0:T(8,128)(2,1)S(1)}, u32[]{:S(2)}, u32[]{:S(2)}) collective-permute-start(bf16[11,64,512]{2,1,0:T(8,128)(2,1)} %get-tuple-element.26.edge.edge0), channel_id=1, source_target_pairs={{0,1},{1,2},{2,3},{3,0},{4,5},{5,6},{6,7},{7,4},{8,9},{9,10},{10,1... | collective-permute-start | bytes 2162696 | tf_op jit(solution)/shard_map/ppermute | solution.py:40
  5.2 4.2 %shard_map.146 = (bf16[144,128]{1,0:T(8,128)(2,1)}, bf16[144,128]{1,0:T(8,128)(2,1)}, bf16[144,128]{1,0:T(8,128)(2,1)}, bf16[144,128]{1,0:T(8,128)(2,1)}) custom-call(s32[16]{0:T(128)} %bitcast.12, s32[8]{0:T(128)} %bitcast.13, s32[4]{0:T(128)} %bitcast.14, s32[2,2]{1,0:T(2,128)} %top_cols.1, bf16[11,64,512]{2,1,0:T(8,128)(2,1)} %get-tuple-element.26.edge.edge0, ...), custom_call_target="tpu_custom_call" | custom-call | flops 1000000 | bytes 100000 | tf_op jit(solution)/shard_map/pallas_call | solution.py:53
  9.3 3.2 %collective-permute-start = (bf16[144,128]{1,0:T(8,128)(2,1)}, bf16[144,128]{1,0:T(8,128)(2,1)S(1)}, u32[]{:S(2)}, u32[]{:S(2)}) collective-permute-start(bf16[144,128]{1,0:T(8,128)(2,1)} %get-tuple-element.29), channel_id=1, source_target_pairs={{0,1},{1,2},{2,3},{3,0},{4,5},{5,6},{6,7},{7,4},{8,9},{9,10},{10,1... | collective-permute-start | bytes 110600 | tf_op jit(solution)/shard_map/ppermute | solution.py:40
  14.1 8.3 %collective-permute-done.part1 = bf16[144,128]{1,0:T(8,128)(2,1)S(1)} collective-permute-done((bf16[144,128]{1,0:T(8,128)(2,1)}, bf16[144,128]{1,0:T(8,128)(2,1)S(1)}, u32[]{:S(2)}, u32[]{:S(2)}) %collective-permute-start) | collective-permute-done | bytes 36896 | tf_op jit(solution)/shard_map/ppermute | solution.py:40
  24.2 3.2 %collective-permute-start.12 = (bf16[11,64,512]{2,1,0:T(8,128)(2,1)S(1)}, bf16[11,64,512]{2,1,0:T(8,128)(2,1)S(1)}, u32[]{:S(2)}, u32[]{:S(2)}) collective-permute-start(bf16[11,64,512]{2,1,0:T(8,128)(2,1)S(1)} %collective-permute-done.6.edge1), channel_id=1, source_target_pairs={{0,1},{1,2},{2,3},{3,0},{4,5},{5,6},{6,7},{7,4},{8,9},{9,10},{10,1... | collective-permute-start | bytes 2162696 | tf_op jit(solution)/shard_map/ppermute | solution.py:40
  28.2 2.0 %collective-permute-start.8 = (bf16[2,64,128]{2,1,0:T(8,128)(2,1)S(1)}, bf16[2,64,128]{2,1,0:T(8,128)(2,1)S(1)}, u32[]{:S(2)}, u32[]{:S(2)}) collective-permute-start(bf16[2,64,128]{2,1,0:T(8,128)(2,1)S(1)} %bitcast.8), channel_id=1, source_target_pairs={{0,32},{4,36},{8,40},{12,44},{16,48},{20,52},{24,56},{28,60},{32,6... | collective-permute-start | bytes 98312 | tf_op jit(solution)/shard_map/ppermute | solution.py:36
  30.1 4.0 %collective-permute-start.9 = (bf16[2,64,128]{2,1,0:T(8,128)(2,1)S(1)}, bf16[2,64,128]{2,1,0:T(8,128)(2,1)S(1)}, u32[]{:S(2)}, u32[]{:S(2)}) collective-permute-start(bf16[2,64,128]{2,1,0:T(8,128)(2,1)S(1)} %bitcast.9), channel_id=1, source_target_pairs={{0,224},{4,228},{8,232},{12,236},{16,240},{20,244},{24,248},{28,25... | collective-permute-start | bytes 98312 | tf_op jit(solution)/shard_map/ppermute | solution.py:36
  36.0 5.1 %collective-permute-start.10 = (bf16[6,64,128]{2,1,0:T(8,128)(2,1)S(1)}, bf16[6,64,128]{2,1,0:T(8,128)(2,1)S(1)}, u32[]{:S(2)}, u32[]{:S(2)}) collective-permute-start(bf16[6,64,128]{2,1,0:T(8,128)(2,1)S(1)} %constant_dynamic-update-slice_fusion.refs_1_), channel_id=1, source_target_pairs={{0,96},{4,100},{8,104},{12,108},{16,112},{20,116},{24,120},{28,124... | collective-permute-start | bytes 294920 | tf_op jit(solution)/shard_map/ppermute | solution.py:36
  41.2 6.0 %collective-permute-done.11.refs_2_ = bf16[4,64,128]{2,1,0:T(8,128)(2,1)S(1)} collective-permute-done((bf16[4,64,128]{2,1,0:T(8,128)(2,1)S(1)}, bf16[4,64,128]{2,1,0:T(8,128)(2,1)S(1)}, u32[]{:S(2)}, u32[]{:S(2)}) %collective-permute-start.11) | collective-permute-done | bytes 65568 | tf_op jit(solution)/shard_map/ppermute | solution.py:36
  48.3 2.8 %collective-permute-start.14 = (bf16[16,64,128]{2,1,0:T(8,128)(2,1)S(1)}, bf16[16,64,128]{2,1,0:T(8,128)(2,1)S(1)}, u32[]{:S(2)}, u32[]{:S(2)}) collective-permute-start(bf16[16,64,128]{2,1,0:T(8,128)(2,1)S(1)} %shard_map.147.refs_0_), channel_id=1, source_target_pairs={{0,24},{4,28},{8,0},{12,4},{16,8},{20,12},{24,16},{28,20},{32,56},... | collective-permute-start | bytes 786440 | tf_op jit(solution)/shard_map/ppermute | solution.py:36
  51.3 1.9 %collective-permute-start.5 = (bf16[11,64,512]{2,1,0:T(8,128)(2,1)S(1)}, bf16[11,64,512]{2,1,0:T(8,128)(2,1)S(1)}, u32[]{:S(2)}, u32[]{:S(2)}) collective-permute-start(bf16[11,64,512]{2,1,0:T(8,128)(2,1)S(1)} %collective-permute-done.4.inner2.down), channel_id=1, source_target_pairs={{0,3},{1,0},{2,1},{3,2},{4,7},{5,4},{6,5},{7,6},{8,11},{9,8},{10,9... | collective-permute-start | bytes 2162696 | tf_op jit(solution)/shard_map/ppermute | solution.py:40
  53.1 3.3 %collective-permute-done.14.refs_2_ = bf16[16,64,128]{2,1,0:T(8,128)(2,1)S(1)} collective-permute-done((bf16[16,64,128]{2,1,0:T(8,128)(2,1)S(1)}, bf16[16,64,128]{2,1,0:T(8,128)(2,1)S(1)}, u32[]{:S(2)}, u32[]{:S(2)}) %collective-permute-start.14) | collective-permute-done | bytes 262176 | tf_op jit(solution)/shard_map/ppermute | solution.py:36
  56.4 3.8 %collective-permute-start.16 = (bf16[8,64,128]{2,1,0:T(8,128)(2,1)S(1)}, bf16[8,64,128]{2,1,0:T(8,128)(2,1)S(1)}, u32[]{:S(2)}, u32[]{:S(2)}) collective-permute-start(bf16[8,64,128]{2,1,0:T(8,128)(2,1)S(1)} %slice.34), channel_id=1, source_target_pairs={{0,24},{4,28},{8,0},{12,4},{16,8},{20,12},{24,16},{28,20},{32,56},... | collective-permute-start | bytes 393224 | tf_op jit(solution)/shard_map/ppermute | solution.py:36
  60.3 2.0 %shard_map.151 = (bf16[24,64,512]{2,1,0:T(8,128)(2,1)S(1)}, bf16[24,64,512]{2,1,0:T(8,128)(2,1)S(1)}) custom-call(bf16[11,64,512]{2,1,0:T(8,128)(2,1)S(1)} %copy-done.1, bf16[11,64,512]{2,1,0:T(8,128)(2,1)S(1)} %collective-permute-done.6.edge1, bf16[11,64,512]{2,1,0:T(8,128)(2,1)S(1)} %collective-permute-done.7.edge2, ...), custom_call_target="tpu_custom_call" | custom-call | flops 1000000 | bytes 100000 | tf_op jit(solution)/shard_map/pallas_call | solution.py:53
  62.7 3.8 %collective-permute-done.15.refs_3_ = bf16[8,64,128]{2,1,0:T(8,128)(2,1)S(1)} collective-permute-done((bf16[8,64,128]{2,1,0:T(8,128)(2,1)S(1)}, bf16[8,64,128]{2,1,0:T(8,128)(2,1)S(1)}, u32[]{:S(2)}, u32[]{:S(2)}) %collective-permute-start.15) | collective-permute-done | bytes 131104 | tf_op jit(solution)/shard_map/ppermute | solution.py:36
  66.5 4.5 %shard_map.148 = (bf16[16,64,512]{2,1,0:T(8,128)(2,1)S(1)}, bf16[8,64,512]{2,1,0:T(8,128)(2,1)S(1)}, bf16[4,64,512]{2,1,0:T(8,128)(2,1)S(1)}, bf16[17,64,512]{2,1,0:T(8,128)(2,1)S(1)}, bf16[17,64,512]{2,1,0:T(8,128)(2,1)S(1)}) custom-call(bf16[11,64,512]{2,1,0:T(8,128)(2,1)S(1)} %copy-done.1, bf16[11,64,512]{2,1,0:T(8,128)(2,1)S(1)} %copy-done, ...), custom_call_target="tpu_custom_call" | custom-call | flops 1000000 | bytes 100000 | tf_op jit(solution)/shard_map/pallas_call | solution.py:53
  71.6 4.6 %collective-permute-start.19 = (bf16[17,64,512]{2,1,0:T(8,128)(2,1)S(1)}, bf16[17,64,512]{2,1,0:T(8,128)(2,1)S(1)}, u32[]{:S(2)}, u32[]{:S(2)}) collective-permute-start(bf16[17,64,512]{2,1,0:T(8,128)(2,1)S(1)} %get-tuple-element.41), channel_id=1, source_target_pairs={{0,252},{4,0},{8,4},{12,8},{16,12},{20,16},{24,20},{28,24},{32,28}... | collective-permute-start | bytes 3342344 | tf_op jit(solution)/shard_map/ppermute | solution.py:36
  77.4 2.6 %collective-permute-done.17.partner = bf16[64,64,128]{2,1,0:T(8,128)(2,1)S(1)} collective-permute-done((bf16[64,64,128]{2,1,0:T(8,128)(2,1)S(1)}, bf16[64,64,128]{2,1,0:T(8,128)(2,1)S(1)}, u32[]{:S(2)}, u32[]{:S(2)}) %collective-permute-start.17) | collective-permute-done | bytes 1048608 | tf_op jit(solution)/shard_map/ppermute | solution.py:36
  80.0 2.3 %shard_map.150 = (bf16[2,64,128]{2,1,0:T(8,128)(2,1)S(1)}, s32[4,8,128]{2,1,0:T(8,128)S(1)}) custom-call(bf16[144,128]{1,0:T(8,128)(2,1)S(1)} %copy-done.6, bf16[144,128]{1,0:T(8,128)(2,1)S(1)} %collective-permute-done.part1, bf16[144,128]{1,0:T(8,128)(2,1)S(1)} %collective-permute-done.1.part2, bf16[144,128]{1,0:T(8,128)(2,1)S(1)} %collective-permute-done.2.part3, ...), custom_call_target="tpu_custom_call" | custom-call | flops 1000000 | bytes 100000 | tf_op jit(solution)/shard_map/pallas_call | solution.py:53
  83.1 2.5 %collective-permute-done.24.chip_ends = bf16[24,64,512]{2,1,0:T(8,128)(2,1)S(1)} collective-permute-done((bf16[24,64,512]{2,1,0:T(8,128)(2,1)S(1)}, bf16[24,64,512]{2,1,0:T(8,128)(2,1)S(1)}, u32[]{:S(2)}, u32[]{:S(2)}) %collective-permute-start.24) | collective-permute-done | bytes 1572896 | tf_op jit(solution)/shard_map/ppermute | solution.py:255
  85.6 3.2 %collective-permute-start.20 = (bf16[2,64,128]{2,1,0:T(8,128)(2,1)S(1)}, bf16[2,64,128]{2,1,0:T(8,128)(2,1)S(1)}, u32[]{:S(2)}, u32[]{:S(2)}) collective-permute-start(bf16[2,64,128]{2,1,0:T(8,128)(2,1)S(1)} %get-tuple-element.42.own_t), channel_id=1, source_target_pairs={{0,1},{1,2},{2,3},{3,0},{4,5},{5,6},{6,7},{7,4},{8,9},{9,10},{10,1... | collective-permute-start | bytes 98312 | tf_op jit(solution)/shard_map/ppermute | solution.py:40
  88.9 7.3 %shard_map.152.near = f32[16,64,512]{2,1,0:T(8,128)S(1)} custom-call(s32[16,12]{1,0:T(8,128)S(1)} %copy-done.7, bf16[11,64,512]{2,1,0:T(8,128)(2,1)S(1)} %copy-done.1, bf16[11,64,512]{2,1,0:T(8,128)(2,1)S(1)} %copy-done, bf16[11,64,512]{2,1,0:T(8,128)(2,1)S(1)} %collective-permute-done.6.edge1, bf16[11,64,512]{2,1,0:T(8,128)(2,1)S(1)} %collective-permute-done.3.inner1.up, ...), custom_call_target="tpu_custom_call" | custom-call | flops 1000000 | bytes 100000 | tf_op jit(solution)/shard_map/pallas_call | solution.py:53
  97.6 7.5 %shard_map.153 = bf16[16,64,512]{2,1,0:T(8,128)(2,1)} custom-call(s32[4,32]{1,0:T(4,128)S(1)} %bitcast.7, bf16[16,64,512]{2,1,0:T(8,128)(2,1)S(1)} %get-tuple-element.35.fine_m, bf16[8,64,512]{2,1,0:T(8,128)(2,1)S(1)} %get-tuple-element.38.middle_m, bf16[4,64,512]{2,1,0:T(8,128)(2,1)S(1)} %get-tuple-element.39.coarse_m, ...), custom_call_target="tpu_custom_call" | custom-call | flops 1000000 | bytes 100000 | tf_op jit(solution)/shard_map/pallas_call | solution.py:53
  (64 shorter events, 11.6 us)
Async XLA Ops:
  3.1 21.1 %collective-permute-start.6 = (bf16[11,64,512]{2,1,0:T(8,128)(2,1)}, bf16[11,64,512]{2,1,0:T(8,128)(2,1)S(1)}, u32[]{:S(2)}, u32[]{:S(2)}) collective-permute-start(bf16[11,64,512]{2,1,0:T(8,128)(2,1)} %get-tuple-element.26.edge.edge0), channel_id=1, source_target_pairs={{0,1},{1,2},{2,3},{3,0},{4,5},{5,6},{6,7},{7,4},{8,9},{9,10},{10,1... | collective-permute-start | bytes 2162696 | tf_op jit(solution)/shard_map/ppermute | solution.py:40
  5.1 23.0 %collective-permute-start.7 = (bf16[11,64,512]{2,1,0:T(8,128)(2,1)}, bf16[11,64,512]{2,1,0:T(8,128)(2,1)S(1)}, u32[]{:S(2)}, u32[]{:S(2)}) collective-permute-start(bf16[11,64,512]{2,1,0:T(8,128)(2,1)} %get-tuple-element.26.edge.edge0), channel_id=1, source_target_pairs={{0,3},{1,0},{2,1},{3,2},{4,7},{5,4},{6,5},{7,6},{8,11},{9,8},{10,9... | collective-permute-start | bytes 2162696 | tf_op jit(solution)/shard_map/ppermute | solution.py:40
  9.3 13.1 %collective-permute-start = (bf16[144,128]{1,0:T(8,128)(2,1)}, bf16[144,128]{1,0:T(8,128)(2,1)S(1)}, u32[]{:S(2)}, u32[]{:S(2)}) collective-permute-start(bf16[144,128]{1,0:T(8,128)(2,1)} %get-tuple-element.29), channel_id=1, source_target_pairs={{0,1},{1,2},{2,3},{3,0},{4,5},{5,6},{6,7},{7,4},{8,9},{9,10},{10,1... | collective-permute-start | bytes 110600 | tf_op jit(solution)/shard_map/ppermute | solution.py:40
  12.6 11.5 %collective-permute-start.1 = (bf16[144,128]{1,0:T(8,128)(2,1)}, bf16[144,128]{1,0:T(8,128)(2,1)S(1)}, u32[]{:S(2)}, u32[]{:S(2)}) collective-permute-start(bf16[144,128]{1,0:T(8,128)(2,1)} %get-tuple-element.30), channel_id=1, source_target_pairs={{0,3},{1,0},{2,1},{3,2},{4,7},{5,4},{6,5},{7,6},{8,11},{9,8},{10,9... | collective-permute-start | bytes 110600 | tf_op jit(solution)/shard_map/ppermute | solution.py:40
  12.6 11.5 %collective-permute-start.2 = (bf16[144,128]{1,0:T(8,128)(2,1)}, bf16[144,128]{1,0:T(8,128)(2,1)S(1)}, u32[]{:S(2)}, u32[]{:S(2)}) collective-permute-start(bf16[144,128]{1,0:T(8,128)(2,1)} %get-tuple-element.31), channel_id=1, source_target_pairs={{0,2},{1,3},{2,0},{3,1},{4,6},{5,7},{6,4},{7,5},{8,10},{9,11},{10,... | collective-permute-start | bytes 110600 | tf_op jit(solution)/shard_map/ppermute | solution.py:40
  24.1 24.1 %collective-permute-start.4 = (bf16[11,64,512]{2,1,0:T(8,128)(2,1)S(1)}, bf16[11,64,512]{2,1,0:T(8,128)(2,1)S(1)}, u32[]{:S(2)}, u32[]{:S(2)}) collective-permute-start(bf16[11,64,512]{2,1,0:T(8,128)(2,1)S(1)} %copy-done), channel_id=1, source_target_pairs={{0,3},{1,0},{2,1},{3,2},{4,7},{5,4},{6,5},{7,6},{8,11},{9,8},{10,9... | collective-permute-start | bytes 2162696 | tf_op jit(solution)/shard_map/ppermute | solution.py:40
  24.2 24.1 %collective-permute-start.12 = (bf16[11,64,512]{2,1,0:T(8,128)(2,1)S(1)}, bf16[11,64,512]{2,1,0:T(8,128)(2,1)S(1)}, u32[]{:S(2)}, u32[]{:S(2)}) collective-permute-start(bf16[11,64,512]{2,1,0:T(8,128)(2,1)S(1)} %collective-permute-done.6.edge1), channel_id=1, source_target_pairs={{0,1},{1,2},{2,3},{3,0},{4,5},{5,6},{6,7},{7,4},{8,9},{9,10},{10,1... | collective-permute-start | bytes 2162696 | tf_op jit(solution)/shard_map/ppermute | solution.py:40
  28.2 7.8 %collective-permute-start.8 = (bf16[2,64,128]{2,1,0:T(8,128)(2,1)S(1)}, bf16[2,64,128]{2,1,0:T(8,128)(2,1)S(1)}, u32[]{:S(2)}, u32[]{:S(2)}) collective-permute-start(bf16[2,64,128]{2,1,0:T(8,128)(2,1)S(1)} %bitcast.8), channel_id=1, source_target_pairs={{0,32},{4,36},{8,40},{12,44},{16,48},{20,52},{24,56},{28,60},{32,6... | collective-permute-start | bytes 98312 | tf_op jit(solution)/shard_map/ppermute | solution.py:36
  30.1 5.8 %collective-permute-start.9 = (bf16[2,64,128]{2,1,0:T(8,128)(2,1)S(1)}, bf16[2,64,128]{2,1,0:T(8,128)(2,1)S(1)}, u32[]{:S(2)}, u32[]{:S(2)}) collective-permute-start(bf16[2,64,128]{2,1,0:T(8,128)(2,1)S(1)} %bitcast.9), channel_id=1, source_target_pairs={{0,224},{4,228},{8,232},{12,236},{16,240},{20,244},{24,248},{28,25... | collective-permute-start | bytes 98312 | tf_op jit(solution)/shard_map/ppermute | solution.py:36
  36.0 11.3 %collective-permute-start.10 = (bf16[6,64,128]{2,1,0:T(8,128)(2,1)S(1)}, bf16[6,64,128]{2,1,0:T(8,128)(2,1)S(1)}, u32[]{:S(2)}, u32[]{:S(2)}) collective-permute-start(bf16[6,64,128]{2,1,0:T(8,128)(2,1)S(1)} %constant_dynamic-update-slice_fusion.refs_1_), channel_id=1, source_target_pairs={{0,96},{4,100},{8,104},{12,108},{16,112},{20,116},{24,120},{28,124... | collective-permute-start | bytes 294920 | tf_op jit(solution)/shard_map/ppermute | solution.py:36
  41.1 6.1 %collective-permute-start.11 = (bf16[4,64,128]{2,1,0:T(8,128)(2,1)S(1)}, bf16[4,64,128]{2,1,0:T(8,128)(2,1)S(1)}, u32[]{:S(2)}, u32[]{:S(2)}) collective-permute-start(bf16[4,64,128]{2,1,0:T(8,128)(2,1)S(1)} %pad_maximum_fusion), channel_id=1, source_target_pairs={{0,160},{4,164},{8,168},{12,172},{16,176},{20,180},{24,184},{28,18... | collective-permute-start | bytes 196616 | tf_op jit(solution)/shard_map/ppermute | solution.py:36
  48.3 8.1 %collective-permute-start.14 = (bf16[16,64,128]{2,1,0:T(8,128)(2,1)S(1)}, bf16[16,64,128]{2,1,0:T(8,128)(2,1)S(1)}, u32[]{:S(2)}, u32[]{:S(2)}) collective-permute-start(bf16[16,64,128]{2,1,0:T(8,128)(2,1)S(1)} %shard_map.147.refs_0_), channel_id=1, source_target_pairs={{0,24},{4,28},{8,0},{12,4},{16,8},{20,12},{24,16},{28,20},{32,56},... | collective-permute-start | bytes 786440 | tf_op jit(solution)/shard_map/ppermute | solution.py:36
  51.1 9.1 %collective-permute-start.13 = (bf16[16,64,128]{2,1,0:T(8,128)(2,1)S(1)}, bf16[16,64,128]{2,1,0:T(8,128)(2,1)S(1)}, u32[]{:S(2)}, u32[]{:S(2)}) collective-permute-start(bf16[16,64,128]{2,1,0:T(8,128)(2,1)S(1)} %shard_map.147.refs_0_), channel_id=1, source_target_pairs={{0,8},{4,12},{8,16},{12,20},{16,24},{20,28},{24,0},{28,4},{32,40},... | collective-permute-start | bytes 786440 | tf_op jit(solution)/shard_map/ppermute | solution.py:36
  51.1 15.4 %collective-permute-start.3 = (bf16[11,64,512]{2,1,0:T(8,128)(2,1)S(1)}, bf16[11,64,512]{2,1,0:T(8,128)(2,1)S(1)}, u32[]{:S(2)}, u32[]{:S(2)}) collective-permute-start(bf16[11,64,512]{2,1,0:T(8,128)(2,1)S(1)} %copy-done), channel_id=1, source_target_pairs={{0,1},{1,2},{2,3},{3,0},{4,5},{5,6},{6,7},{7,4},{8,9},{9,10},{10,1... | collective-permute-start | bytes 2162696 | tf_op jit(solution)/shard_map/ppermute | solution.py:40
  51.3 15.2 %collective-permute-start.5 = (bf16[11,64,512]{2,1,0:T(8,128)(2,1)S(1)}, bf16[11,64,512]{2,1,0:T(8,128)(2,1)S(1)}, u32[]{:S(2)}, u32[]{:S(2)}) collective-permute-start(bf16[11,64,512]{2,1,0:T(8,128)(2,1)S(1)} %collective-permute-done.4.inner2.down), channel_id=1, source_target_pairs={{0,3},{1,0},{2,1},{3,2},{4,7},{5,4},{6,5},{7,6},{8,11},{9,8},{10,9... | collective-permute-start | bytes 2162696 | tf_op jit(solution)/shard_map/ppermute | solution.py:40
  56.4 6.3 %collective-permute-start.16 = (bf16[8,64,128]{2,1,0:T(8,128)(2,1)S(1)}, bf16[8,64,128]{2,1,0:T(8,128)(2,1)S(1)}, u32[]{:S(2)}, u32[]{:S(2)}) collective-permute-start(bf16[8,64,128]{2,1,0:T(8,128)(2,1)S(1)} %slice.34), channel_id=1, source_target_pairs={{0,24},{4,28},{8,0},{12,4},{16,8},{20,12},{24,16},{28,20},{32,56},... | collective-permute-start | bytes 393224 | tf_op jit(solution)/shard_map/ppermute | solution.py:36
  60.2 6.3 %collective-permute-start.15 = (bf16[8,64,128]{2,1,0:T(8,128)(2,1)S(1)}, bf16[8,64,128]{2,1,0:T(8,128)(2,1)S(1)}, u32[]{:S(2)}, u32[]{:S(2)}) collective-permute-start(bf16[8,64,128]{2,1,0:T(8,128)(2,1)S(1)} %slice.33), channel_id=1, source_target_pairs={{0,8},{4,12},{8,16},{12,20},{16,24},{20,28},{24,0},{28,4},{32,40},... | collective-permute-start | bytes 393224 | tf_op jit(solution)/shard_map/ppermute | solution.py:36
  62.4 23.2 %collective-permute-start.24 = (bf16[24,64,512]{2,1,0:T(8,128)(2,1)S(1)}, bf16[24,64,512]{2,1,0:T(8,128)(2,1)S(1)}, u32[]{:S(2)}, u32[]{:S(2)}) collective-permute-start(bf16[24,64,512]{2,1,0:T(8,128)(2,1)S(1)} %get-tuple-element.46), channel_id=1, source_target_pairs={{0,252},{4,8},{8,4},{12,16},{16,12},{20,24},{24,20},{28,32},{32,28... | collective-permute-start | bytes 4718600 | tf_op jit(solution)/shard_map/ppermute | solution.py:255
  66.5 19.1 %collective-permute-start.23 = (bf16[24,64,512]{2,1,0:T(8,128)(2,1)S(1)}, bf16[24,64,512]{2,1,0:T(8,128)(2,1)S(1)}, u32[]{:S(2)}, u32[]{:S(2)}) collective-permute-start(bf16[24,64,512]{2,1,0:T(8,128)(2,1)S(1)} %get-tuple-element.45), channel_id=1, source_target_pairs={{0,4},{4,0},{8,12},{12,8},{16,20},{20,16},{24,28},{28,24},{32,36},... | collective-permute-start | bytes 4718600 | tf_op jit(solution)/shard_map/ppermute | solution.py:36
  71.0 26.5 %collective-permute-start.18 = (bf16[17,64,512]{2,1,0:T(8,128)(2,1)S(1)}, bf16[17,64,512]{2,1,0:T(8,128)(2,1)S(1)}, u32[]{:S(2)}, u32[]{:S(2)}) collective-permute-start(bf16[17,64,512]{2,1,0:T(8,128)(2,1)S(1)} %get-tuple-element.40), channel_id=1, source_target_pairs={{0,4},{4,8},{8,12},{12,16},{16,20},{20,24},{24,28},{28,32},{32,36}... | collective-permute-start | bytes 3342344 | tf_op jit(solution)/shard_map/ppermute | solution.py:36
  71.6 25.9 %collective-permute-start.19 = (bf16[17,64,512]{2,1,0:T(8,128)(2,1)S(1)}, bf16[17,64,512]{2,1,0:T(8,128)(2,1)S(1)}, u32[]{:S(2)}, u32[]{:S(2)}) collective-permute-start(bf16[17,64,512]{2,1,0:T(8,128)(2,1)S(1)} %get-tuple-element.41), channel_id=1, source_target_pairs={{0,252},{4,0},{8,4},{12,8},{16,12},{20,16},{24,20},{28,24},{32,28}... | collective-permute-start | bytes 3342344 | tf_op jit(solution)/shard_map/ppermute | solution.py:36
  82.3 15.2 %collective-permute-start.22 = (bf16[2,64,128]{2,1,0:T(8,128)(2,1)S(1)}, bf16[2,64,128]{2,1,0:T(8,128)(2,1)S(1)}, u32[]{:S(2)}, u32[]{:S(2)}) collective-permute-start(bf16[2,64,128]{2,1,0:T(8,128)(2,1)S(1)} %get-tuple-element.42.own_t), channel_id=1, source_target_pairs={{0,2},{1,3},{2,0},{3,1},{4,6},{5,7},{6,4},{7,5},{8,10},{9,11},{10,... | collective-permute-start | bytes 98312 | tf_op jit(solution)/shard_map/ppermute | solution.py:40
  85.6 11.9 %collective-permute-start.21 = (bf16[2,64,128]{2,1,0:T(8,128)(2,1)S(1)}, bf16[2,64,128]{2,1,0:T(8,128)(2,1)S(1)}, u32[]{:S(2)}, u32[]{:S(2)}) collective-permute-start(bf16[2,64,128]{2,1,0:T(8,128)(2,1)S(1)} %get-tuple-element.42.own_t), channel_id=1, source_target_pairs={{0,3},{1,0},{2,1},{3,2},{4,7},{5,4},{6,5},{7,6},{8,11},{9,8},{10,9... | collective-permute-start | bytes 98312 | tf_op jit(solution)/shard_map/ppermute | solution.py:40
  85.6 11.9 %collective-permute-start.20 = (bf16[2,64,128]{2,1,0:T(8,128)(2,1)S(1)}, bf16[2,64,128]{2,1,0:T(8,128)(2,1)S(1)}, u32[]{:S(2)}, u32[]{:S(2)}) collective-permute-start(bf16[2,64,128]{2,1,0:T(8,128)(2,1)S(1)} %get-tuple-element.42.own_t), channel_id=1, source_target_pairs={{0,1},{1,2},{2,3},{3,0},{4,5},{5,6},{6,7},{7,4},{8,9},{9,10},{10,1... | collective-permute-start | bytes 98312 | tf_op jit(solution)/shard_map/ppermute | solution.py:40
  (11 other events, 188.0 us)

commit v3 on v2

--- a/solution.py
+++ b/solution.py
@@ -43,22 +43,23 @@
 SMEM = pl.BlockSpec(memory_space=pltpu.SMEM)
 ANY = pl.BlockSpec(memory_space=pl.ANY)
 HBM = pl.BlockSpec(memory_space=pltpu.HBM)
+VMEM = pl.BlockSpec(memory_space=pltpu.VMEM)
 
 
 def after(array, *others):
     return lax.optimization_barrier((array,) + others)[0]
 
 
-def kernel_call(kernel, scalars, arrays, outs, scratch=(), copies=32, limit=16, given=(), flops=10**6):
+def kernel_call(kernel, scalars, arrays, outs, scratch=(), copies=32, limit=16, given=(), near=(), out_spec=ANY, flops=10**6):
     return pl.pallas_call(
         kernel,
         out_shape=outs,
-        in_specs=[SMEM] * len(scalars) + [ANY] * len(arrays) + [HBM] * len(given),
-        out_specs=jax.tree.map(lambda _: ANY, outs),
+        in_specs=[SMEM] * len(scalars) + [ANY] * len(arrays) + [HBM] * len(given) + [VMEM] * len(near),
+        out_specs=jax.tree.map(lambda _: out_spec, outs),
         scratch_shapes=list(scratch) + [pltpu.SemaphoreType.DMA((copies,))],
         cost_estimate=pl.CostEstimate(flops=flops, bytes_accessed=10**5, transcendentals=0),
         compiler_params=pltpu.CompilerParams(vmem_limit_bytes=limit * MIB),
-    )(*scalars, *arrays, *given)
+    )(*scalars, *arrays, *given, *near)
 
 
 class Copies:
@@ -196,40 +197,31 @@
 
 def moments_kernel(
     edge0, inner0, edge1, inner1, edge2, inner2, edge3, inner3, fine_t, middle_t,
-    fine_m, middle_m, coarse_m, to_right, to_left, edges, inners, v_fine, v_middle, moments, sems,
-):
-    copies = Copies(sems)
-    loads = [copies.start(a, edges.at[k]) for k, a in enumerate((edge0, edge1, edge2, edge3))]
-    loads += [copies.start(a.at[pl.ds(0, 7)], inners.at[k]) for k, a in enumerate((inner0, inner1, inner2, inner3))]
-    loads += [copies.start(fine_t, v_fine), copies.start(middle_t, v_middle)]
-    for load in loads:
-        load.wait()
+    fine_m, middle_m, coarse_m, to_right, to_left, sems,
+):
+    edges, inners = (edge0, edge1, edge2, edge3), (inner0, inner1, inner2, inner3)
     fine = []
     for c in range(LEAVES):
-        turned = [basis_of(inners.at[k], c) for k in range(LV)]
-        points = [leaf_of(edges.at[k], inners.at[k], c) for k in range(LV)]
+        turned = [basis_of(inner, c) for inner in inners]
+        points = [leaf_of(edge, inner, c) for edge, inner in zip(edges, inners, strict=True)]
         fine.append(mm(jnp.concatenate(turned, axis=1), jnp.concatenate(points, axis=0)).astype(BF))
-        moments[c] = fine[c]
-    out = [
-        copies.start(moments.at[pl.ds(8, 8)], to_right.at[pl.ds(0, 8)]),
-        copies.start(moments.at[pl.ds(0, 8)], to_left.at[pl.ds(0, 8)]),
-        copies.start(moments.at[pl.ds(0, 16)], fine_m),
-    ]
-    middle = lifted(v_fine, fine, 16)
+        fine_m[c] = fine[c]
+        if c < 8:
+            to_left[c] = fine[c]
+        else:
+            to_right[c - 8] = fine[c]
+    middle = lifted(fine_t, fine, 16)
     for c in range(8):
-        moments[16 + c] = middle[c]
-    out += [
-        copies.start(moments.at[pl.ds(19, 5)], to_right.at[pl.ds(8, 5)]),
-        copies.start(moments.at[pl.ds(16, 5)], to_left.at[pl.ds(8, 5)]),
-        copies.start(moments.at[pl.ds(16, 8)], middle_m),
-    ]
-    coarse = lifted(v_middle, middle, 8)
+        middle_m[c] = middle[c]
+        if c < 5:
+            to_left[8 + c] = middle[c]
+        if c >= 3:
+            to_right[5 + c] = middle[c]
+    coarse = lifted(middle_t, middle, 8)
     for c in range(4):
-        moments[24 + c] = coarse[c]
-    out += [copies.start(moments.at[pl.ds(24, 4)], to.at[pl.ds(13, 4)]) for to in (to_right, to_left)]
-    out.append(copies.start(moments.at[pl.ds(24, 4)], coarse_m))
-    for copy in out:
-        copy.wait()
+        coarse_m[c] = coarse[c]
+        to_right[13 + c] = coarse[c]
+        to_left[13 + c] = coarse[c]
 
 
 def ends_kernel(edge0, edge1, edge2, edge3, to_core, to_chip, v_core, v_chip, sems):
@@ -275,10 +267,9 @@
 
 def near_kernel(
     near_cols, edge0, inner0, edge1, inner1, edge2, inner2, edge3, inner3, core_ends, chip_ends,
-    blocks, out, points, held, total, slots, sems,
+    held, out, points, total, slots, sems,
 ):
     copies = Copies(sems)
-    block_copies = [copies.start(blocks.at[pl.ds(0, 4)], held.at[pl.ds(0, 4)])]
     even = own_core() == 0
     loads = []
     for k, (edge, inner) in enumerate(((edge0, inner0), (edge1, inner1), (edge2, inner2), (edge3, inner3))):
@@ -289,8 +280,6 @@
         loads.append(copies.either(even, (chip, core), points.at[pl.ds(0, LOW), row, :]))
         core, chip = (end.at[pl.ds(LOW * k, HIGH)] for end in (core_ends, chip_ends))
         loads.append(copies.either(even, (core, chip), points.at[pl.ds(LOW + 16, HIGH), row, :]))
-    for g in range(1, 4):
-        block_copies.append(copies.start(blocks.at[pl.ds(4 * g, 4)], held.at[pl.ds(4 * g, 4)]))
     first_leaf = lax.axis_index("leaf") * LEAVES
 
     def place_slots(c, carry):
@@ -303,7 +292,6 @@
         load.wait()
     stores = []
     for g in range(4):
-        block_copies[g].wait()
         for source in range(15):
             held_by = [c for c in range(4) if 0 <= source - c < 12]
             rows = jnp.concatenate([held[4 * g + c, slots[4 * g + c, source - c]] for c in held_by], axis=0)
@@ -350,31 +338,27 @@
 
 def last_kernel(
     s_cols, fine_m, middle_m, coarse_m, low, high, inner0, inner1, inner2, inner3,
-    own_t, up_t, down_t, far_t, near, fine_t, middle_t, coarse_t, basis, out,
-    wide, v_couplings, top, v_fine, v_middle, v_coarse, v_basis, v_near, v_out, sems,
+    own_t, up_t, down_t, far_t, near, fine_t, middle_t, coarse_t, basis, out, wide, top, v_out, sems,
 ):
     copies = Copies(sems)
-    early = []
-    for k, inner in enumerate((inner0, inner1, inner2, inner3)):
-        early.append(copies.start(inner.at[pl.ds(7, 4)], v_couplings.at[k]))
-    early += [
-        copies.start(coarse_t, v_coarse), copies.start(low.at[pl.ds(13, 4)], wide.at[pl.ds(0, 4)]),
+    inners = (inner0, inner1, inner2, inner3)
+    early = [
+        copies.start(low.at[pl.ds(13, 4)], wide.at[pl.ds(0, 4)]),
         copies.start(coarse_m, wide.at[pl.ds(4, 4)]), copies.start(high.at[pl.ds(13, 4)], wide.at[pl.ds(8, 4)]),
     ]
     for k, piece in enumerate((own_t, up_t, down_t, far_t)):
-        early.append(copies.start(piece, top.at[lvl_at(k)]))
+        top[lvl_at(k)] = piece[...]
     early_middle = [
-        copies.start(middle_t, v_middle), copies.start(low.at[pl.ds(8, 5)], wide.at[pl.ds(12, 5)]),
+        copies.start(low.at[pl.ds(8, 5)], wide.at[pl.ds(12, 5)]),
         copies.start(middle_m, wide.at[pl.ds(17, 8)]), copies.start(high.at[pl.ds(8, 5)], wide.at[pl.ds(25, 5)]),
     ]
     early_fine = [
-        copies.start(fine_t, v_fine), copies.start(basis, v_basis), copies.start(low.at[pl.ds(0, 8)], wide.at[pl.ds(30, 8)]),
+        copies.start(low.at[pl.ds(0, 8)], wide.at[pl.ds(30, 8)]),
         copies.start(fine_m, wide.at[pl.ds(38, 16)]), copies.start(high.at[pl.ds(0, 8)], wide.at[pl.ds(54, 8)]),
     ]
-    near_loads = [copies.start(near.at[pl.ds(4 * g, 4)], v_near.at[pl.ds(4 * g, 4)]) for g in range(4)]
 
     def term(place, c, at):
-        lhs = jnp.concatenate([v_couplings[k, at // 8, :, lanes_of(at)] for k in range(LV)], axis=1)
+        lhs = jnp.concatenate([inner[7 + at // 8, :, lanes_of(at)] for inner in inners], axis=1)
         return mm(lhs, jnp.concatenate([wide[place + c + s_cols[k, at]] for k in range(LV)], axis=0))
 
     for load in early:
@@ -382,20 +366,18 @@
     coarse = []
     for c in range(4):
         parent = jnp.concatenate([top[j, c // 2] for j in range(LV)], axis=1)
-        coarse.append((term(4, c, 24 + c) + mm(v_coarse[c].astype(BF), parent)).astype(BF))
+        coarse.append((term(4, c, 24 + c) + mm(coarse_t[c].astype(BF), parent)).astype(BF))
     for load in early_middle:
         load.wait()
     middle = [
-        (term(17, c, 16 + c) + mm(v_middle[c].astype(BF), coarse[c // 2])).astype(BF) for c in range(8)
+        (term(17, c, 16 + c) + mm(middle_t[c].astype(BF), coarse[c // 2])).astype(BF) for c in range(8)
     ]
     for load in early_fine:
         load.wait()
     stores = []
     for c in range(16):
-        if c % 4 == 0:
-            near_loads[c // 4].wait()
-        local = term(38, c, c) + mm(v_fine[c].astype(BF), middle[c // 2])
-        v_out[c] = (v_near[c] + mm(v_basis[c], local.astype(BF))).astype(BF)
+        local = term(38, c, c) + mm(fine_t[c].astype(BF), middle[c // 2])
+        v_out[c] = (near[c] + mm(basis[c], local.astype(BF))).astype(BF)
         if c % 4 == 3:
             stores.append(copies.start(v_out.at[pl.ds(c - 3, 4)], out.at[pl.ds(c - 3, 4)]))
     for store in stores:
@@ -466,13 +448,10 @@
     fine_m, middle_m, coarse_m, to_right, to_left = kernel_call(
         moments_kernel,
         (),
-        pairs,
-        given=(transfer_fine, transfer_middle),
+        (),
+        near=pairs + (transfer_fine, transfer_middle),
         outs=(shape((16, 64, 512)), shape((8, 64, 512)), shape((4, 64, 512))) + (shape((17, 64, 512)),) * 2,
-        scratch=[
-            v((LV, 11, 64, 512), BF), v((LV, 7, 64, 512), BF), v((16, 64, 64), F32), v((8, 64, 64), F32),
-            v((28, 64, 512), BF),
-        ],
+        out_spec=VMEM,
     )
     low_m, high_m = over_leaf(to_right, step=1), over_leaf(to_left, step=-1)
 
@@ -493,23 +472,20 @@
         (near_cols,),
         pairs + (core_ends, chip_ends),
         shape((16, 64, 512), F32),
-        given=(near_blocks,),
+        near=(near_blocks,),
         limit=24,
         scratch=[
-            v((27, 256, 512), BF), v((16, 12, 64, 256), BF), v((16, 64, 512), F32), pltpu.SMEM((16, 12), jnp.int32),
+            v((27, 256, 512), BF), v((16, 64, 512), F32), pltpu.SMEM((16, 12), jnp.int32),
         ],
     )
     return kernel_call(
         last_kernel,
         (columns[:, 0, 0:32],),
-        (fine_m, middle_m, coarse_m, low_m, high_m) + inners + (term_top, up_t, down_t, far_t, near),
+        (fine_m, middle_m, coarse_m, low_m, high_m),
         shape((16, 64, 512)),
-        given=(transfer_fine, transfer_middle, transfer_coarse, leaf_basis),
-        copies=40,
-        scratch=[
-            v((62, 64, 512), BF), v((LV, 4, 64, 512), BF), v((LV, 2, 64, PART), BF), v((16, 64, 64), F32),
-            v((8, 64, 64), F32), v((4, 64, 64), F32), v((16, 64, 64), BF), v((16, 64, 512), F32), v((16, 64, 512), BF),
-        ],
+        near=inners
+        + (term_top, up_t, down_t, far_t, near, transfer_fine, transfer_middle, transfer_coarse, leaf_basis),
+        scratch=[v((62, 64, 512), BF), v((LV, 2, 64, PART), BF), v((16, 64, 512), BF)],
     )
 
 

time: 106 us -> 104 us (0.981)
  Pallas kernels: 32.9 us -> 28.3 us
  waiting for transfers between devices: 31.6 us -> 35 us
    pallas_call x9, Pallas kernels: 32.9 us -> 28.3 us  [kernel_call(): pl.pallas_call(kernel, out_shape=outs, in_specs=[SMEM] * len(scalars) + [...]
    ppermute x1, waiting for transfers between devices: 2.48 us -> 5.51 us  [chip_swap(): lax.ppermute(array, 'leaf', [(i, (i + (1 if i % CS else -1)) % leaves) fo...]
  transfers between devices with their start and end apart: 25 -> 25, of which waited for: 10 -> 10; matrix products, arithmetic and copies ran while one was open for 1% -> 1% of each run, Pallas kernels for 21% -> 18%
where the time goes in v3:
time: 104 us
  starting transfers between devices  39.5 us (38%)
  waiting for transfers between devices  35 us (34%)
  Pallas kernels  28.3 us (27%)
    pallas_call x9, Pallas kernels, kernel_call(): pl.pallas_call(kernel, out_shape=outs, in_specs=[SMEM] * len(scalars) + [...  28.3 us
    ppermute x12, starting transfers between devices, over_leaf(): return lax.ppermute(array, 'leaf', leaf_pairs(**move))  23.1 us
    ppermute x12, waiting for transfers between devices, over_leaf(): return lax.ppermute(array, 'leaf', leaf_pairs(**move))  19.5 us
    ppermute x12, starting transfers between devices, over_lvl(): return lax.ppermute(array, 'lvl', [(i, (i + step) % LV) for i in range(LV)])  16.2 us
    ppermute x12, waiting for transfers between devices, over_lvl(): return lax.ppermute(array, 'lvl', [(i, (i + step) % LV) for i in range(LV)])  9.99 us
    ppermute x1, waiting for transfers between devices, chip_swap(): lax.ppermute(array, 'leaf', [(i, (i + (1 if i % CS else -1)) % leaves) fo...  5.51 us
  transfers between devices with their start and end apart: 25, of which 10 were waited for; matrix products, arithmetic and copies ran while one was open for 1% of the time, Pallas kernels for 18%

profile of v3, /device:TPU:24, one launch (start us, length us, event | category | flops | bytes accessed | tf_op | source)
XLA Modules:
  0.0 104.1 jit_solution(14398807487266732346)
XLA Ops:
  0.0 3.0 %shard_map.145 = (bf16[11,64,512]{2,1,0:T(8,128)(2,1)}, bf16[11,64,512]{2,1,0:T(8,128)(2,1)}) custom-call(bf16[16,64,512]{2,1,0:T(8,128)(2,1)} %charges.1, bf16[16,64,64]{2,1,0:T(8,128)(2,1)} %basis.3, f32[16,1,64,64]{3,2,1,0:T(8,128)} %fine_c.1, f32[8,1,64,64]{3,2,1,0:T(8,128)} %middle_c.1, f32[4,1,64,64]{3,2,1,0:T(8,128)} %coarse_c.1, f32[2,2,64,64]{3,2,1,0:T(8,128)} %top_c.1), custom_call_target="tpu_custom_call" | custom-call | flops 1000000 | bytes 100000 | tf_op jit(solution)/shard_map/pallas_call | solution.py:54
  3.1 2.0 %collective-permute-start.6 = (bf16[11,64,512]{2,1,0:T(8,128)(2,1)}, bf16[11,64,512]{2,1,0:T(8,128)(2,1)S(1)}, u32[]{:S(2)}, u32[]{:S(2)}) collective-permute-start(bf16[11,64,512]{2,1,0:T(8,128)(2,1)} %get-tuple-element.26.edge.edge0), channel_id=1, source_target_pairs={{0,1},{1,2},{2,3},{3,0},{4,5},{5,6},{6,7},{7,4},{8,9},{9,10},{10,1... | collective-permute-start | bytes 2162696 | tf_op jit(solution)/shard_map/ppermute | solution.py:40
  5.2 4.2 %shard_map.146 = (bf16[144,128]{1,0:T(8,128)(2,1)}, bf16[144,128]{1,0:T(8,128)(2,1)}, bf16[144,128]{1,0:T(8,128)(2,1)}, bf16[144,128]{1,0:T(8,128)(2,1)}) custom-call(s32[16]{0:T(128)} %bitcast.12, s32[8]{0:T(128)} %bitcast.13, s32[4]{0:T(128)} %bitcast.14, s32[2,2]{1,0:T(2,128)} %top_cols.1, bf16[11,64,512]{2,1,0:T(8,128)(2,1)} %get-tuple-element.26.edge.edge0, ...), custom_call_target="tpu_custom_call" | custom-call | flops 1000000 | bytes 100000 | tf_op jit(solution)/shard_map/pallas_call | solution.py:54
  9.3 3.2 %collective-permute-start = (bf16[144,128]{1,0:T(8,128)(2,1)}, bf16[144,128]{1,0:T(8,128)(2,1)S(1)}, u32[]{:S(2)}, u32[]{:S(2)}) collective-permute-start(bf16[144,128]{1,0:T(8,128)(2,1)} %get-tuple-element.29), channel_id=1, source_target_pairs={{0,1},{1,2},{2,3},{3,0},{4,5},{5,6},{6,7},{7,4},{8,9},{9,10},{10,1... | collective-permute-start | bytes 110600 | tf_op jit(solution)/shard_map/ppermute | solution.py:40
  14.1 8.3 %collective-permute-done.part1 = bf16[144,128]{1,0:T(8,128)(2,1)S(1)} collective-permute-done((bf16[144,128]{1,0:T(8,128)(2,1)}, bf16[144,128]{1,0:T(8,128)(2,1)S(1)}, u32[]{:S(2)}, u32[]{:S(2)}) %collective-permute-start) | collective-permute-done | bytes 36896 | tf_op jit(solution)/shard_map/ppermute | solution.py:40
  24.2 3.2 %collective-permute-start.12 = (bf16[11,64,512]{2,1,0:T(8,128)(2,1)S(1)}, bf16[11,64,512]{2,1,0:T(8,128)(2,1)S(1)}, u32[]{:S(2)}, u32[]{:S(2)}) collective-permute-start(bf16[11,64,512]{2,1,0:T(8,128)(2,1)S(1)} %collective-permute-done.6.edge1), channel_id=1, source_target_pairs={{0,1},{1,2},{2,3},{3,0},{4,5},{5,6},{6,7},{7,4},{8,9},{9,10},{10,1... | collective-permute-start | bytes 2162696 | tf_op jit(solution)/shard_map/ppermute | solution.py:40
  28.2 2.0 %collective-permute-start.8 = (bf16[2,64,128]{2,1,0:T(8,128)(2,1)S(1)}, bf16[2,64,128]{2,1,0:T(8,128)(2,1)S(1)}, u32[]{:S(2)}, u32[]{:S(2)}) collective-permute-start(bf16[2,64,128]{2,1,0:T(8,128)(2,1)S(1)} %bitcast.8), channel_id=1, source_target_pairs={{0,32},{4,36},{8,40},{12,44},{16,48},{20,52},{24,56},{28,60},{32,6... | collective-permute-start | bytes 98312 | tf_op jit(solution)/shard_map/ppermute | solution.py:36
  30.1 4.0 %collective-permute-start.9 = (bf16[2,64,128]{2,1,0:T(8,128)(2,1)S(1)}, bf16[2,64,128]{2,1,0:T(8,128)(2,1)S(1)}, u32[]{:S(2)}, u32[]{:S(2)}) collective-permute-start(bf16[2,64,128]{2,1,0:T(8,128)(2,1)S(1)} %bitcast.9), channel_id=1, source_target_pairs={{0,224},{4,228},{8,232},{12,236},{16,240},{20,244},{24,248},{28,25... | collective-permute-start | bytes 98312 | tf_op jit(solution)/shard_map/ppermute | solution.py:36
  34.2 1.8 %collective-permute-done.8 = bf16[2,64,128]{2,1,0:T(8,128)(2,1)S(1)} collective-permute-done((bf16[2,64,128]{2,1,0:T(8,128)(2,1)S(1)}, bf16[2,64,128]{2,1,0:T(8,128)(2,1)S(1)}, u32[]{:S(2)}, u32[]{:S(2)}) %collective-permute-start.8) | collective-permute-done | bytes 32800 | tf_op jit(solution)/shard_map/ppermute | solution.py:36
  36.0 5.1 %collective-permute-start.10 = (bf16[6,64,128]{2,1,0:T(8,128)(2,1)S(1)}, bf16[6,64,128]{2,1,0:T(8,128)(2,1)S(1)}, u32[]{:S(2)}, u32[]{:S(2)}) collective-permute-start(bf16[6,64,128]{2,1,0:T(8,128)(2,1)S(1)} %constant_dynamic-update-slice_fusion.refs_1_), channel_id=1, source_target_pairs={{0,96},{4,100},{8,104},{12,108},{16,112},{20,116},{24,120},{28,124... | collective-permute-start | bytes 294920 | tf_op jit(solution)/shard_map/ppermute | solution.py:36
  41.2 6.0 %collective-permute-done.11.refs_2_ = bf16[4,64,128]{2,1,0:T(8,128)(2,1)S(1)} collective-permute-done((bf16[4,64,128]{2,1,0:T(8,128)(2,1)S(1)}, bf16[4,64,128]{2,1,0:T(8,128)(2,1)S(1)}, u32[]{:S(2)}, u32[]{:S(2)}) %collective-permute-start.11) | collective-permute-done | bytes 65568 | tf_op jit(solution)/shard_map/ppermute | solution.py:36
  48.3 2.8 %collective-permute-start.14 = (bf16[16,64,128]{2,1,0:T(8,128)(2,1)S(1)}, bf16[16,64,128]{2,1,0:T(8,128)(2,1)S(1)}, u32[]{:S(2)}, u32[]{:S(2)}) collective-permute-start(bf16[16,64,128]{2,1,0:T(8,128)(2,1)S(1)} %shard_map.147.refs_0_), channel_id=1, source_target_pairs={{0,24},{4,28},{8,0},{12,4},{16,8},{20,12},{24,16},{28,20},{32,56},... | collective-permute-start | bytes 786440 | tf_op jit(solution)/shard_map/ppermute | solution.py:36
  51.3 1.9 %collective-permute-start.5 = (bf16[11,64,512]{2,1,0:T(8,128)(2,1)S(1)}, bf16[11,64,512]{2,1,0:T(8,128)(2,1)S(1)}, u32[]{:S(2)}, u32[]{:S(2)}) collective-permute-start(bf16[11,64,512]{2,1,0:T(8,128)(2,1)S(1)} %collective-permute-done.4.inner2.down), channel_id=1, source_target_pairs={{0,3},{1,0},{2,1},{3,2},{4,7},{5,4},{6,5},{7,6},{8,11},{9,8},{10,9... | collective-permute-start | bytes 2162696 | tf_op jit(solution)/shard_map/ppermute | solution.py:40
  53.1 3.3 %collective-permute-done.14.refs_2_ = bf16[16,64,128]{2,1,0:T(8,128)(2,1)S(1)} collective-permute-done((bf16[16,64,128]{2,1,0:T(8,128)(2,1)S(1)}, bf16[16,64,128]{2,1,0:T(8,128)(2,1)S(1)}, u32[]{:S(2)}, u32[]{:S(2)}) %collective-permute-start.14) | collective-permute-done | bytes 262176 | tf_op jit(solution)/shard_map/ppermute | solution.py:36
  56.4 3.8 %collective-permute-start.16 = (bf16[8,64,128]{2,1,0:T(8,128)(2,1)S(1)}, bf16[8,64,128]{2,1,0:T(8,128)(2,1)S(1)}, u32[]{:S(2)}, u32[]{:S(2)}) collective-permute-start(bf16[8,64,128]{2,1,0:T(8,128)(2,1)S(1)} %slice.34), channel_id=1, source_target_pairs={{0,24},{4,28},{8,0},{12,4},{16,8},{20,12},{24,16},{28,20},{32,56},... | collective-permute-start | bytes 393224 | tf_op jit(solution)/shard_map/ppermute | solution.py:36
  60.3 2.0 %shard_map.151 = (bf16[24,64,512]{2,1,0:T(8,128)(2,1)S(1)}, bf16[24,64,512]{2,1,0:T(8,128)(2,1)S(1)}) custom-call(bf16[11,64,512]{2,1,0:T(8,128)(2,1)S(1)} %copy-done.1, bf16[11,64,512]{2,1,0:T(8,128)(2,1)S(1)} %collective-permute-done.6.edge1, bf16[11,64,512]{2,1,0:T(8,128)(2,1)S(1)} %collective-permute-done.7.edge2, ...), custom_call_target="tpu_custom_call" | custom-call | flops 1000000 | bytes 100000 | tf_op jit(solution)/shard_map/pallas_call | solution.py:54
  62.7 3.8 %collective-permute-done.15.refs_3_ = bf16[8,64,128]{2,1,0:T(8,128)(2,1)S(1)} collective-permute-done((bf16[8,64,128]{2,1,0:T(8,128)(2,1)S(1)}, bf16[8,64,128]{2,1,0:T(8,128)(2,1)S(1)}, u32[]{:S(2)}, u32[]{:S(2)}) %collective-permute-start.15) | collective-permute-done | bytes 131104 | tf_op jit(solution)/shard_map/ppermute | solution.py:36
  68.6 4.6 %collective-permute-start.19 = (bf16[17,64,512]{2,1,0:T(8,128)(2,1)S(1)}, bf16[17,64,512]{2,1,0:T(8,128)(2,1)S(1)}, u32[]{:S(2)}, u32[]{:S(2)}) collective-permute-start(bf16[17,64,512]{2,1,0:T(8,128)(2,1)S(1)} %get-tuple-element.41), channel_id=1, source_target_pairs={{0,252},{4,0},{8,4},{12,8},{16,12},{20,16},{24,20},{28,24},{32,28}... | collective-permute-start | bytes 3342344 | tf_op jit(solution)/shard_map/ppermute | solution.py:36
  74.4 2.6 %collective-permute-done.17.partner = bf16[64,64,128]{2,1,0:T(8,128)(2,1)S(1)} collective-permute-done((bf16[64,64,128]{2,1,0:T(8,128)(2,1)S(1)}, bf16[64,64,128]{2,1,0:T(8,128)(2,1)S(1)}, u32[]{:S(2)}, u32[]{:S(2)}) %collective-permute-start.17) | collective-permute-done | bytes 1048608 | tf_op jit(solution)/shard_map/ppermute | solution.py:36
  77.0 2.2 %shard_map.150 = (bf16[2,64,128]{2,1,0:T(8,128)(2,1)S(1)}, s32[4,8,128]{2,1,0:T(8,128)S(1)}) custom-call(bf16[144,128]{1,0:T(8,128)(2,1)S(1)} %copy-done.6, bf16[144,128]{1,0:T(8,128)(2,1)S(1)} %collective-permute-done.part1, bf16[144,128]{1,0:T(8,128)(2,1)S(1)} %collective-permute-done.1.part2, bf16[144,128]{1,0:T(8,128)(2,1)S(1)} %collective-permute-done.2.part3, ...), custom_call_target="tpu_custom_call" | custom-call | flops 1000000 | bytes 100000 | tf_op jit(solution)/shard_map/pallas_call | solution.py:54
  80.1 5.5 %collective-permute-done.24.chip_ends = bf16[24,64,512]{2,1,0:T(8,128)(2,1)S(1)} collective-permute-done((bf16[24,64,512]{2,1,0:T(8,128)(2,1)S(1)}, bf16[24,64,512]{2,1,0:T(8,128)(2,1)S(1)}, u32[]{:S(2)}, u32[]{:S(2)}) %collective-permute-start.24) | collective-permute-done | bytes 1572896 | tf_op jit(solution)/shard_map/ppermute | solution.py:247
  85.6 3.2 %collective-permute-start.20 = (bf16[2,64,128]{2,1,0:T(8,128)(2,1)S(1)}, bf16[2,64,128]{2,1,0:T(8,128)(2,1)S(1)}, u32[]{:S(2)}, u32[]{:S(2)}) collective-permute-start(bf16[2,64,128]{2,1,0:T(8,128)(2,1)S(1)} %get-tuple-element.42.own_t), channel_id=1, source_target_pairs={{0,1},{1,2},{2,3},{3,0},{4,5},{5,6},{6,7},{7,4},{8,9},{9,10},{10,1... | collective-permute-start | bytes 98312 | tf_op jit(solution)/shard_map/ppermute | solution.py:40
  88.9 6.9 %shard_map.152.near = f32[16,64,512]{2,1,0:T(8,128)S(1)} custom-call(s32[16,12]{1,0:T(8,128)S(1)} %copy-done.7, bf16[11,64,512]{2,1,0:T(8,128)(2,1)S(1)} %copy-done.1, bf16[11,64,512]{2,1,0:T(8,128)(2,1)S(1)} %copy-done, bf16[11,64,512]{2,1,0:T(8,128)(2,1)S(1)} %collective-permute-done.6.edge1, bf16[11,64,512]{2,1,0:T(8,128)(2,1)S(1)} %collective-permute-done.3.inner1.up, ...), custom_call_target="tpu_custom_call" | custom-call | flops 1000000 | bytes 100000 | tf_op jit(solution)/shard_map/pallas_call | solution.py:54
  97.6 6.4 %shard_map.153 = bf16[16,64,512]{2,1,0:T(8,128)(2,1)} custom-call(s32[4,32]{1,0:T(4,128)S(1)} %bitcast.7, bf16[16,64,512]{2,1,0:T(8,128)(2,1)S(1)} %get-tuple-element.35.fine_m, bf16[8,64,512]{2,1,0:T(8,128)(2,1)S(1)} %get-tuple-element.38.middle_m, bf16[4,64,512]{2,1,0:T(8,128)(2,1)S(1)} %get-tuple-element.39.coarse_m, ...), custom_call_target="tpu_custom_call" | custom-call | flops 1000000 | bytes 100000 | tf_op jit(solution)/shard_map/pallas_call | solution.py:54
  (64 shorter events, 11.8 us)
Async XLA Ops:
  3.1 21.1 %collective-permute-start.6 = (bf16[11,64,512]{2,1,0:T(8,128)(2,1)}, bf16[11,64,512]{2,1,0:T(8,128)(2,1)S(1)}, u32[]{:S(2)}, u32[]{:S(2)}) collective-permute-start(bf16[11,64,512]{2,1,0:T(8,128)(2,1)} %get-tuple-element.26.edge.edge0), channel_id=1, source_target_pairs={{0,1},{1,2},{2,3},{3,0},{4,5},{5,6},{6,7},{7,4},{8,9},{9,10},{10,1... | collective-permute-start | bytes 2162696 | tf_op jit(solution)/shard_map/ppermute | solution.py:40
  5.1 23.0 %collective-permute-start.7 = (bf16[11,64,512]{2,1,0:T(8,128)(2,1)}, bf16[11,64,512]{2,1,0:T(8,128)(2,1)S(1)}, u32[]{:S(2)}, u32[]{:S(2)}) collective-permute-start(bf16[11,64,512]{2,1,0:T(8,128)(2,1)} %get-tuple-element.26.edge.edge0), channel_id=1, source_target_pairs={{0,3},{1,0},{2,1},{3,2},{4,7},{5,4},{6,5},{7,6},{8,11},{9,8},{10,9... | collective-permute-start | bytes 2162696 | tf_op jit(solution)/shard_map/ppermute | solution.py:40
  9.3 13.1 %collective-permute-start = (bf16[144,128]{1,0:T(8,128)(2,1)}, bf16[144,128]{1,0:T(8,128)(2,1)S(1)}, u32[]{:S(2)}, u32[]{:S(2)}) collective-permute-start(bf16[144,128]{1,0:T(8,128)(2,1)} %get-tuple-element.29), channel_id=1, source_target_pairs={{0,1},{1,2},{2,3},{3,0},{4,5},{5,6},{6,7},{7,4},{8,9},{9,10},{10,1... | collective-permute-start | bytes 110600 | tf_op jit(solution)/shard_map/ppermute | solution.py:40
  12.6 11.5 %collective-permute-start.1 = (bf16[144,128]{1,0:T(8,128)(2,1)}, bf16[144,128]{1,0:T(8,128)(2,1)S(1)}, u32[]{:S(2)}, u32[]{:S(2)}) collective-permute-start(bf16[144,128]{1,0:T(8,128)(2,1)} %get-tuple-element.30), channel_id=1, source_target_pairs={{0,3},{1,0},{2,1},{3,2},{4,7},{5,4},{6,5},{7,6},{8,11},{9,8},{10,9... | collective-permute-start | bytes 110600 | tf_op jit(solution)/shard_map/ppermute | solution.py:40
  12.6 11.5 %collective-permute-start.2 = (bf16[144,128]{1,0:T(8,128)(2,1)}, bf16[144,128]{1,0:T(8,128)(2,1)S(1)}, u32[]{:S(2)}, u32[]{:S(2)}) collective-permute-start(bf16[144,128]{1,0:T(8,128)(2,1)} %get-tuple-element.31), channel_id=1, source_target_pairs={{0,2},{1,3},{2,0},{3,1},{4,6},{5,7},{6,4},{7,5},{8,10},{9,11},{10,... | collective-permute-start | bytes 110600 | tf_op jit(solution)/shard_map/ppermute | solution.py:40
  24.1 24.1 %collective-permute-start.4 = (bf16[11,64,512]{2,1,0:T(8,128)(2,1)S(1)}, bf16[11,64,512]{2,1,0:T(8,128)(2,1)S(1)}, u32[]{:S(2)}, u32[]{:S(2)}) collective-permute-start(bf16[11,64,512]{2,1,0:T(8,128)(2,1)S(1)} %copy-done), channel_id=1, source_target_pairs={{0,3},{1,0},{2,1},{3,2},{4,7},{5,4},{6,5},{7,6},{8,11},{9,8},{10,9... | collective-permute-start | bytes 2162696 | tf_op jit(solution)/shard_map/ppermute | solution.py:40
  24.2 24.1 %collective-permute-start.12 = (bf16[11,64,512]{2,1,0:T(8,128)(2,1)S(1)}, bf16[11,64,512]{2,1,0:T(8,128)(2,1)S(1)}, u32[]{:S(2)}, u32[]{:S(2)}) collective-permute-start(bf16[11,64,512]{2,1,0:T(8,128)(2,1)S(1)} %collective-permute-done.6.edge1), channel_id=1, source_target_pairs={{0,1},{1,2},{2,3},{3,0},{4,5},{5,6},{6,7},{7,4},{8,9},{9,10},{10,1... | collective-permute-start | bytes 2162696 | tf_op jit(solution)/shard_map/ppermute | solution.py:40
  28.2 7.8 %collective-permute-start.8 = (bf16[2,64,128]{2,1,0:T(8,128)(2,1)S(1)}, bf16[2,64,128]{2,1,0:T(8,128)(2,1)S(1)}, u32[]{:S(2)}, u32[]{:S(2)}) collective-permute-start(bf16[2,64,128]{2,1,0:T(8,128)(2,1)S(1)} %bitcast.8), channel_id=1, source_target_pairs={{0,32},{4,36},{8,40},{12,44},{16,48},{20,52},{24,56},{28,60},{32,6... | collective-permute-start | bytes 98312 | tf_op jit(solution)/shard_map/ppermute | solution.py:36
  30.1 5.8 %collective-permute-start.9 = (bf16[2,64,128]{2,1,0:T(8,128)(2,1)S(1)}, bf16[2,64,128]{2,1,0:T(8,128)(2,1)S(1)}, u32[]{:S(2)}, u32[]{:S(2)}) collective-permute-start(bf16[2,64,128]{2,1,0:T(8,128)(2,1)S(1)} %bitcast.9), channel_id=1, source_target_pairs={{0,224},{4,228},{8,232},{12,236},{16,240},{20,244},{24,248},{28,25... | collective-permute-start | bytes 98312 | tf_op jit(solution)/shard_map/ppermute | solution.py:36
  36.0 11.3 %collective-permute-start.10 = (bf16[6,64,128]{2,1,0:T(8,128)(2,1)S(1)}, bf16[6,64,128]{2,1,0:T(8,128)(2,1)S(1)}, u32[]{:S(2)}, u32[]{:S(2)}) collective-permute-start(bf16[6,64,128]{2,1,0:T(8,128)(2,1)S(1)} %constant_dynamic-update-slice_fusion.refs_1_), channel_id=1, source_target_pairs={{0,96},{4,100},{8,104},{12,108},{16,112},{20,116},{24,120},{28,124... | collective-permute-start | bytes 294920 | tf_op jit(solution)/shard_map/ppermute | solution.py:36
  41.1 6.1 %collective-permute-start.11 = (bf16[4,64,128]{2,1,0:T(8,128)(2,1)S(1)}, bf16[4,64,128]{2,1,0:T(8,128)(2,1)S(1)}, u32[]{:S(2)}, u32[]{:S(2)}) collective-permute-start(bf16[4,64,128]{2,1,0:T(8,128)(2,1)S(1)} %pad_maximum_fusion), channel_id=1, source_target_pairs={{0,160},{4,164},{8,168},{12,172},{16,176},{20,180},{24,184},{28,18... | collective-permute-start | bytes 196616 | tf_op jit(solution)/shard_map/ppermute | solution.py:36
  48.3 8.1 %collective-permute-start.14 = (bf16[16,64,128]{2,1,0:T(8,128)(2,1)S(1)}, bf16[16,64,128]{2,1,0:T(8,128)(2,1)S(1)}, u32[]{:S(2)}, u32[]{:S(2)}) collective-permute-start(bf16[16,64,128]{2,1,0:T(8,128)(2,1)S(1)} %shard_map.147.refs_0_), channel_id=1, source_target_pairs={{0,24},{4,28},{8,0},{12,4},{16,8},{20,12},{24,16},{28,20},{32,56},... | collective-permute-start | bytes 786440 | tf_op jit(solution)/shard_map/ppermute | solution.py:36
  51.1 9.1 %collective-permute-start.13 = (bf16[16,64,128]{2,1,0:T(8,128)(2,1)S(1)}, bf16[16,64,128]{2,1,0:T(8,128)(2,1)S(1)}, u32[]{:S(2)}, u32[]{:S(2)}) collective-permute-start(bf16[16,64,128]{2,1,0:T(8,128)(2,1)S(1)} %shard_map.147.refs_0_), channel_id=1, source_target_pairs={{0,8},{4,12},{8,16},{12,20},{16,24},{20,28},{24,0},{28,4},{32,40},... | collective-permute-start | bytes 786440 | tf_op jit(solution)/shard_map/ppermute | solution.py:36
  51.1 15.4 %collective-permute-start.3 = (bf16[11,64,512]{2,1,0:T(8,128)(2,1)S(1)}, bf16[11,64,512]{2,1,0:T(8,128)(2,1)S(1)}, u32[]{:S(2)}, u32[]{:S(2)}) collective-permute-start(bf16[11,64,512]{2,1,0:T(8,128)(2,1)S(1)} %copy-done), channel_id=1, source_target_pairs={{0,1},{1,2},{2,3},{3,0},{4,5},{5,6},{6,7},{7,4},{8,9},{9,10},{10,1... | collective-permute-start | bytes 2162696 | tf_op jit(solution)/shard_map/ppermute | solution.py:40
  51.3 15.2 %collective-permute-start.5 = (bf16[11,64,512]{2,1,0:T(8,128)(2,1)S(1)}, bf16[11,64,512]{2,1,0:T(8,128)(2,1)S(1)}, u32[]{:S(2)}, u32[]{:S(2)}) collective-permute-start(bf16[11,64,512]{2,1,0:T(8,128)(2,1)S(1)} %collective-permute-done.4.inner2.down), channel_id=1, source_target_pairs={{0,3},{1,0},{2,1},{3,2},{4,7},{5,4},{6,5},{7,6},{8,11},{9,8},{10,9... | collective-permute-start | bytes 2162696 | tf_op jit(solution)/shard_map/ppermute | solution.py:40
  56.4 6.3 %collective-permute-start.16 = (bf16[8,64,128]{2,1,0:T(8,128)(2,1)S(1)}, bf16[8,64,128]{2,1,0:T(8,128)(2,1)S(1)}, u32[]{:S(2)}, u32[]{:S(2)}) collective-permute-start(bf16[8,64,128]{2,1,0:T(8,128)(2,1)S(1)} %slice.34), channel_id=1, source_target_pairs={{0,24},{4,28},{8,0},{12,4},{16,8},{20,12},{24,16},{28,20},{32,56},... | collective-permute-start | bytes 393224 | tf_op jit(solution)/shard_map/ppermute | solution.py:36
  60.2 6.3 %collective-permute-start.15 = (bf16[8,64,128]{2,1,0:T(8,128)(2,1)S(1)}, bf16[8,64,128]{2,1,0:T(8,128)(2,1)S(1)}, u32[]{:S(2)}, u32[]{:S(2)}) collective-permute-start(bf16[8,64,128]{2,1,0:T(8,128)(2,1)S(1)} %slice.33), channel_id=1, source_target_pairs={{0,8},{4,12},{8,16},{12,20},{16,24},{20,28},{24,0},{28,4},{32,40},... | collective-permute-start | bytes 393224 | tf_op jit(solution)/shard_map/ppermute | solution.py:36
  62.4 23.2 %collective-permute-start.24 = (bf16[24,64,512]{2,1,0:T(8,128)(2,1)S(1)}, bf16[24,64,512]{2,1,0:T(8,128)(2,1)S(1)}, u32[]{:S(2)}, u32[]{:S(2)}) collective-permute-start(bf16[24,64,512]{2,1,0:T(8,128)(2,1)S(1)} %get-tuple-element.46), channel_id=1, source_target_pairs={{0,252},{4,8},{8,4},{12,16},{16,12},{20,24},{24,20},{28,32},{32,28... | collective-permute-start | bytes 4718600 | tf_op jit(solution)/shard_map/ppermute | solution.py:247
  66.5 19.1 %collective-permute-start.23 = (bf16[24,64,512]{2,1,0:T(8,128)(2,1)S(1)}, bf16[24,64,512]{2,1,0:T(8,128)(2,1)S(1)}, u32[]{:S(2)}, u32[]{:S(2)}) collective-permute-start(bf16[24,64,512]{2,1,0:T(8,128)(2,1)S(1)} %get-tuple-element.45), channel_id=1, source_target_pairs={{0,4},{4,0},{8,12},{12,8},{16,20},{20,16},{24,28},{28,24},{32,36},... | collective-permute-start | bytes 4718600 | tf_op jit(solution)/shard_map/ppermute | solution.py:36
  68.0 29.5 %collective-permute-start.18 = (bf16[17,64,512]{2,1,0:T(8,128)(2,1)S(1)}, bf16[17,64,512]{2,1,0:T(8,128)(2,1)S(1)}, u32[]{:S(2)}, u32[]{:S(2)}) collective-permute-start(bf16[17,64,512]{2,1,0:T(8,128)(2,1)S(1)} %get-tuple-element.40), channel_id=1, source_target_pairs={{0,4},{4,8},{8,12},{12,16},{16,20},{20,24},{24,28},{28,32},{32,36}... | collective-permute-start | bytes 3342344 | tf_op jit(solution)/shard_map/ppermute | solution.py:36
  68.6 29.0 %collective-permute-start.19 = (bf16[17,64,512]{2,1,0:T(8,128)(2,1)S(1)}, bf16[17,64,512]{2,1,0:T(8,128)(2,1)S(1)}, u32[]{:S(2)}, u32[]{:S(2)}) collective-permute-start(bf16[17,64,512]{2,1,0:T(8,128)(2,1)S(1)} %get-tuple-element.41), channel_id=1, source_target_pairs={{0,252},{4,0},{8,4},{12,8},{16,12},{20,16},{24,20},{28,24},{32,28}... | collective-permute-start | bytes 3342344 | tf_op jit(solution)/shard_map/ppermute | solution.py:36
  79.3 18.3 %collective-permute-start.22 = (bf16[2,64,128]{2,1,0:T(8,128)(2,1)S(1)}, bf16[2,64,128]{2,1,0:T(8,128)(2,1)S(1)}, u32[]{:S(2)}, u32[]{:S(2)}) collective-permute-start(bf16[2,64,128]{2,1,0:T(8,128)(2,1)S(1)} %get-tuple-element.42.own_t), channel_id=1, source_target_pairs={{0,2},{1,3},{2,0},{3,1},{4,6},{5,7},{6,4},{7,5},{8,10},{9,11},{10,... | collective-permute-start | bytes 98312 | tf_op jit(solution)/shard_map/ppermute | solution.py:40
  85.6 11.9 %collective-permute-start.21 = (bf16[2,64,128]{2,1,0:T(8,128)(2,1)S(1)}, bf16[2,64,128]{2,1,0:T(8,128)(2,1)S(1)}, u32[]{:S(2)}, u32[]{:S(2)}) collective-permute-start(bf16[2,64,128]{2,1,0:T(8,128)(2,1)S(1)} %get-tuple-element.42.own_t), channel_id=1, source_target_pairs={{0,3},{1,0},{2,1},{3,2},{4,7},{5,4},{6,5},{7,6},{8,11},{9,8},{10,9... | collective-permute-start | bytes 98312 | tf_op jit(solution)/shard_map/ppermute | solution.py:40
  85.6 11.9 %collective-permute-start.20 = (bf16[2,64,128]{2,1,0:T(8,128)(2,1)S(1)}, bf16[2,64,128]{2,1,0:T(8,128)(2,1)S(1)}, u32[]{:S(2)}, u32[]{:S(2)}) collective-permute-start(bf16[2,64,128]{2,1,0:T(8,128)(2,1)S(1)} %get-tuple-element.42.own_t), channel_id=1, source_target_pairs={{0,1},{1,2},{2,3},{3,0},{4,5},{5,6},{6,7},{7,4},{8,9},{9,10},{10,1... | collective-permute-start | bytes 98312 | tf_op jit(solution)/shard_map/ppermute | solution.py:40
  (11 other events, 191.1 us)

commit v4 on v3

--- a/solution.py
+++ b/solution.py
@@ -338,45 +338,49 @@
 
 def last_kernel(
     s_cols, fine_m, middle_m, coarse_m, low, high, inner0, inner1, inner2, inner3,
-    own_t, up_t, down_t, far_t, near, fine_t, middle_t, coarse_t, basis, out, wide, top, v_out, sems,
+    own_t, up_t, down_t, far_t, near, fine_t, middle_t, coarse_t, basis, out, v_couplings, top, v_out, slots, sems,
 ):
     copies = Copies(sems)
-    inners = (inner0, inner1, inner2, inner3)
-    early = [
-        copies.start(low.at[pl.ds(13, 4)], wide.at[pl.ds(0, 4)]),
-        copies.start(coarse_m, wide.at[pl.ds(4, 4)]), copies.start(high.at[pl.ds(13, 4)], wide.at[pl.ds(8, 4)]),
+    loads = [
+        copies.start(inner.at[pl.ds(7, 4)], v_couplings.at[k])
+        for k, inner in enumerate((inner0, inner1, inner2, inner3))
     ]
     for k, piece in enumerate((own_t, up_t, down_t, far_t)):
         top[lvl_at(k)] = piece[...]
-    early_middle = [
-        copies.start(low.at[pl.ds(8, 5)], wide.at[pl.ds(12, 5)]),
-        copies.start(middle_m, wide.at[pl.ds(17, 8)]), copies.start(high.at[pl.ds(8, 5)], wide.at[pl.ds(25, 5)]),
-    ]
-    early_fine = [
-        copies.start(low.at[pl.ds(0, 8)], wide.at[pl.ds(30, 8)]),
-        copies.start(fine_m, wide.at[pl.ds(38, 16)]), copies.start(high.at[pl.ds(0, 8)], wide.at[pl.ds(54, 8)]),
-    ]
-
-    def term(place, c, at):
-        lhs = jnp.concatenate([inner[7 + at // 8, :, lanes_of(at)] for inner in inners], axis=1)
-        return mm(lhs, jnp.concatenate([wide[place + c + s_cols[k, at]] for k in range(LV)], axis=0))
-
-    for load in early:
-        load.wait()
+    for at in range(28):
+        reach = 8 if at < 16 else 5 if at < 24 else 4
+        for k in range(LV):
+            away = s_cols[k, at]
+            slots[at, jnp.where(away < 0, away + reach, away - reach + 3)] = k
+    for load in loads:
+        load.wait()
+
+    def term(moments, first, reach, rim, c, at):
+        count = moments.shape[0]
+        lhs, rhs = [], []
+        for place, away in enumerate((-reach, 1 - reach, reach - 1, reach)):
+            lhs.append(v_couplings[slots[at, place], at // 8, :, lanes_of(at)])
+            source = c + away
+            if source < 0:
+                rhs.append(low[first + rim + source])
+            elif source < count:
+                rhs.append(moments[source])
+            else:
+                rhs.append(high[first + source - count])
+        return mm(jnp.concatenate(lhs, axis=1), jnp.concatenate(rhs, axis=0))
+
     coarse = []
     for c in range(4):
         parent = jnp.concatenate([top[j, c // 2] for j in range(LV)], axis=1)
-        coarse.append((term(4, c, 24 + c) + mm(coarse_t[c].astype(BF), parent)).astype(BF))
-    for load in early_middle:
-        load.wait()
+        local = term(coarse_m, 13, 4, 4, c, 24 + c) + mm(coarse_t[c].astype(BF), parent)
+        coarse.append(local.astype(BF))
     middle = [
-        (term(17, c, 16 + c) + mm(middle_t[c].astype(BF), coarse[c // 2])).astype(BF) for c in range(8)
-    ]
-    for load in early_fine:
-        load.wait()
+        (term(middle_m, 8, 5, 5, c, 16 + c) + mm(middle_t[c].astype(BF), coarse[c // 2])).astype(BF)
+        for c in range(8)
+    ]
     stores = []
     for c in range(16):
-        local = term(38, c, c) + mm(fine_t[c].astype(BF), middle[c // 2])
+        local = term(fine_m, 0, 8, 8, c, c) + mm(fine_t[c].astype(BF), middle[c // 2])
         v_out[c] = (near[c] + mm(basis[c], local.astype(BF))).astype(BF)
         if c % 4 == 3:
             stores.append(copies.start(v_out.at[pl.ds(c - 3, 4)], out.at[pl.ds(c - 3, 4)]))
@@ -481,11 +485,13 @@
     return kernel_call(
         last_kernel,
         (columns[:, 0, 0:32],),
-        (fine_m, middle_m, coarse_m, low_m, high_m),
+        (),
         shape((16, 64, 512)),
-        near=inners
+        near=(fine_m, middle_m, coarse_m, low_m, high_m) + inners
         + (term_top, up_t, down_t, far_t, near, transfer_fine, transfer_middle, transfer_coarse, leaf_basis),
-        scratch=[v((62, 64, 512), BF), v((LV, 2, 64, PART), BF), v((16, 64, 512), BF)],
+        scratch=[
+            v((LV, 4, 64, 512), BF), v((LV, 2, 64, PART), BF), v((16, 64, 512), BF), pltpu.SMEM((28, LV), jnp.int32),
+        ],
     )
 
 

time: 104 us -> 104 us (level)
  no operation moved by 1% of the time
where the time goes in v4:
time: 104 us
  starting transfers between devices  39.5 us (38%)
  waiting for transfers between devices  35 us (34%)
  Pallas kernels  28 us (27%)
    pallas_call x9, Pallas kernels, kernel_call(): pl.pallas_call(kernel, out_shape=outs, in_specs=[SMEM] * len(scalars) + [...  28 us
    ppermute x12, starting transfers between devices, over_leaf(): return lax.ppermute(array, 'leaf', leaf_pairs(**move))  23.1 us
    ppermute x12, waiting for transfers between devices, over_leaf(): return lax.ppermute(array, 'leaf', leaf_pairs(**move))  19.5 us
    ppermute x12, starting transfers between devices, over_lvl(): return lax.ppermute(array, 'lvl', [(i, (i + step) % LV) for i in range(LV)])  16.2 us
    ppermute x12, waiting for transfers between devices, over_lvl(): return lax.ppermute(array, 'lvl', [(i, (i + step) % LV) for i in range(LV)])  9.99 us
    ppermute x1, waiting for transfers between devices, chip_swap(): lax.ppermute(array, 'leaf', [(i, (i + (1 if i % CS else -1)) % leaves) fo...  5.5 us
  transfers between devices with their start and end apart: 25, of which 10 were waited for; matrix products, arithmetic and copies ran while one was open for 1% of the time, Pallas kernels for 18%

profile of v4, /device:TPU:24, one launch (start us, length us, event | category | flops | bytes accessed | tf_op | source)
XLA Modules:
  0.0 103.9 jit_solution(14707237131268687376)
XLA Ops:
  0.0 3.0 %shard_map.145 = (bf16[11,64,512]{2,1,0:T(8,128)(2,1)}, bf16[11,64,512]{2,1,0:T(8,128)(2,1)}) custom-call(bf16[16,64,512]{2,1,0:T(8,128)(2,1)} %charges.1, bf16[16,64,64]{2,1,0:T(8,128)(2,1)} %basis.3, f32[16,1,64,64]{3,2,1,0:T(8,128)} %fine_c.1, f32[8,1,64,64]{3,2,1,0:T(8,128)} %middle_c.1, f32[4,1,64,64]{3,2,1,0:T(8,128)} %coarse_c.1, f32[2,2,64,64]{3,2,1,0:T(8,128)} %top_c.1), custom_call_target="tpu_custom_call" | custom-call | flops 1000000 | bytes 100000 | tf_op jit(solution)/shard_map/pallas_call | solution.py:54
  3.1 2.0 %collective-permute-start.6 = (bf16[11,64,512]{2,1,0:T(8,128)(2,1)}, bf16[11,64,512]{2,1,0:T(8,128)(2,1)S(1)}, u32[]{:S(2)}, u32[]{:S(2)}) collective-permute-start(bf16[11,64,512]{2,1,0:T(8,128)(2,1)} %get-tuple-element.26.edge.edge0), channel_id=1, source_target_pairs={{0,1},{1,2},{2,3},{3,0},{4,5},{5,6},{6,7},{7,4},{8,9},{9,10},{10,1... | collective-permute-start | bytes 2162696 | tf_op jit(solution)/shard_map/ppermute | solution.py:40
  5.2 4.2 %shard_map.146 = (bf16[144,128]{1,0:T(8,128)(2,1)}, bf16[144,128]{1,0:T(8,128)(2,1)}, bf16[144,128]{1,0:T(8,128)(2,1)}, bf16[144,128]{1,0:T(8,128)(2,1)}) custom-call(s32[16]{0:T(128)} %bitcast.12, s32[8]{0:T(128)} %bitcast.13, s32[4]{0:T(128)} %bitcast.14, s32[2,2]{1,0:T(2,128)} %top_cols.1, bf16[11,64,512]{2,1,0:T(8,128)(2,1)} %get-tuple-element.26.edge.edge0, ...), custom_call_target="tpu_custom_call" | custom-call | flops 1000000 | bytes 100000 | tf_op jit(solution)/shard_map/pallas_call | solution.py:54
  9.3 3.2 %collective-permute-start = (bf16[144,128]{1,0:T(8,128)(2,1)}, bf16[144,128]{1,0:T(8,128)(2,1)S(1)}, u32[]{:S(2)}, u32[]{:S(2)}) collective-permute-start(bf16[144,128]{1,0:T(8,128)(2,1)} %get-tuple-element.29), channel_id=1, source_target_pairs={{0,1},{1,2},{2,3},{3,0},{4,5},{5,6},{6,7},{7,4},{8,9},{9,10},{10,1... | collective-permute-start | bytes 110600 | tf_op jit(solution)/shard_map/ppermute | solution.py:40
  14.1 8.3 %collective-permute-done.part1 = bf16[144,128]{1,0:T(8,128)(2,1)S(1)} collective-permute-done((bf16[144,128]{1,0:T(8,128)(2,1)}, bf16[144,128]{1,0:T(8,128)(2,1)S(1)}, u32[]{:S(2)}, u32[]{:S(2)}) %collective-permute-start) | collective-permute-done | bytes 36896 | tf_op jit(solution)/shard_map/ppermute | solution.py:40
  24.2 3.2 %collective-permute-start.12 = (bf16[11,64,512]{2,1,0:T(8,128)(2,1)S(1)}, bf16[11,64,512]{2,1,0:T(8,128)(2,1)S(1)}, u32[]{:S(2)}, u32[]{:S(2)}) collective-permute-start(bf16[11,64,512]{2,1,0:T(8,128)(2,1)S(1)} %collective-permute-done.6.edge1), channel_id=1, source_target_pairs={{0,1},{1,2},{2,3},{3,0},{4,5},{5,6},{6,7},{7,4},{8,9},{9,10},{10,1... | collective-permute-start | bytes 2162696 | tf_op jit(solution)/shard_map/ppermute | solution.py:40
  28.2 2.0 %collective-permute-start.8 = (bf16[2,64,128]{2,1,0:T(8,128)(2,1)S(1)}, bf16[2,64,128]{2,1,0:T(8,128)(2,1)S(1)}, u32[]{:S(2)}, u32[]{:S(2)}) collective-permute-start(bf16[2,64,128]{2,1,0:T(8,128)(2,1)S(1)} %bitcast.8), channel_id=1, source_target_pairs={{0,32},{4,36},{8,40},{12,44},{16,48},{20,52},{24,56},{28,60},{32,6... | collective-permute-start | bytes 98312 | tf_op jit(solution)/shard_map/ppermute | solution.py:36
  30.1 4.0 %collective-permute-start.9 = (bf16[2,64,128]{2,1,0:T(8,128)(2,1)S(1)}, bf16[2,64,128]{2,1,0:T(8,128)(2,1)S(1)}, u32[]{:S(2)}, u32[]{:S(2)}) collective-permute-start(bf16[2,64,128]{2,1,0:T(8,128)(2,1)S(1)} %bitcast.9), channel_id=1, source_target_pairs={{0,224},{4,228},{8,232},{12,236},{16,240},{20,244},{24,248},{28,25... | collective-permute-start | bytes 98312 | tf_op jit(solution)/shard_map/ppermute | solution.py:36
  34.2 1.8 %collective-permute-done.8 = bf16[2,64,128]{2,1,0:T(8,128)(2,1)S(1)} collective-permute-done((bf16[2,64,128]{2,1,0:T(8,128)(2,1)S(1)}, bf16[2,64,128]{2,1,0:T(8,128)(2,1)S(1)}, u32[]{:S(2)}, u32[]{:S(2)}) %collective-permute-start.8) | collective-permute-done | bytes 32800 | tf_op jit(solution)/shard_map/ppermute | solution.py:36
  36.0 5.1 %collective-permute-start.10 = (bf16[6,64,128]{2,1,0:T(8,128)(2,1)S(1)}, bf16[6,64,128]{2,1,0:T(8,128)(2,1)S(1)}, u32[]{:S(2)}, u32[]{:S(2)}) collective-permute-start(bf16[6,64,128]{2,1,0:T(8,128)(2,1)S(1)} %constant_dynamic-update-slice_fusion.refs_1_), channel_id=1, source_target_pairs={{0,96},{4,100},{8,104},{12,108},{16,112},{20,116},{24,120},{28,124... | collective-permute-start | bytes 294920 | tf_op jit(solution)/shard_map/ppermute | solution.py:36
  41.2 6.0 %collective-permute-done.11.refs_2_ = bf16[4,64,128]{2,1,0:T(8,128)(2,1)S(1)} collective-permute-done((bf16[4,64,128]{2,1,0:T(8,128)(2,1)S(1)}, bf16[4,64,128]{2,1,0:T(8,128)(2,1)S(1)}, u32[]{:S(2)}, u32[]{:S(2)}) %collective-permute-start.11) | collective-permute-done | bytes 65568 | tf_op jit(solution)/shard_map/ppermute | solution.py:36
  48.3 2.8 %collective-permute-start.14 = (bf16[16,64,128]{2,1,0:T(8,128)(2,1)S(1)}, bf16[16,64,128]{2,1,0:T(8,128)(2,1)S(1)}, u32[]{:S(2)}, u32[]{:S(2)}) collective-permute-start(bf16[16,64,128]{2,1,0:T(8,128)(2,1)S(1)} %shard_map.147.refs_0_), channel_id=1, source_target_pairs={{0,24},{4,28},{8,0},{12,4},{16,8},{20,12},{24,16},{28,20},{32,56},... | collective-permute-start | bytes 786440 | tf_op jit(solution)/shard_map/ppermute | solution.py:36
  51.3 1.9 %collective-permute-start.5 = (bf16[11,64,512]{2,1,0:T(8,128)(2,1)S(1)}, bf16[11,64,512]{2,1,0:T(8,128)(2,1)S(1)}, u32[]{:S(2)}, u32[]{:S(2)}) collective-permute-start(bf16[11,64,512]{2,1,0:T(8,128)(2,1)S(1)} %collective-permute-done.4.inner2.down), channel_id=1, source_target_pairs={{0,3},{1,0},{2,1},{3,2},{4,7},{5,4},{6,5},{7,6},{8,11},{9,8},{10,9... | collective-permute-start | bytes 2162696 | tf_op jit(solution)/shard_map/ppermute | solution.py:40
  53.1 3.3 %collective-permute-done.14.refs_2_ = bf16[16,64,128]{2,1,0:T(8,128)(2,1)S(1)} collective-permute-done((bf16[16,64,128]{2,1,0:T(8,128)(2,1)S(1)}, bf16[16,64,128]{2,1,0:T(8,128)(2,1)S(1)}, u32[]{:S(2)}, u32[]{:S(2)}) %collective-permute-start.14) | collective-permute-done | bytes 262176 | tf_op jit(solution)/shard_map/ppermute | solution.py:36
  56.4 3.8 %collective-permute-start.16 = (bf16[8,64,128]{2,1,0:T(8,128)(2,1)S(1)}, bf16[8,64,128]{2,1,0:T(8,128)(2,1)S(1)}, u32[]{:S(2)}, u32[]{:S(2)}) collective-permute-start(bf16[8,64,128]{2,1,0:T(8,128)(2,1)S(1)} %slice.34), channel_id=1, source_target_pairs={{0,24},{4,28},{8,0},{12,4},{16,8},{20,12},{24,16},{28,20},{32,56},... | collective-permute-start | bytes 393224 | tf_op jit(solution)/shard_map/ppermute | solution.py:36
  60.3 2.0 %shard_map.151 = (bf16[24,64,512]{2,1,0:T(8,128)(2,1)S(1)}, bf16[24,64,512]{2,1,0:T(8,128)(2,1)S(1)}) custom-call(bf16[11,64,512]{2,1,0:T(8,128)(2,1)S(1)} %copy-done.1, bf16[11,64,512]{2,1,0:T(8,128)(2,1)S(1)} %collective-permute-done.6.edge1, bf16[11,64,512]{2,1,0:T(8,128)(2,1)S(1)} %collective-permute-done.7.edge2, ...), custom_call_target="tpu_custom_call" | custom-call | flops 1000000 | bytes 100000 | tf_op jit(solution)/shard_map/pallas_call | solution.py:54
  62.7 3.8 %collective-permute-done.15.refs_3_ = bf16[8,64,128]{2,1,0:T(8,128)(2,1)S(1)} collective-permute-done((bf16[8,64,128]{2,1,0:T(8,128)(2,1)S(1)}, bf16[8,64,128]{2,1,0:T(8,128)(2,1)S(1)}, u32[]{:S(2)}, u32[]{:S(2)}) %collective-permute-start.15) | collective-permute-done | bytes 131104 | tf_op jit(solution)/shard_map/ppermute | solution.py:36
  68.6 4.6 %collective-permute-start.19 = (bf16[17,64,512]{2,1,0:T(8,128)(2,1)S(1)}, bf16[17,64,512]{2,1,0:T(8,128)(2,1)S(1)}, u32[]{:S(2)}, u32[]{:S(2)}) collective-permute-start(bf16[17,64,512]{2,1,0:T(8,128)(2,1)S(1)} %get-tuple-element.41), channel_id=1, source_target_pairs={{0,252},{4,0},{8,4},{12,8},{16,12},{20,16},{24,20},{28,24},{32,28}... | collective-permute-start | bytes 3342344 | tf_op jit(solution)/shard_map/ppermute | solution.py:36
  74.4 2.6 %collective-permute-done.17.partner = bf16[64,64,128]{2,1,0:T(8,128)(2,1)S(1)} collective-permute-done((bf16[64,64,128]{2,1,0:T(8,128)(2,1)S(1)}, bf16[64,64,128]{2,1,0:T(8,128)(2,1)S(1)}, u32[]{:S(2)}, u32[]{:S(2)}) %collective-permute-start.17) | collective-permute-done | bytes 1048608 | tf_op jit(solution)/shard_map/ppermute | solution.py:36
  77.0 2.3 %shard_map.150 = (bf16[2,64,128]{2,1,0:T(8,128)(2,1)S(1)}, s32[4,8,128]{2,1,0:T(8,128)S(1)}) custom-call(bf16[144,128]{1,0:T(8,128)(2,1)S(1)} %copy-done.6, bf16[144,128]{1,0:T(8,128)(2,1)S(1)} %collective-permute-done.part1, bf16[144,128]{1,0:T(8,128)(2,1)S(1)} %collective-permute-done.1.part2, bf16[144,128]{1,0:T(8,128)(2,1)S(1)} %collective-permute-done.2.part3, ...), custom_call_target="tpu_custom_call" | custom-call | flops 1000000 | bytes 100000 | tf_op jit(solution)/shard_map/pallas_call | solution.py:54
  80.1 5.5 %collective-permute-done.24.chip_ends = bf16[24,64,512]{2,1,0:T(8,128)(2,1)S(1)} collective-permute-done((bf16[24,64,512]{2,1,0:T(8,128)(2,1)S(1)}, bf16[24,64,512]{2,1,0:T(8,128)(2,1)S(1)}, u32[]{:S(2)}, u32[]{:S(2)}) %collective-permute-start.24) | collective-permute-done | bytes 1572896 | tf_op jit(solution)/shard_map/ppermute | solution.py:247
  85.6 3.2 %collective-permute-start.20 = (bf16[2,64,128]{2,1,0:T(8,128)(2,1)S(1)}, bf16[2,64,128]{2,1,0:T(8,128)(2,1)S(1)}, u32[]{:S(2)}, u32[]{:S(2)}) collective-permute-start(bf16[2,64,128]{2,1,0:T(8,128)(2,1)S(1)} %get-tuple-element.42.own_t), channel_id=1, source_target_pairs={{0,1},{1,2},{2,3},{3,0},{4,5},{5,6},{6,7},{7,4},{8,9},{9,10},{10,1... | collective-permute-start | bytes 98312 | tf_op jit(solution)/shard_map/ppermute | solution.py:40
  88.9 6.9 %shard_map.152.near = f32[16,64,512]{2,1,0:T(8,128)S(1)} custom-call(s32[16,12]{1,0:T(8,128)S(1)} %copy-done.7, bf16[11,64,512]{2,1,0:T(8,128)(2,1)S(1)} %copy-done.1, bf16[11,64,512]{2,1,0:T(8,128)(2,1)S(1)} %copy-done, bf16[11,64,512]{2,1,0:T(8,128)(2,1)S(1)} %collective-permute-done.6.edge1, bf16[11,64,512]{2,1,0:T(8,128)(2,1)S(1)} %collective-permute-done.3.inner1.up, ...), custom_call_target="tpu_custom_call" | custom-call | flops 1000000 | bytes 100000 | tf_op jit(solution)/shard_map/pallas_call | solution.py:54
  97.6 6.1 %shard_map.153 = bf16[16,64,512]{2,1,0:T(8,128)(2,1)} custom-call(s32[4,32]{1,0:T(4,128)S(1)} %bitcast.7, bf16[16,64,512]{2,1,0:T(8,128)(2,1)S(1)} %get-tuple-element.35.fine_m, bf16[8,64,512]{2,1,0:T(8,128)(2,1)S(1)} %get-tuple-element.38.middle_m, bf16[4,64,512]{2,1,0:T(8,128)(2,1)S(1)} %get-tuple-element.39.coarse_m, ...), custom_call_target="tpu_custom_call" | custom-call | flops 1000000 | bytes 100000 | tf_op jit(solution)/shard_map/pallas_call | solution.py:54
  (64 shorter events, 11.8 us)
Async XLA Ops:
  3.1 21.1 %collective-permute-start.6 = (bf16[11,64,512]{2,1,0:T(8,128)(2,1)}, bf16[11,64,512]{2,1,0:T(8,128)(2,1)S(1)}, u32[]{:S(2)}, u32[]{:S(2)}) collective-permute-start(bf16[11,64,512]{2,1,0:T(8,128)(2,1)} %get-tuple-element.26.edge.edge0), channel_id=1, source_target_pairs={{0,1},{1,2},{2,3},{3,0},{4,5},{5,6},{6,7},{7,4},{8,9},{9,10},{10,1... | collective-permute-start | bytes 2162696 | tf_op jit(solution)/shard_map/ppermute | solution.py:40
  5.1 23.0 %collective-permute-start.7 = (bf16[11,64,512]{2,1,0:T(8,128)(2,1)}, bf16[11,64,512]{2,1,0:T(8,128)(2,1)S(1)}, u32[]{:S(2)}, u32[]{:S(2)}) collective-permute-start(bf16[11,64,512]{2,1,0:T(8,128)(2,1)} %get-tuple-element.26.edge.edge0), channel_id=1, source_target_pairs={{0,3},{1,0},{2,1},{3,2},{4,7},{5,4},{6,5},{7,6},{8,11},{9,8},{10,9... | collective-permute-start | bytes 2162696 | tf_op jit(solution)/shard_map/ppermute | solution.py:40
  9.3 13.1 %collective-permute-start = (bf16[144,128]{1,0:T(8,128)(2,1)}, bf16[144,128]{1,0:T(8,128)(2,1)S(1)}, u32[]{:S(2)}, u32[]{:S(2)}) collective-permute-start(bf16[144,128]{1,0:T(8,128)(2,1)} %get-tuple-element.29), channel_id=1, source_target_pairs={{0,1},{1,2},{2,3},{3,0},{4,5},{5,6},{6,7},{7,4},{8,9},{9,10},{10,1... | collective-permute-start | bytes 110600 | tf_op jit(solution)/shard_map/ppermute | solution.py:40
  12.6 11.5 %collective-permute-start.1 = (bf16[144,128]{1,0:T(8,128)(2,1)}, bf16[144,128]{1,0:T(8,128)(2,1)S(1)}, u32[]{:S(2)}, u32[]{:S(2)}) collective-permute-start(bf16[144,128]{1,0:T(8,128)(2,1)} %get-tuple-element.30), channel_id=1, source_target_pairs={{0,3},{1,0},{2,1},{3,2},{4,7},{5,4},{6,5},{7,6},{8,11},{9,8},{10,9... | collective-permute-start | bytes 110600 | tf_op jit(solution)/shard_map/ppermute | solution.py:40
  12.6 11.5 %collective-permute-start.2 = (bf16[144,128]{1,0:T(8,128)(2,1)}, bf16[144,128]{1,0:T(8,128)(2,1)S(1)}, u32[]{:S(2)}, u32[]{:S(2)}) collective-permute-start(bf16[144,128]{1,0:T(8,128)(2,1)} %get-tuple-element.31), channel_id=1, source_target_pairs={{0,2},{1,3},{2,0},{3,1},{4,6},{5,7},{6,4},{7,5},{8,10},{9,11},{10,... | collective-permute-start | bytes 110600 | tf_op jit(solution)/shard_map/ppermute | solution.py:40
  24.1 24.1 %collective-permute-start.4 = (bf16[11,64,512]{2,1,0:T(8,128)(2,1)S(1)}, bf16[11,64,512]{2,1,0:T(8,128)(2,1)S(1)}, u32[]{:S(2)}, u32[]{:S(2)}) collective-permute-start(bf16[11,64,512]{2,1,0:T(8,128)(2,1)S(1)} %copy-done), channel_id=1, source_target_pairs={{0,3},{1,0},{2,1},{3,2},{4,7},{5,4},{6,5},{7,6},{8,11},{9,8},{10,9... | collective-permute-start | bytes 2162696 | tf_op jit(solution)/shard_map/ppermute | solution.py:40
  24.2 24.1 %collective-permute-start.12 = (bf16[11,64,512]{2,1,0:T(8,128)(2,1)S(1)}, bf16[11,64,512]{2,1,0:T(8,128)(2,1)S(1)}, u32[]{:S(2)}, u32[]{:S(2)}) collective-permute-start(bf16[11,64,512]{2,1,0:T(8,128)(2,1)S(1)} %collective-permute-done.6.edge1), channel_id=1, source_target_pairs={{0,1},{1,2},{2,3},{3,0},{4,5},{5,6},{6,7},{7,4},{8,9},{9,10},{10,1... | collective-permute-start | bytes 2162696 | tf_op jit(solution)/shard_map/ppermute | solution.py:40
  28.2 7.8 %collective-permute-start.8 = (bf16[2,64,128]{2,1,0:T(8,128)(2,1)S(1)}, bf16[2,64,128]{2,1,0:T(8,128)(2,1)S(1)}, u32[]{:S(2)}, u32[]{:S(2)}) collective-permute-start(bf16[2,64,128]{2,1,0:T(8,128)(2,1)S(1)} %bitcast.8), channel_id=1, source_target_pairs={{0,32},{4,36},{8,40},{12,44},{16,48},{20,52},{24,56},{28,60},{32,6... | collective-permute-start | bytes 98312 | tf_op jit(solution)/shard_map/ppermute | solution.py:36
  30.1 5.8 %collective-permute-start.9 = (bf16[2,64,128]{2,1,0:T(8,128)(2,1)S(1)}, bf16[2,64,128]{2,1,0:T(8,128)(2,1)S(1)}, u32[]{:S(2)}, u32[]{:S(2)}) collective-permute-start(bf16[2,64,128]{2,1,0:T(8,128)(2,1)S(1)} %bitcast.9), channel_id=1, source_target_pairs={{0,224},{4,228},{8,232},{12,236},{16,240},{20,244},{24,248},{28,25... | collective-permute-start | bytes 98312 | tf_op jit(solution)/shard_map/ppermute | solution.py:36
  36.0 11.3 %collective-permute-start.10 = (bf16[6,64,128]{2,1,0:T(8,128)(2,1)S(1)}, bf16[6,64,128]{2,1,0:T(8,128)(2,1)S(1)}, u32[]{:S(2)}, u32[]{:S(2)}) collective-permute-start(bf16[6,64,128]{2,1,0:T(8,128)(2,1)S(1)} %constant_dynamic-update-slice_fusion.refs_1_), channel_id=1, source_target_pairs={{0,96},{4,100},{8,104},{12,108},{16,112},{20,116},{24,120},{28,124... | collective-permute-start | bytes 294920 | tf_op jit(solution)/shard_map/ppermute | solution.py:36
  41.1 6.1 %collective-permute-start.11 = (bf16[4,64,128]{2,1,0:T(8,128)(2,1)S(1)}, bf16[4,64,128]{2,1,0:T(8,128)(2,1)S(1)}, u32[]{:S(2)}, u32[]{:S(2)}) collective-permute-start(bf16[4,64,128]{2,1,0:T(8,128)(2,1)S(1)} %pad_maximum_fusion), channel_id=1, source_target_pairs={{0,160},{4,164},{8,168},{12,172},{16,176},{20,180},{24,184},{28,18... | collective-permute-start | bytes 196616 | tf_op jit(solution)/shard_map/ppermute | solution.py:36
  48.3 8.1 %collective-permute-start.14 = (bf16[16,64,128]{2,1,0:T(8,128)(2,1)S(1)}, bf16[16,64,128]{2,1,0:T(8,128)(2,1)S(1)}, u32[]{:S(2)}, u32[]{:S(2)}) collective-permute-start(bf16[16,64,128]{2,1,0:T(8,128)(2,1)S(1)} %shard_map.147.refs_0_), channel_id=1, source_target_pairs={{0,24},{4,28},{8,0},{12,4},{16,8},{20,12},{24,16},{28,20},{32,56},... | collective-permute-start | bytes 786440 | tf_op jit(solution)/shard_map/ppermute | solution.py:36
  51.1 9.1 %collective-permute-start.13 = (bf16[16,64,128]{2,1,0:T(8,128)(2,1)S(1)}, bf16[16,64,128]{2,1,0:T(8,128)(2,1)S(1)}, u32[]{:S(2)}, u32[]{:S(2)}) collective-permute-start(bf16[16,64,128]{2,1,0:T(8,128)(2,1)S(1)} %shard_map.147.refs_0_), channel_id=1, source_target_pairs={{0,8},{4,12},{8,16},{12,20},{16,24},{20,28},{24,0},{28,4},{32,40},... | collective-permute-start | bytes 786440 | tf_op jit(solution)/shard_map/ppermute | solution.py:36
  51.1 15.4 %collective-permute-start.3 = (bf16[11,64,512]{2,1,0:T(8,128)(2,1)S(1)}, bf16[11,64,512]{2,1,0:T(8,128)(2,1)S(1)}, u32[]{:S(2)}, u32[]{:S(2)}) collective-permute-start(bf16[11,64,512]{2,1,0:T(8,128)(2,1)S(1)} %copy-done), channel_id=1, source_target_pairs={{0,1},{1,2},{2,3},{3,0},{4,5},{5,6},{6,7},{7,4},{8,9},{9,10},{10,1... | collective-permute-start | bytes 2162696 | tf_op jit(solution)/shard_map/ppermute | solution.py:40
  51.3 15.2 %collective-permute-start.5 = (bf16[11,64,512]{2,1,0:T(8,128)(2,1)S(1)}, bf16[11,64,512]{2,1,0:T(8,128)(2,1)S(1)}, u32[]{:S(2)}, u32[]{:S(2)}) collective-permute-start(bf16[11,64,512]{2,1,0:T(8,128)(2,1)S(1)} %collective-permute-done.4.inner2.down), channel_id=1, source_target_pairs={{0,3},{1,0},{2,1},{3,2},{4,7},{5,4},{6,5},{7,6},{8,11},{9,8},{10,9... | collective-permute-start | bytes 2162696 | tf_op jit(solution)/shard_map/ppermute | solution.py:40
  56.4 6.3 %collective-permute-start.16 = (bf16[8,64,128]{2,1,0:T(8,128)(2,1)S(1)}, bf16[8,64,128]{2,1,0:T(8,128)(2,1)S(1)}, u32[]{:S(2)}, u32[]{:S(2)}) collective-permute-start(bf16[8,64,128]{2,1,0:T(8,128)(2,1)S(1)} %slice.34), channel_id=1, source_target_pairs={{0,24},{4,28},{8,0},{12,4},{16,8},{20,12},{24,16},{28,20},{32,56},... | collective-permute-start | bytes 393224 | tf_op jit(solution)/shard_map/ppermute | solution.py:36
  60.2 6.3 %collective-permute-start.15 = (bf16[8,64,128]{2,1,0:T(8,128)(2,1)S(1)}, bf16[8,64,128]{2,1,0:T(8,128)(2,1)S(1)}, u32[]{:S(2)}, u32[]{:S(2)}) collective-permute-start(bf16[8,64,128]{2,1,0:T(8,128)(2,1)S(1)} %slice.33), channel_id=1, source_target_pairs={{0,8},{4,12},{8,16},{12,20},{16,24},{20,28},{24,0},{28,4},{32,40},... | collective-permute-start | bytes 393224 | tf_op jit(solution)/shard_map/ppermute | solution.py:36
  62.4 23.2 %collective-permute-start.24 = (bf16[24,64,512]{2,1,0:T(8,128)(2,1)S(1)}, bf16[24,64,512]{2,1,0:T(8,128)(2,1)S(1)}, u32[]{:S(2)}, u32[]{:S(2)}) collective-permute-start(bf16[24,64,512]{2,1,0:T(8,128)(2,1)S(1)} %get-tuple-element.46), channel_id=1, source_target_pairs={{0,252},{4,8},{8,4},{12,16},{16,12},{20,24},{24,20},{28,32},{32,28... | collective-permute-start | bytes 4718600 | tf_op jit(solution)/shard_map/ppermute | solution.py:247
  66.5 19.1 %collective-permute-start.23 = (bf16[24,64,512]{2,1,0:T(8,128)(2,1)S(1)}, bf16[24,64,512]{2,1,0:T(8,128)(2,1)S(1)}, u32[]{:S(2)}, u32[]{:S(2)}) collective-permute-start(bf16[24,64,512]{2,1,0:T(8,128)(2,1)S(1)} %get-tuple-element.45), channel_id=1, source_target_pairs={{0,4},{4,0},{8,12},{12,8},{16,20},{20,16},{24,28},{28,24},{32,36},... | collective-permute-start | bytes 4718600 | tf_op jit(solution)/shard_map/ppermute | solution.py:36
  68.0 29.5 %collective-permute-start.18 = (bf16[17,64,512]{2,1,0:T(8,128)(2,1)S(1)}, bf16[17,64,512]{2,1,0:T(8,128)(2,1)S(1)}, u32[]{:S(2)}, u32[]{:S(2)}) collective-permute-start(bf16[17,64,512]{2,1,0:T(8,128)(2,1)S(1)} %get-tuple-element.40), channel_id=1, source_target_pairs={{0,4},{4,8},{8,12},{12,16},{16,20},{20,24},{24,28},{28,32},{32,36}... | collective-permute-start | bytes 3342344 | tf_op jit(solution)/shard_map/ppermute | solution.py:36
  68.6 29.0 %collective-permute-start.19 = (bf16[17,64,512]{2,1,0:T(8,128)(2,1)S(1)}, bf16[17,64,512]{2,1,0:T(8,128)(2,1)S(1)}, u32[]{:S(2)}, u32[]{:S(2)}) collective-permute-start(bf16[17,64,512]{2,1,0:T(8,128)(2,1)S(1)} %get-tuple-element.41), channel_id=1, source_target_pairs={{0,252},{4,0},{8,4},{12,8},{16,12},{20,16},{24,20},{28,24},{32,28}... | collective-permute-start | bytes 3342344 | tf_op jit(solution)/shard_map/ppermute | solution.py:36
  79.3 18.3 %collective-permute-start.22 = (bf16[2,64,128]{2,1,0:T(8,128)(2,1)S(1)}, bf16[2,64,128]{2,1,0:T(8,128)(2,1)S(1)}, u32[]{:S(2)}, u32[]{:S(2)}) collective-permute-start(bf16[2,64,128]{2,1,0:T(8,128)(2,1)S(1)} %get-tuple-element.42.own_t), channel_id=1, source_target_pairs={{0,2},{1,3},{2,0},{3,1},{4,6},{5,7},{6,4},{7,5},{8,10},{9,11},{10,... | collective-permute-start | bytes 98312 | tf_op jit(solution)/shard_map/ppermute | solution.py:40
  85.6 11.9 %collective-permute-start.21 = (bf16[2,64,128]{2,1,0:T(8,128)(2,1)S(1)}, bf16[2,64,128]{2,1,0:T(8,128)(2,1)S(1)}, u32[]{:S(2)}, u32[]{:S(2)}) collective-permute-start(bf16[2,64,128]{2,1,0:T(8,128)(2,1)S(1)} %get-tuple-element.42.own_t), channel_id=1, source_target_pairs={{0,3},{1,0},{2,1},{3,2},{4,7},{5,4},{6,5},{7,6},{8,11},{9,8},{10,9... | collective-permute-start | bytes 98312 | tf_op jit(solution)/shard_map/ppermute | solution.py:40
  85.6 11.9 %collective-permute-start.20 = (bf16[2,64,128]{2,1,0:T(8,128)(2,1)S(1)}, bf16[2,64,128]{2,1,0:T(8,128)(2,1)S(1)}, u32[]{:S(2)}, u32[]{:S(2)}) collective-permute-start(bf16[2,64,128]{2,1,0:T(8,128)(2,1)S(1)} %get-tuple-element.42.own_t), channel_id=1, source_target_pairs={{0,1},{1,2},{2,3},{3,0},{4,5},{5,6},{6,7},{7,4},{8,9},{9,10},{10,1... | collective-permute-start | bytes 98312 | tf_op jit(solution)/shard_map/ppermute | solution.py:40
  (11 other events, 191.1 us)
